TPU v7x, 32 devices: a whole 2x2x4 slice. The times are simulated.
32 devices in a mesh: dp: 16 (over z, y, core), tensor: 2 (over x).
Axes of the slice: x: 2, y: 2, z: 4, core: 2. Of those that a mesh axis runs over, the one named last changes fastest.
Arguments:
- tokens: bfloat16 [16384, 1024], P(('dp', 'tensor')), may hold values from -6 to 6
- cond: bfloat16 [16, 1024], P('dp'), may hold values from -6 to 6
- cotangent: bfloat16 [16384, 1024], P(('dp', 'tensor')), may hold values from -6 to 6
- w_qkv: bfloat16 [1024, 3, 1024], P('dp', None, 'tensor'), may hold values from -0.1875 to 0.1875
- b_qv: bfloat16 [2, 1024], P(None, ('tensor', 'dp')), may hold values from -2 to 2
- w_proj: bfloat16 [1024, 1024], P('tensor', 'dp'), may hold values from -1 to 1
- b_proj: bfloat16 [1024], P(('tensor', 'dp')), may hold values from -2 to 2
- w_fc1: bfloat16 [1024, 4096], P('dp', 'tensor'), may hold values from -0.1875 to 0.1875
- b_fc1: bfloat16 [4096], P(('tensor', 'dp')), may hold values from -3 to 3
- w_fc2: bfloat16 [4096, 1024], P('tensor', 'dp'), may hold values from -0.09375 to 0.09375
- b_fc2: bfloat16 [1024], P(('tensor', 'dp')), may hold values from -2 to 2
- w_ada: bfloat16 [1024, 6, 1024], P('dp', None, 'tensor'), may hold values from -0.1875 to 0.1875
- b_ada: bfloat16 [6, 1024], P(None, ('tensor', 'dp')), may hold values from -2 to 2
Outputs:
- block_out: bfloat16 [16384, 1024], P(('dp', 'tensor'))
- grad_tokens: bfloat16 [16384, 1024], P(('dp', 'tensor'))
- grad_cond: float32 [16, 1024], P('dp')
- grad_w_qkv: float32 [1024, 3, 1024], P('dp', None, 'tensor')
- grad_b_qv: float32 [2, 1024], P(None, ('tensor', 'dp'))
- grad_w_proj: float32 [1024, 1024], P('tensor', 'dp')
- grad_b_proj: float32 [1024], P(('tensor', 'dp'))
- grad_w_fc1: float32 [1024, 4096], P('dp', 'tensor')
- grad_b_fc1: float32 [4096], P(('tensor', 'dp'))
- grad_w_fc2: float32 [4096, 1024], P('tensor', 'dp')
- grad_b_fc2: float32 [1024], P(('tensor', 'dp'))
- grad_w_ada: float32 [1024, 6, 1024], P('dp', None, 'tensor')
- grad_b_ada: float32 [6, 1024], P(None, ('tensor', 'dp'))
All inputs are finite; a program needn't handle non-finite values.
Results may differ from a plain program's by a relative error of at most 0.02.
Values may be sent and summed in bfloat16 or wider, within the bound.
No kernel may reach another device: no remote copies, remote signals or barrier semaphores. Data moves between devices by JAX's collectives and lax.ppermute only.
A program may use at most 256 MiB of HBM per device.

v0:
```python
from functools import partial

import jax
import jax.numpy as jnp
from jax import lax
from jax.sharding import PartitionSpec as P

HEAD_DIM = 64
LEN = 1024


norm_eps = 1e-06
highest = lax.Precision.HIGHEST


def normalize(values):
    centred = values - jnp.mean(values, -1, keepdims=True)
    rstd = lax.rsqrt(jnp.mean(centred * centred, -1, keepdims=True) + norm_eps)
    return (centred * rstd, rstd)


def norm_back(grad_n, normed, rstd):
    first = jnp.mean(grad_n, -1, keepdims=True)
    second = jnp.mean(grad_n * normed, -1, keepdims=True)
    return rstd * (grad_n - first - normed * second)


def shards(
    tokens, cond, cotangent, w_qkv, b_qv, w_proj, b_proj, w_fc1, b_fc1, w_fc2, b_fc2, w_ada, b_ada
):
    tensor_size = lax.axis_size("tensor")
    tensor_pos = lax.axis_index("tensor")
    row_count, model_width = tokens.shape
    latents = cond.shape[0]
    group_rows = row_count * tensor_size
    qkv_w, qv_bias, proj_w, proj_bias, fc1_w, fc1_bias, fc2_w, fc2_bias, ada_w, ada_bias = (
        lax.all_gather(w_qkv, "dp", axis=0, tiled=True),
        lax.all_gather(b_qv, "dp", axis=1, tiled=True),
        lax.all_gather(w_proj, "dp", axis=1, tiled=True),
        lax.all_gather(b_proj, "dp", axis=0, tiled=True),
        lax.all_gather(w_fc1, "dp", axis=0, tiled=True),
        lax.all_gather(b_fc1, "dp", axis=0, tiled=True),
        lax.all_gather(w_fc2, "dp", axis=1, tiled=True),
        lax.all_gather(b_fc2, "dp", axis=0, tiled=True),
        lax.all_gather(w_ada, "dp", axis=0, tiled=True),
        lax.all_gather(b_ada, "dp", axis=1, tiled=True),
    )
    local_width = qkv_w.shape[2]
    local_heads = local_width // HEAD_DIM
    score_scale = HEAD_DIM ** (-0.5)
    col_start = tensor_pos * local_width

    def spread_cols(column_block):
        return lax.dynamic_update_slice(
            jnp.zeros((model_width,), jnp.float32), column_block.astype(jnp.float32), (col_start,)
        )

    def own_cols(values):
        return lax.dynamic_slice_in_dim(values, col_start, local_width, 0)

    silu_cond = jax.nn.silu(cond.astype(jnp.float32)).astype(jnp.bfloat16)
    mod_part = jnp.einsum(
        "sd,dkc->skc", silu_cond, ada_w, preferred_element_type=jnp.float32
    ) + ada_bias.astype(jnp.float32)
    modul = lax.all_gather(mod_part, "tensor", axis=2, tiled=True)
    row_latent = (tensor_pos * row_count + jnp.arange(row_count, dtype=jnp.int32)) // LEN
    one_hot = (row_latent[:, None] == jnp.arange(latents, dtype=jnp.int32)[None, :]).astype(
        jnp.float32
    )
    row_mod = jnp.einsum("rs,skc->rkc", one_hot, modul, precision=highest)
    shift_one, scale_one, gate_one, shift_two, scale_two, gate_two = [
        row_mod[:, member] for member in range(6)
    ]
    inputs = tokens.astype(jnp.float32)
    normed_one, rstd_one = normalize(inputs)
    hidden_one = (normed_one * (1.0 + scale_one) + shift_one).astype(jnp.bfloat16)
    rows_one = lax.all_gather(hidden_one, "tensor", axis=0, tiled=True)
    bias_three = jnp.stack([qv_bias[0], jnp.zeros_like(qv_bias[0]), qv_bias[1]]).astype(jnp.float32)
    qkv_all = (
        jnp.einsum("rd,dkc->rkc", rows_one, qkv_w, preferred_element_type=jnp.float32) + bias_three
    ).astype(jnp.bfloat16)
    block_rows = min(512, LEN)
    per_latent = LEN // block_rows
    total_blocks = latents * per_latent
    shape_heads = (latents, LEN, local_heads, HEAD_DIM)
    queries = qkv_all[:, 0].reshape(total_blocks, block_rows, local_heads, HEAD_DIM)
    keys_all = qkv_all[:, 1].reshape(shape_heads)
    values_all = qkv_all[:, 2].reshape(shape_heads)
    block_ids = jnp.arange(total_blocks, dtype=jnp.int32)

    def scores_of(block_id, query_block):
        latent_id = block_id // per_latent
        key_rows = lax.dynamic_index_in_dim(keys_all, latent_id, 0, keepdims=False)
        value_rows = lax.dynamic_index_in_dim(values_all, latent_id, 0, keepdims=False)
        scores = (
            jnp.einsum("qhd,khd->hqk", query_block, key_rows, preferred_element_type=jnp.float32)
            * score_scale
        )
        return (latent_id, key_rows, value_rows, scores)

    def attend(inputs_pair):
        block_id, query_block = inputs_pair
        latent_id, key_rows, value_rows, scores = scores_of(block_id, query_block)
        row_peak = jnp.max(scores, -1, keepdims=True)
        exp_terms = jnp.exp(scores - row_peak)
        row_total = jnp.sum(exp_terms, -1, keepdims=True)
        softmax_low = (exp_terms / row_total).astype(jnp.bfloat16)
        attended = jnp.einsum(
            "hqk,khd->qhd", softmax_low, value_rows, preferred_element_type=jnp.float32
        )
        return (attended.astype(jnp.bfloat16), (row_peak + jnp.log(row_total))[..., 0])

    attended, log_totals = lax.map(attend, (block_ids, queries))
    heads_out = attended.reshape(group_rows, local_width)
    proj_full_bias = spread_cols(proj_bias)
    part_rows = heads_out
    branch_attn = lax.psum_scatter(
        (jnp.dot(part_rows, proj_w, preferred_element_type=jnp.float32) + proj_full_bias).astype(
            jnp.bfloat16
        ),
        "tensor",
        scatter_dimension=0,
        tiled=True,
    ).astype(jnp.float32)
    middle = inputs + gate_one * branch_attn
    normed_two, rstd_two = normalize(middle)
    hidden_two = (normed_two * (1.0 + scale_two) + shift_two).astype(jnp.bfloat16)
    grad_out = cotangent.astype(jnp.float32)
    grad_m = (gate_two * grad_out).astype(jnp.bfloat16)
    rows_two = lax.all_gather(hidden_two, "tensor", axis=0, tiled=True)
    pre_act = jnp.dot(rows_two, fc1_w, preferred_element_type=jnp.float32) + fc1_bias.astype(
        jnp.float32
    )
    activ = jax.nn.gelu(pre_act, approximate=True).astype(jnp.bfloat16)
    fc2_full_bias = spread_cols(fc2_bias)
    part_rows = activ
    branch_mlp = lax.psum_scatter(
        (jnp.dot(part_rows, fc2_w, preferred_element_type=jnp.float32) + fc2_full_bias).astype(
            jnp.bfloat16
        ),
        "tensor",
        scatter_dimension=0,
        tiled=True,
    ).astype(jnp.float32)
    grad_m_rows = lax.all_gather(grad_m, "tensor", axis=0, tiled=True)
    grad_fc2 = jnp.einsum("rf,rd->fd", activ, grad_m_rows, preferred_element_type=jnp.float32)
    grad_fc2_bias = own_cols(jnp.sum(grad_m_rows, 0, dtype=jnp.float32))
    grad_act = jnp.einsum("rd,fd->rf", grad_m_rows, fc2_w, preferred_element_type=jnp.float32)
    _, gelu_back = jax.vjp(partial(jax.nn.gelu, approximate=True), pre_act)
    grad_pre = gelu_back(grad_act)[0].astype(jnp.bfloat16)
    grad_fc1 = jnp.einsum("rd,rf->df", rows_two, grad_pre, preferred_element_type=jnp.float32)
    grad_fc1_bias = jnp.sum(grad_pre, 0, dtype=jnp.float32)
    part_rows = grad_pre
    grad_hidden_two = lax.psum_scatter(
        jnp.einsum("rf,df->rd", part_rows, fc1_w, preferred_element_type=jnp.float32).astype(
            jnp.bfloat16
        ),
        "tensor",
        scatter_dimension=0,
        tiled=True,
    ).astype(jnp.float32)
    block_out = (middle + gate_two * branch_mlp).astype(jnp.bfloat16)
    grad_mid = grad_out + norm_back(grad_hidden_two * (1.0 + scale_two), normed_two, rstd_two)
    grad_a = (gate_one * grad_mid).astype(jnp.bfloat16)
    grad_a_rows = lax.all_gather(grad_a, "tensor", axis=0, tiled=True)
    grad_proj = jnp.einsum("rc,rd->cd", heads_out, grad_a_rows, preferred_element_type=jnp.float32)
    grad_proj_bias = own_cols(jnp.sum(grad_a_rows, 0, dtype=jnp.float32))
    grad_heads = jnp.einsum(
        "rd,cd->rc", grad_a_rows, proj_w, preferred_element_type=jnp.float32
    ).astype(jnp.bfloat16)
    grad_heads = grad_heads.reshape(total_blocks, block_rows, local_heads, HEAD_DIM)

    def attend_back(carry, inputs_four):
        key_acc, value_acc = carry
        block_id, query_block, grad_block, log_block = inputs_four
        latent_id, key_rows, value_rows, scores = scores_of(block_id, query_block)
        probs = jnp.exp(scores - log_block[..., None])
        probs_low = probs.astype(jnp.bfloat16)
        grad_probs = jnp.einsum(
            "qhd,khd->hqk", grad_block, value_rows, preferred_element_type=jnp.float32
        )
        row_dot = jnp.sum(probs * grad_probs, -1, keepdims=True)
        grad_scores = (probs * (grad_probs - row_dot)).astype(jnp.bfloat16)
        grad_query = (
            jnp.einsum("hqk,khd->qhd", grad_scores, key_rows, preferred_element_type=jnp.float32)
            * score_scale
        ).astype(jnp.bfloat16)
        key_new = (
            jnp.einsum("hqk,qhd->khd", grad_scores, query_block, preferred_element_type=jnp.float32)
            * score_scale
        )
        value_new = jnp.einsum(
            "hqk,qhd->khd", probs_low, grad_block, preferred_element_type=jnp.float32
        )
        key_old = lax.dynamic_index_in_dim(key_acc, latent_id, 0, keepdims=False)
        value_old = lax.dynamic_index_in_dim(value_acc, latent_id, 0, keepdims=False)
        key_acc = lax.dynamic_update_index_in_dim(key_acc, key_old + key_new, latent_id, 0)
        value_acc = lax.dynamic_update_index_in_dim(value_acc, value_old + value_new, latent_id, 0)
        return ((key_acc, value_acc), grad_query)

    zero_heads = jnp.zeros(shape_heads, jnp.float32)
    (grad_keys, grad_values), grad_queries = lax.scan(
        attend_back, (zero_heads, zero_heads), (block_ids, queries, grad_heads, log_totals)
    )
    grad_qkv = jnp.stack(
        [
            grad_queries.reshape(group_rows, local_width),
            grad_keys.reshape(group_rows, local_width).astype(jnp.bfloat16),
            grad_values.reshape(group_rows, local_width).astype(jnp.bfloat16),
        ],
        1,
    )
    grad_qkv_w = jnp.einsum("rd,rkc->dkc", rows_one, grad_qkv, preferred_element_type=jnp.float32)
    grad_qv_bias = jnp.stack(
        [
            jnp.sum(grad_qkv[:, 0], 0, dtype=jnp.float32),
            jnp.sum(grad_qkv[:, 2], 0, dtype=jnp.float32),
        ]
    )
    part_rows = grad_qkv
    grad_hidden_one = lax.psum_scatter(
        jnp.einsum("rkc,dkc->rd", part_rows, qkv_w, preferred_element_type=jnp.float32).astype(
            jnp.bfloat16
        ),
        "tensor",
        scatter_dimension=0,
        tiled=True,
    ).astype(jnp.float32)
    grad_tokens = (
        grad_mid + norm_back(grad_hidden_one * (1.0 + scale_one), normed_one, rstd_one)
    ).astype(jnp.bfloat16)
    row_grads = jnp.stack(
        [
            grad_hidden_one,
            grad_hidden_one * normed_one,
            grad_mid * branch_attn,
            grad_hidden_two,
            grad_hidden_two * normed_two,
            grad_out * branch_mlp,
        ],
        1,
    )
    grad_mod = jnp.einsum("rs,rkc->skc", one_hot, row_grads, precision=highest)
    grad_mod_part = lax.psum_scatter(grad_mod, "tensor", scatter_dimension=2, tiled=True).astype(
        jnp.bfloat16
    )
    grad_ada = jnp.einsum(
        "sd,skc->dkc", silu_cond, grad_mod_part, preferred_element_type=jnp.float32
    )
    grad_ada_bias = jnp.sum(grad_mod_part, 0, dtype=jnp.float32)
    grad_silu = lax.psum(
        jnp.einsum("skc,dkc->sd", grad_mod_part, ada_w, preferred_element_type=jnp.float32),
        "tensor",
    )
    _, silu_back = jax.vjp(jax.nn.silu, cond.astype(jnp.float32))
    grad_cond = silu_back(grad_silu)[0]
    results = tuple(
        (
            lax.psum_scatter(
                grad_qkv_w.astype(jnp.bfloat16), "dp", scatter_dimension=0, tiled=True
            ).astype(jnp.float32),
            lax.psum_scatter(
                grad_qv_bias.astype(jnp.bfloat16), "dp", scatter_dimension=1, tiled=True
            ).astype(jnp.float32),
            lax.psum_scatter(
                grad_proj.astype(jnp.bfloat16), "dp", scatter_dimension=1, tiled=True
            ).astype(jnp.float32),
            lax.psum_scatter(
                grad_proj_bias.astype(jnp.bfloat16), "dp", scatter_dimension=0, tiled=True
            ).astype(jnp.float32),
            lax.psum_scatter(
                grad_fc1.astype(jnp.bfloat16), "dp", scatter_dimension=0, tiled=True
            ).astype(jnp.float32),
            lax.psum_scatter(
                grad_fc1_bias.astype(jnp.bfloat16), "dp", scatter_dimension=0, tiled=True
            ).astype(jnp.float32),
            lax.psum_scatter(
                grad_fc2.astype(jnp.bfloat16), "dp", scatter_dimension=1, tiled=True
            ).astype(jnp.float32),
            lax.psum_scatter(
                grad_fc2_bias.astype(jnp.bfloat16), "dp", scatter_dimension=0, tiled=True
            ).astype(jnp.float32),
            lax.psum_scatter(
                grad_ada.astype(jnp.bfloat16), "dp", scatter_dimension=0, tiled=True
            ).astype(jnp.float32),
            lax.psum_scatter(
                grad_ada_bias.astype(jnp.bfloat16), "dp", scatter_dimension=1, tiled=True
            ).astype(jnp.float32),
        )
    )
    return (block_out, grad_tokens, grad_cond) + results


def solution(mesh):
    placed = (
        P(("dp", "tensor"), None),
        P("dp", None),
        P(("dp", "tensor"), None),
        P("dp", None, "tensor"),
        P(None, ("tensor", "dp")),
        P("tensor", "dp"),
        P(("tensor", "dp")),
        P("dp", "tensor"),
        P(("tensor", "dp")),
        P("tensor", "dp"),
        P(("tensor", "dp")),
        P("dp", None, "tensor"),
        P(None, ("tensor", "dp")),
    )
    return jax.shard_map(
        shards,
        mesh=mesh,
        in_specs=placed,
        out_specs=(
            P(("dp", "tensor"), None),
            P(("dp", "tensor"), None),
            P("dp", None),
            P("dp", None, "tensor"),
            P(None, ("tensor", "dp")),
            P("tensor", "dp"),
            P(("tensor", "dp")),
            P("dp", "tensor"),
            P(("tensor", "dp")),
            P("tensor", "dp"),
            P(("tensor", "dp")),
            P("dp", None, "tensor"),
            P(None, ("tensor", "dp")),
        ),
        check_vma=False,
    )
```

profile of v0, /device:TPU:0, one launch (start us, length us, event | category | flops | bytes accessed | tf_op | source)
XLA Modules:
  0.0 1204.5 jit_solution(15654131699601810002)
XLA Ops:
  8.7 23.6 %all-gather.1 = bf16[16,32,6]{1,2,0:T(8,128)(2,1)S(1)} all-gather(bf16[1,32,6]{1,2,0:T(8,128)(2,1)} %bitcast.282), channel_id=1, replica_groups=mesh['dp'=16,'tensor'=2] {'dp'}, dimensions={0}, use_global_device_ids=true | all-gather | bytes 6528 | tf_op jit(solution)/shard_map/all_gather | solution.py:46
  36.8 38.1 %all-gather.14.cloned.1.call-done = bf16[1024,6,512]{2,0,1:T(8,128)(2,1)} async-done(((bf16[64,6,512]{2,0,1:T(8,128)(2,1)}), bf16[1024,6,512]{2,0,1:T(8,128)(2,1)}) %all-gather.14.cloned.1.call-update) | async-done | bytes 6291472 | tf_op jit(solution)/shard_map/all_gather | solution.py:45
  95.2 30.6 %all-reduce = bf16[512]{0:T(512)(128)(2,1)S(1)} all-reduce(bf16[512]{0:T(512)(128)(2,1)S(1)} %dynamic-update-slice), channel_id=1, replica_groups=mesh['dp'=16,'tensor'=2] {'dp'}, use_global_device_ids=true, to_apply=%add | all-reduce | flops 512 | bytes 2048
  125.8 17.0 %all-gather.2 = bf16[16,32,2]{1,2,0:T(2,128)(2,1)S(1)} all-gather(bf16[1,32,2]{1,2,0:T(2,128)(2,1)S(1)} %bitcast.283), channel_id=1, replica_groups=mesh['dp'=16,'tensor'=2] {'dp'}, dimensions={0}, use_global_device_ids=true | all-gather | bytes 2176 | tf_op jit(solution)/shard_map/all_gather | solution.py:38
  166.7 22.6 %while.28 = (s32[]{:T(128)}, bf16[2,512,8,64]{1,3,2,0:T(8,128)(2,1)}, f32[2,8,512]{2,1,0:T(8,128)S(1)}, bf16[2,512,8,64]{1,3,2,0:T(8,128)(2,1)S(1)}, bf16[1,1024...) while((s32[]{:T(128)}, bf16[2,512,8,64]{1,3,2,0:T(8,128)(2,1)}, ...), condition=%wide.region_5.6_spmd, body=%wide.region_2.5_spmd.sunk | while | flops 1111748608 | bytes 66191540 | solution.py:113
  200.7 29.8 %reduce-scatter.17.cloned.1.call-done = bf16[512,1024]{1,0:T(8,128)(2,1)} async-done(((bf16[1024,1024]{1,0:T(8,128)(2,1)}), bf16[512,1024]{1,0:T(8,128)(2,1)}) %reduce-scatter.17.cloned.1.call-update) | async-done | bytes 1048592 | tf_op jit(solution)/shard_map/reduce_scatter | solution.py:117
  240.3 21.3 %all-gather.3 = bf16[16,1,128]{2,1,0:T(2,128)(2,1)S(1)} all-gather(bf16[1,1,128]{2,1,0:T(2,128)(2,1)S(1)} %bitcast.284), channel_id=1, replica_groups=mesh['dp'=16,'tensor'=2] {'dp'}, dimensions={0}, use_global_device_ids=true | all-gather | bytes 4352 | tf_op jit(solution)/shard_map/all_gather | solution.py:42
  261.6 21.9 %all-gather.24.cloned.1.call-done = bf16[1024,2048]{1,0:T(8,128)(2,1)} async-done(((bf16[64,2048]{1,0:T(8,128)(2,1)}), bf16[1024,2048]{1,0:T(8,128)(2,1)}) %all-gather.24.cloned.1.call-update) | async-done | bytes 4194320 | tf_op jit(solution)/shard_map/all_gather | solution.py:41
  283.6 33.3 %all-gather.22.cloned.1.call-done = bf16[1024,1024]{1,0:T(8,128)(2,1)} async-done(((bf16[512,1024]{1,0:T(8,128)(2,1)}), bf16[1024,1024]{1,0:T(8,128)(2,1)}) %all-gather.22.cloned.1.call-update) | async-done | bytes 2097168 | tf_op jit(solution)/shard_map/all_gather | solution.py:130
  327.5 42.5 %all-gather.26.cloned.1.call-done = bf16[2048,1024]{0,1:T(8,128)(2,1)} async-done(((bf16[2048,64]{0,1:T(8,128)(2,1)}), bf16[2048,1024]{0,1:T(8,128)(2,1)}) %all-gather.26.cloned.1.call-update) | async-done | bytes 4194320 | tf_op jit(solution)/shard_map/all_gather | solution.py:43
  369.9 33.3 %all-gather.28.cloned.1.call-done = bf16[1024,1024]{1,0:T(8,128)(2,1)} async-done(((bf16[512,1024]{1,0:T(8,128)(2,1)}), bf16[1024,1024]{1,0:T(8,128)(2,1)}) %all-gather.28.cloned.1.call-update) | async-done | bytes 2097168 | tf_op jit(solution)/shard_map/all_gather | solution.py:145
  403.2 13.7 %fusion.98 = (bf16[2048]{0:T(1024)(128)(2,1)}, bf16[1024,2048]{1,0:T(8,128)(2,1)S(1)}) fusion(f32[1024,2048]{1,0:T(8,128)} %fusion.104, f32[2048]{0:T(1024)S(1)} %bitcast.278, bf16[1024,1024]{1,0:T(8,128)(2,1)} %all-gather.28.cloned.1.call-done, bf16[2048,1024]{0,1:T(8,128)(2,1)} %all-gather.26.cloned.1.call-done), kind=kOutput, calls=%fused_computation.181 | convolution fusion | flops 4341102592 | bytes 18886656 | tf_op jit(solution)/shard_map/rd,fd->rf/dot_general | solution.py:148
  424.8 31.9 %reduce-scatter.21.cloned.1.call-done = bf16[512,1024]{1,0:T(8,128)(2,1)} async-done(((bf16[1024,1024]{1,0:T(8,128)(2,1)}), bf16[512,1024]{1,0:T(8,128)(2,1)}) %reduce-scatter.21.cloned.1.call-update) | async-done | bytes 1048592 | tf_op jit(solution)/shard_map/reduce_scatter | solution.py:154
  465.0 33.2 %all-gather.30.cloned.1.call-done = bf16[1024,1024]{1,0:T(8,128)(2,1)} async-done(((bf16[512,1024]{1,0:T(8,128)(2,1)}), bf16[1024,1024]{1,0:T(8,128)(2,1)}) %all-gather.30.cloned.1.call-update) | async-done | bytes 2097168 | tf_op jit(solution)/shard_map/all_gather | solution.py:165
  514.1 79.4 %while.29 = (s32[]{:T(128)}, f32[1,1024,8,64]{1,3,2,0:T(8,128)}, f32[1,1024,8,64]{1,3,2,0:T(8,128)}, bf16[2,512,8,64]{1,3,2,0:T(8,128)(2,1)}, bf16[2,512,8,64]{1...) while((s32[]{:T(128)}, f32[1,1024,8,64]{1,3,2,0:T(8,128)}, ...), condition=%wide.region_15.16_spmd, body=%wide.region_13.15_spmd.sunk | while | flops 2736779264 | bytes 177848512 | solution.py:202
  614.1 33.7 %all-reduce.5 = (bf16[512]{0:T(512)(128)(2,1)S(1)}, bf16[512]{0:T(512)(128)(2,1)S(1)}, bf16[2048]{0:T(1024)(128)(2,1)S(1)}, bf16[512]{0:T(512)(128)(2,1)S(1)}) all-reduce(bf16[512]{0:T(512)(128)(2,1)S(1)} %dynamic-update-slice.1, bf16[512]{0:T(512)(128)(2,1)S(1)} %dynamic_slice.61, ...), channel_id=1, replica_groups=mesh['dp'=16,'tensor'=2] {'dp'}, use_global_device_ids=true, to_apply=%add.1 | all-reduce | flops 3584 | bytes 14336
  672.6 15.0 %reduce-scatter.19.cloned.1.call-done = bf16[512,1024]{1,0:T(8,128)(2,1)} async-done(((bf16[1024,1024]{1,0:T(8,128)(2,1)}), bf16[512,1024]{1,0:T(8,128)(2,1)}) %reduce-scatter.19.cloned.1.call-update) | async-done | bytes 1048592 | tf_op jit(solution)/shard_map/reduce_scatter | solution.py:137
  742.2 42.8 %reduce-scatter.33.cloned.1.call-done = bf16[2048,64]{0,1:T(8,128)(2,1)} async-done(((bf16[2048,1024]{0,1:T(8,128)(2,1)}), bf16[2048,64]{0,1:T(8,128)(2,1)}) %reduce-scatter.33.cloned.1.call-update) | async-done | bytes 262160 | tf_op jit(solution)/shard_map/reduce_scatter | solution.py:277
  786.7 74.4 %reduce-scatter.31.cloned.1.call-done = bf16[64,2048]{1,0:T(8,128)(2,1)} async-done(((bf16[1024,2048]{1,0:T(8,128)(2,1)}), bf16[64,2048]{1,0:T(8,128)(2,1)}) %reduce-scatter.31.cloned.1.call-update) | async-done | bytes 262160 | tf_op jit(solution)/shard_map/reduce_scatter | solution.py:271
  864.7 54.4 %reduce-scatter.37.cloned.1.call-done = bf16[32,2]{1,0:T(8,128)(2,1)} async-done(((bf16[512,2]{1,0:T(8,128)(2,1)}), bf16[32,2]{1,0:T(8,128)(2,1)}) %reduce-scatter.37.cloned.1.call-update) | async-done | bytes 144
  920.4 58.5 %reduce-scatter.29.cloned.1.call-done = bf16[512,64]{0,1:T(8,128)(2,1)} async-done(((bf16[512,1024]{0,1:T(8,128)(2,1)}), bf16[512,64]{0,1:T(8,128)(2,1)}) %reduce-scatter.29.cloned.1.call-update) | async-done | bytes 65552 | tf_op jit(solution)/shard_map/reduce_scatter | solution.py:265
  994.8 42.8 %reduce-scatter.39.cloned.1.call-done = bf16[32,6]{1,0:T(8,128)(2,1)} async-done(((bf16[512,6]{1,0:T(8,128)(2,1)}), bf16[32,6]{1,0:T(8,128)(2,1)}) %reduce-scatter.39.cloned.1.call-update) | async-done | bytes 400
  1038.9 67.9 %reduce-scatter.27.cloned.1.call-done = bf16[64,3,512]{2,0,1:T(8,128)(2,1)} async-done(((bf16[1024,3,512]{2,0,1:T(8,128)(2,1)}), bf16[64,3,512]{2,0,1:T(8,128)(2,1)}) %reduce-scatter.27.cloned.1.call-update) | async-done | bytes 196624 | tf_op jit(solution)/shard_map/reduce_scatter | solution.py:259
  1108.5 86.9 %reduce-scatter.35.cloned.1.call-done = bf16[64,6,512]{2,0,1:T(8,128)(2,1)} async-done(((bf16[1024,6,512]{2,0,1:T(8,128)(2,1)}), bf16[64,6,512]{2,0,1:T(8,128)(2,1)}) %reduce-scatter.35.cloned.1.call-update) | async-done | bytes 393232 | tf_op jit(solution)/shard_map/reduce_scatter | solution.py:283
  (273 shorter events, 340.8 us)
Async XLA Ops:
  7.2 67.7 %all-gather.14.cloned.1.call-start = ((), (), s32[]{:S(2)}) async-start(), calls=%async_computation.12 | async-start | bytes 6684672 | tf_op jit(solution)/shard_map/all_gather | solution.py:45
  7.9 135.5 %all-gather.18.cloned.1.call-start = ((), (), s32[]{:S(2)}) async-start(), calls=%async_computation.14 | async-start | bytes 3342336 | tf_op jit(solution)/shard_map/all_gather | solution.py:37
  8.7 146.7 %all-gather.16.cloned.1.call-start = ((), (), s32[]{:S(2)}) async-start(), calls=%async_computation.13 | async-start | bytes 3145728 | tf_op jit(solution)/shard_map/all_gather | solution.py:77
  93.0 102.3 %all-gather.20.cloned.1.call-start = ((), (), s32[]{:S(2)}) async-start(), calls=%async_computation.15 | async-start | bytes 1114112 | tf_op jit(solution)/shard_map/all_gather | solution.py:39
  93.6 136.9 %reduce-scatter.17.cloned.1.call-start = ((), (), s32[]{:S(2)}) async-start(), calls=%async_computation.16 | async-start | bytes 3145728 | tf_op jit(solution)/shard_map/reduce_scatter | solution.py:117
  199.6 84.0 %all-gather.24.cloned.1.call-start = ((), (), s32[]{:S(2)}) async-start(), calls=%async_computation.18 | async-start | bytes 4456448 | tf_op jit(solution)/shard_map/all_gather | solution.py:41
  200.2 116.6 %all-gather.22.cloned.1.call-start = ((), (), s32[]{:S(2)}) async-start(), calls=%async_computation.17 | async-start | bytes 3145728 | tf_op jit(solution)/shard_map/all_gather | solution.py:130
  233.1 226.9 %copy-start.19 = (f32[512]{0:T(512)}, f32[512]{0:T(512)S(1)}, u32[]{:S(2)}) copy-start(f32[512]{0:T(512)S(1)} %broadcast_multiply_fusion.5) | copy-start | bytes 6148
  233.5 226.6 %copy-start.23 = (f32[512]{0:T(512)}, f32[512]{0:T(512)S(1)}, u32[]{:S(2)}) copy-start(f32[512]{0:T(512)S(1)} %add_rsqrt_fusion) | copy-start | bytes 6148
  238.8 131.2 %all-gather.26.cloned.1.call-start = ((), (), s32[]{:S(2)}) async-start(), calls=%async_computation.19 | async-start | bytes 4456448 | tf_op jit(solution)/shard_map/all_gather | solution.py:43
  239.6 163.7 %all-gather.28.cloned.1.call-start = ((), (), s32[]{:S(2)}) async-start(), calls=%async_computation.21 | async-start | bytes 3145728 | tf_op jit(solution)/shard_map/all_gather | solution.py:145
  240.3 216.5 %reduce-scatter.21.cloned.1.call-start = ((), (), s32[]{:S(2)}) async-start(), calls=%async_computation.22 | async-start | bytes 3145728 | tf_op jit(solution)/shard_map/reduce_scatter | solution.py:154
  261.6 141.6 %copy-start.29 = (f32[16,1,128]{2,1,0:T(1,128)}, f32[16,1,128]{2,1,0:T(1,128)S(1)}, u32[]{:S(2)}) copy-start(f32[16,1,128]{2,1,0:T(1,128)S(1)} %convert_element_type.268) | copy-start | bytes 24580
  424.7 73.5 %all-gather.30.cloned.1.call-start = ((), (), s32[]{:S(2)}) async-start(), calls=%async_computation.23 | async-start | bytes 3145728 | tf_op jit(solution)/shard_map/all_gather | solution.py:165
  465.0 194.4 %reduce-scatter.23.cloned.1.call-start = ((), (), s32[]{:S(2)}) async-start(), calls=%async_computation.24 | async-start | bytes 3145728 | tf_op jit(solution)/shard_map/reduce_scatter | solution.py:221
  611.3 76.3 %reduce-scatter.19.cloned.1.call-start = ((), (), s32[]{:S(2)}) async-start(), calls=%async_computation.20 | async-start | bytes 3145728 | tf_op jit(solution)/shard_map/reduce_scatter | solution.py:137
  659.3 67.4 %reduce-scatter.25.cloned.1.call-start = ((), (), s32[]{:S(2)}) async-start(), calls=%async_computation.25 | async-start | bytes 49152 | tf_op jit(solution)/shard_map/reduce_scatter | solution.py:244
  698.9 86.0 %reduce-scatter.33.cloned.1.call-start = ((), (), s32[]{:S(2)}) async-start(), calls=%async_computation.29 | async-start | bytes 4456448 | tf_op jit(solution)/shard_map/reduce_scatter | solution.py:277
  709.9 151.3 %reduce-scatter.31.cloned.1.call-start = ((), (), s32[]{:S(2)}) async-start(), calls=%async_computation.28 | async-start | bytes 4456448 | tf_op jit(solution)/shard_map/reduce_scatter | solution.py:271
  719.3 199.8 %reduce-scatter.37.cloned.1.call-start = ((), (), s32[]{:S(2)}) async-start(), calls=%async_computation.31 | async-start | bytes 139264
  722.0 256.9 %reduce-scatter.29.cloned.1.call-start = ((), (), s32[]{:S(2)}) async-start(), calls=%async_computation.27 | async-start | bytes 1114112 | tf_op jit(solution)/shard_map/reduce_scatter | solution.py:265
  726.6 311.0 %reduce-scatter.39.cloned.1.call-start = ((), (), s32[]{:S(2)}) async-start(), calls=%async_computation.32 | async-start | bytes 139264
  728.2 378.6 %reduce-scatter.27.cloned.1.call-start = ((), (), s32[]{:S(2)}) async-start(), calls=%async_computation.26 | async-start | bytes 3342336 | tf_op jit(solution)/shard_map/reduce_scatter | solution.py:259
  736.2 459.3 %reduce-scatter.35.cloned.1.call-start = ((), (), s32[]{:S(2)}) async-start(), calls=%async_computation.30 | async-start | bytes 6684672 | tf_op jit(solution)/shard_map/reduce_scatter | solution.py:283
  (45 other events, 446.1 us)
Sparse Core Ops, SparseCore 0:
  10.2 64.6 all-gather.13
  77.1 44.0 all-gather.17
  123.3 32.0 all-gather.15
  157.4 37.9 all-gather.19
  199.7 30.7 reduce-scatter.16
  232.8 50.7 all-gather.23
  285.2 31.5 all-gather.21
  319.2 50.7 all-gather.25
  371.6 31.5 all-gather.27
  424.9 31.8 reduce-scatter.20
  465.1 33.1 all-gather.29
  611.4 31.8 reduce-scatter.22
  659.4 28.1 reduce-scatter.18
  699.0 9.8 reduce-scatter.24
  712.6 72.3 reduce-scatter.32
  789.2 71.9 reduce-scatter.30
  865.0 54.0 reduce-scatter.36
  922.6 56.3 reduce-scatter.28
  983.3 54.1 reduce-scatter.38
  1041.7 65.0 reduce-scatter.26
  1111.3 84.1 reduce-scatter.34
where the time goes:
time: 1210 us; the launch traced here: 1200 us
  waiting for transfers between devices  725 us (60%)
  matrix products  181 us (15%)
  blocking collectives  135 us (11%)
  other arithmetic  108 us (9%)
  local copies, waits for them, and re-layouts  36.9 us (3%)
  between operations  17 us (1%)
    unnamed x23, waiting for transfers between devices  101 us
    reduce_scatter x1, waiting for transfers between devices, shards(): lax.psum_scatter(grad_ada.astype(jnp.bfloat16), 'dp', scatter_dimension=0...  86.9 us
    reduce_scatter x1, waiting for transfers between devices, shards(): lax.psum_scatter(grad_fc1.astype(jnp.bfloat16), 'dp', scatter_dimension=0...  74.4 us
    reduce_scatter x1, waiting for transfers between devices, shards(): lax.psum_scatter(grad_qkv_w.astype(jnp.bfloat16), 'dp', scatter_dimension...  67.9 us
    unnamed x2, blocking collectives  64.3 us
    reduce_scatter x1, waiting for transfers between devices, shards(): lax.psum_scatter(grad_proj.astype(jnp.bfloat16), 'dp', scatter_dimension=...  58.5 us
    reduce_scatter x1, waiting for transfers between devices, shards(): lax.psum_scatter(grad_fc2.astype(jnp.bfloat16), 'dp', scatter_dimension=1...  42.8 us
    all_gather x1, waiting for transfers between devices, shards(): lax.all_gather(w_fc2, 'dp', axis=1, tiled=True)  42.5 us
  transfers between devices with their start and end apart: 21, of which 18 were waited for; matrix products, arithmetic and copies ran while one was open for 14% of the time, Pallas kernels for 0%

commit v1 on v0

v1 whole, which is shorter than its diff:
```python
import math
from functools import partial

import jax
import jax.numpy as jnp
from jax import lax
from jax.experimental import pallas as pl
from jax.experimental.pallas import tpu as pltpu
from jax.sharding import PartitionSpec as P

HEAD_DIM = 64
LEN = 1024
PAIR = 2 * HEAD_DIM

norm_eps = 1e-06
highest = lax.Precision.HIGHEST
f32 = jnp.float32
bf16 = jnp.bfloat16

score_scale = HEAD_DIM ** (-0.5)
log2_scale = score_scale * math.log2(math.e)


def dot_nn(a, b):
    return lax.dot_general(a, b, (((1,), (0,)), ((), ())), preferred_element_type=f32)


def dot_nt(a, b):
    return lax.dot_general(a, b, (((1,), (1,)), ((), ())), preferred_element_type=f32)


def dot_tn(a, b):
    return lax.dot_general(a, b, (((0,), (0,)), ((), ())), preferred_element_type=f32)


def head_masks():
    lane = lax.broadcasted_iota(jnp.int32, (1, PAIR), 1)
    return [(lane < HEAD_DIM), (lane >= HEAD_DIM)]


def attend_kernel(step_rows, q_ref, k_ref, v_ref, o_ref, lse_ref):
    rows = q_ref.shape[0]
    masks = head_masks()
    keys = k_ref[...]
    values_t = v_ref[...].astype(f32).T.astype(bf16)
    sub = lax.broadcasted_iota(jnp.int32, (PAIR, 1), 0)
    for start in range(0, rows, step_rows):
        queries = q_ref[start : start + step_rows, :]
        out_t = []
        for head in range(2):
            q_head = jnp.where(masks[head], queries, jnp.zeros_like(queries))
            scores = dot_nt(keys, q_head) * log2_scale
            peak = jnp.max(scores, 0, keepdims=True)
            terms = jnp.exp2(scores - peak)
            total = jnp.sum(terms, 0, keepdims=True)
            out_t.append(dot_nn(values_t, terms.astype(bf16)) * (1.0 / total))
            lse_ref[0, head : head + 1, start : start + step_rows] = peak + jnp.log2(total)
        joined = jnp.where(sub < HEAD_DIM, out_t[0], out_t[1])
        o_ref[start : start + step_rows, :] = joined.T.astype(bf16)


def attend(qkv, local_width):
    rows = qkv.shape[0]
    pairs = local_width // PAIR
    heads = local_width // HEAD_DIM
    spec = [
        pl.BlockSpec((rows, PAIR), partial(lambda part, i: (0, part * pairs + i), part))
        for part in range(3)
    ]
    return pl.pallas_call(
        partial(attend_kernel, 256),
        grid=(pairs,),
        in_specs=spec,
        out_specs=[
            pl.BlockSpec((rows, PAIR), lambda i: (0, i)),
            pl.BlockSpec((1, 2, rows), lambda i: (i, 0, 0)),
        ],
        out_shape=[
            jax.ShapeDtypeStruct((rows, local_width), bf16),
            jax.ShapeDtypeStruct((pairs, 2, rows), f32),
        ],
        compiler_params=pltpu.CompilerParams(vmem_limit_bytes=48 * 1024 * 1024),
        cost_estimate=pl.CostEstimate(
            flops=4 * heads * rows * rows * 256,
            bytes_accessed=rows * local_width * 8,
            transcendentals=heads * rows * rows,
        ),
        name="attend",
    )(qkv, qkv, qkv)


def attend_back_kernel(step_rows, q_ref, k_ref, v_ref, do_ref, lse_ref, dqkv_ref):
    rows = q_ref.shape[0]
    masks = head_masks()
    keys = k_ref[...]
    values = v_ref[...]
    sub = lax.broadcasted_iota(jnp.int32, (PAIR, 1), 0)
    keys_t = keys.astype(f32).T.astype(bf16)
    d_keys = jnp.zeros((rows, PAIR), f32)
    d_values = jnp.zeros((rows, PAIR), f32)
    for start in range(0, rows, step_rows):
        queries = q_ref[start : start + step_rows, :]
        d_out = do_ref[start : start + step_rows, :]
        dq_t = []
        for head in range(2):
            q_head = jnp.where(masks[head], queries, jnp.zeros_like(queries))
            do_head = jnp.where(masks[head], d_out, jnp.zeros_like(d_out))
            lse = lse_ref[0, head : head + 1, start : start + step_rows]
            probs = jnp.exp2(dot_nt(keys, q_head) * log2_scale - lse)
            d_probs = dot_nt(values, do_head)
            weighted = probs * d_probs
            row_dot = jnp.sum(weighted, 0, keepdims=True)
            d_scores = (weighted - probs * row_dot).astype(bf16)
            d_values = d_values + dot_nn(probs.astype(bf16), do_head)
            d_keys = d_keys + dot_nn(d_scores, q_head)
            dq_t.append(dot_nn(keys_t, d_scores))
        joined = jnp.where(sub < HEAD_DIM, dq_t[0], dq_t[1])
        dqkv_ref[0, start : start + step_rows, :] = (joined.T * score_scale).astype(bf16)
    dqkv_ref[1] = (d_keys * score_scale).astype(bf16)
    dqkv_ref[2] = d_values.astype(bf16)


def attend_back(qkv, grad_heads, lse, local_width):
    rows = qkv.shape[0]
    pairs = local_width // PAIR
    heads = local_width // HEAD_DIM
    spec = [
        pl.BlockSpec((rows, PAIR), partial(lambda part, i: (0, part * pairs + i), part))
        for part in range(3)
    ]
    return pl.pallas_call(
        partial(attend_back_kernel, 256),
        grid=(pairs,),
        in_specs=spec
        + [
            pl.BlockSpec((rows, PAIR), lambda i: (0, i)),
            pl.BlockSpec((1, 2, rows), lambda i: (i, 0, 0)),
        ],
        out_specs=pl.BlockSpec((3, rows, PAIR), lambda i: (0, 0, i)),
        out_shape=jax.ShapeDtypeStruct((3, rows, local_width), bf16),
        compiler_params=pltpu.CompilerParams(vmem_limit_bytes=48 * 1024 * 1024),
        cost_estimate=pl.CostEstimate(
            flops=10 * heads * rows * rows * 256,
            bytes_accessed=rows * local_width * 14,
            transcendentals=heads * rows * rows,
        ),
        name="attend_back",
    )(qkv, qkv, qkv, grad_heads, lse)


def normalize(values):
    centred = values - jnp.mean(values, -1, keepdims=True)
    rstd = lax.rsqrt(jnp.mean(centred * centred, -1, keepdims=True) + norm_eps)
    return (centred * rstd, rstd)


def norm_back(grad_n, normed, rstd):
    first = jnp.mean(grad_n, -1, keepdims=True)
    second = jnp.mean(grad_n * normed, -1, keepdims=True)
    return rstd * (grad_n - first - normed * second)


def gelu_both(v):
    c = math.sqrt(2.0 / math.pi)
    sq = v * v
    th = jnp.tanh(c * v * (1.0 + 0.044715 * sq))
    half = 0.5 * (1.0 + th)
    slope = half + 0.5 * v * (1.0 - th * th) * c * (1.0 + 3 * 0.044715 * sq)
    return v * half, slope


def shift(x, axis, step):
    size = lax.axis_size(axis)
    return lax.ppermute(x, axis, [(i, (i + step) % size) for i in range(size)])


def xor_step(x, axis, bit):
    size = lax.axis_size(axis)
    return lax.ppermute(x, axis, [(i, i ^ bit) for i in range(size)])


def xor_gather(x, axis):
    size, bit = lax.axis_size(axis), 1
    out = x[None]
    while bit < size:
        out = jnp.concatenate([out, xor_step(out, axis, bit)], 0)
        bit *= 2
    return out


def xor_scatter_sum(x, axis):
    half = lax.axis_size(axis) // 2
    while half:
        x = x[:half] + xor_step(x[half:], axis, half)
        half //= 2
    return x[0]


def xor_sum(x, axis):
    size, bit = lax.axis_size(axis), 1
    while bit < size:
        x = x + xor_step(x, axis, bit)
        bit *= 2
    return x


def sort_xor(x, axis):
    size = lax.axis_size(axis)
    me = lax.axis_index(axis)
    order = jnp.arange(size, dtype=jnp.int32)
    pick = ((order[:, None] ^ me) == order[None, :]).astype(f32)
    flat = x.reshape(size, -1).astype(f32)
    return jnp.dot(pick, flat, precision=highest).reshape(x.shape)


def rel_gather(x, axis):
    return [x] + [shift(x, axis, s) for s in range(1, lax.axis_size(axis))]


def sort_rel(parts, axis):
    size = lax.axis_size(axis)
    me = lax.axis_index(axis)
    out = []
    for target in range(size):
        value = jnp.zeros_like(parts[0])
        for s in range(size):
            value = jnp.where(lax.rem(me - s + size, size) == target, parts[s], value)
        out.append(value)
    return out


def shards(
    tokens, cond, cotangent, w_qkv, b_qv, w_proj, b_proj, w_fc1, b_fc1, w_fc2, b_fc2, w_ada, b_ada
):
    tensor_size = lax.axis_size("tensor")
    dp_size = lax.axis_size("dp")
    tensor_pos = lax.axis_index("tensor")
    dp_pos = lax.axis_index("dp")
    row_count, width = tokens.shape
    group_rows = row_count * tensor_size
    depth = w_qkv.shape[0]
    local_width = w_qkv.shape[2]
    hidden = w_fc1.shape[1]
    assert cond.shape[0] == 1 and group_rows == LEN

    proj_t = w_proj.T
    proj_parts = rel_gather(proj_t, "tensor")
    attn_shard = jnp.concatenate([w_qkv.reshape(depth, 3 * local_width)] + proj_parts, 1)
    mlp_shard = jnp.concatenate([w_fc1, w_fc2.T], 1)
    attn_w = lax.all_gather(attn_shard, "dp", axis=0, tiled=True)
    mlp_w = lax.all_gather(mlp_shard, "dp", axis=0, tiled=True)
    qkv_w = attn_w[:, : 3 * local_width]
    proj_w = attn_w[:, 3 * local_width :]
    fc1_w = mlp_w[:, :hidden]
    fc2_w = mlp_w[:, hidden:]

    tok_parts = rel_gather(tokens, "tensor")
    vectors = jnp.concatenate(
        [b_qv.reshape(-1), b_proj, b_fc1, b_fc2, b_ada.reshape(-1)]
    )
    vec_size = vectors.shape[0]
    packed = jnp.concatenate([cond.reshape(-1)] + rel_gather(vectors, "tensor"))
    packed = xor_gather(packed, "dp")
    cond_all = packed[:, :width]
    vec_all = sort_xor(packed[:, width:], "dp").reshape(dp_size, tensor_size, vec_size)
    vec_sorted = sort_rel([vec_all[:, s] for s in range(tensor_size)], "tensor")
    own_vec = vec_all[:, 0]
    piece = b_proj.shape[0]
    n_fc1 = b_fc1.shape[0]
    at_proj = 2 * piece
    at_fc1 = at_proj + piece
    at_fc2 = at_fc1 + n_fc1
    at_ada = at_fc2 + piece
    qv_bias = own_vec[:, :at_proj].reshape(dp_size, 2, piece).transpose(1, 0, 2).reshape(2, local_width)
    fc1_bias = own_vec[:, at_fc1:at_fc2].reshape(hidden)
    ada_bias = (
        own_vec[:, at_ada:].reshape(dp_size, 6, piece).transpose(1, 0, 2).reshape(6, local_width)
    )
    proj_bias = jnp.concatenate([v[:, at_proj:at_fc1].reshape(-1) for v in vec_sorted])
    fc2_bias = jnp.concatenate([v[:, at_fc2:at_ada].reshape(-1) for v in vec_sorted])

    silu_all = jax.nn.silu(cond_all.astype(f32)).astype(bf16)
    silu_own = lax.dynamic_slice(silu_all, (0, dp_pos * depth), (dp_size, depth))
    ada_flat = w_ada.reshape(depth, 6 * local_width)
    mod_part = dot_nn(silu_own, ada_flat)
    mod_half = xor_scatter_sum(mod_part, "dp").reshape(6, local_width) + ada_bias
    modul = jnp.concatenate(sort_rel(rel_gather(mod_half, "tensor"), "tensor"), 1)
    shift_one, scale_one, gate_one, shift_two, scale_two, gate_two = [
        modul[k : k + 1] for k in range(6)
    ]

    inputs = jnp.concatenate(tok_parts, 0).astype(f32)
    normed_one, rstd_one = normalize(inputs)
    hidden_one = (normed_one * (1.0 + scale_one) + shift_one).astype(bf16)
    bias_three = jnp.concatenate([qv_bias[0], jnp.zeros_like(qv_bias[0]), qv_bias[1]])
    qkv = (dot_nn(hidden_one, qkv_w) + bias_three).astype(bf16)
    heads_out, lse = attend(qkv, local_width)
    heads_parts = [
        jnp.roll(part, s * row_count, 0)
        for s, part in enumerate(rel_gather(heads_out, "tensor"))
    ]
    heads_all = jnp.concatenate(heads_parts, 1)
    branch_attn = dot_nt(heads_all, proj_w) + proj_bias
    middle = inputs + gate_one * branch_attn
    normed_two, rstd_two = normalize(middle)
    hidden_two = (normed_two * (1.0 + scale_two) + shift_two).astype(bf16)

    cot_all = jnp.concatenate(rel_gather(cotangent, "tensor"), 0)
    grad_m = (gate_two * cot_all.astype(f32)).astype(bf16)
    grad_act = dot_nn(grad_m, fc2_w)
    pre_act = dot_nn(hidden_two, fc1_w) + fc1_bias
    activ, slope = gelu_both(pre_act)
    activ = activ.astype(bf16)
    grad_pre = (grad_act * slope).astype(bf16)

    def to_owners(rows_full, weight):
        own = dot_nt(rows_full[:row_count], weight)
        for s in range(1, tensor_size):
            part = dot_nt(rows_full[s * row_count : (s + 1) * row_count], weight).astype(bf16)
            own = own + shift(part, "tensor", -s).astype(f32)
        return own

    grad_hidden_two = to_owners(grad_pre, fc1_w)
    branch_mlp = dot_nt(activ, fc2_w)
    mlp_own = branch_mlp[:row_count]
    for s in range(1, tensor_size):
        part = branch_mlp[s * row_count : (s + 1) * row_count].astype(bf16)
        mlp_own = mlp_own + shift(part, "tensor", -s).astype(f32)
    branch_mlp = mlp_own + fc2_bias
    grad_out = cotangent.astype(f32)
    mid_own = middle[:row_count]
    block_out = (mid_own + gate_two * branch_mlp).astype(bf16)
    mlp_grads = jnp.concatenate(
        [dot_tn(hidden_two, grad_pre).astype(bf16), dot_tn(grad_m, activ).astype(bf16)], 1
    )
    mlp_grads = lax.psum_scatter(mlp_grads, "dp", scatter_dimension=0, tiled=True)

    n2, r2 = normed_two[:row_count], rstd_two[:row_count]
    grad_mid = grad_out + norm_back(grad_hidden_two * (1.0 + scale_two), n2, r2)
    grad_a = (gate_one * grad_mid).astype(bf16)
    grad_heads_all = dot_nn(grad_a, proj_w).astype(bf16)
    grad_heads = [grad_heads_all[:, :local_width]]
    for j in range(1, tensor_size):
        s = tensor_size - j
        part = grad_heads_all[:, s * local_width : (s + 1) * local_width]
        grad_heads.append(shift(part, "tensor", -s))
    grad_heads = jnp.concatenate(grad_heads, 0)
    grad_a_rows = jnp.concatenate(rel_gather(grad_a, "tensor"), 0)
    grad_proj = dot_tn(grad_a_rows, heads_out).astype(bf16)
    dqkv = attend_back(qkv, grad_heads, lse, local_width)
    dqkv = jnp.concatenate([dqkv[0], dqkv[1], dqkv[2]], 1)
    grad_hidden_one = to_owners(dqkv, qkv_w)
    attn_grads = jnp.concatenate([dot_tn(hidden_one, dqkv).astype(bf16), grad_proj], 1)
    attn_grads = lax.psum_scatter(attn_grads, "dp", scatter_dimension=0, tiled=True)

    n1, r1 = normed_one[:row_count], rstd_one[:row_count]
    grad_tokens = (
        grad_mid + norm_back(grad_hidden_one * (1.0 + scale_one), n1, r1)
    ).astype(bf16)

    def row_sum(v):
        return jnp.sum(v, 0, dtype=f32)

    grad_mod = jnp.stack(
        [
            row_sum(grad_hidden_one),
            row_sum(grad_hidden_one * n1),
            row_sum(grad_mid * branch_attn[:row_count]),
            row_sum(grad_hidden_two),
            row_sum(grad_hidden_two * n2),
            row_sum(grad_out * branch_mlp),
        ]
    )

    def cols_of(values, owner):
        return lax.dynamic_slice_in_dim(values, owner * local_width, local_width, values.ndim - 1)

    grad_mod_own = cols_of(grad_mod, tensor_pos)
    for s in range(1, tensor_size):
        owner = lax.rem(tensor_pos - s + tensor_size, tensor_size)
        grad_mod_own = grad_mod_own + shift(cols_of(grad_mod, owner), "tensor", -s)
    grad_mod_all = xor_gather(grad_mod_own.astype(bf16).reshape(6 * local_width), "dp")
    grad_ada = dot_tn(silu_own, grad_mod_all).reshape(depth, 6, local_width)
    ada_sum = jnp.sum(grad_mod_all, 0, dtype=f32).reshape(6, local_width)
    grad_ada_bias = lax.dynamic_slice_in_dim(ada_sum, dp_pos * piece, piece, 1)
    grad_silu_part = dot_nt(grad_mod_all, ada_flat)
    for s in range(1, tensor_size):
        grad_silu_part = grad_silu_part + shift(dot_nt(grad_mod_all, ada_flat), "tensor", s)
    grad_silu_all = xor_gather(grad_silu_part, "dp")
    order = jnp.arange(dp_size, dtype=jnp.int32)
    mine = (order[:, None] == order[None, :]).astype(f32)
    grad_silu = sort_xor(jnp.sum(grad_silu_all * mine[:, :, None], 1), "dp").reshape(1, width)
    _, silu_back = jax.vjp(jax.nn.silu, cond.astype(f32))
    grad_cond = silu_back(grad_silu)[0]

    grad_vec = jnp.concatenate(
        [
            row_sum(dqkv[:, :local_width].astype(f32)),
            row_sum(dqkv[:, 2 * local_width :].astype(f32)),
            cols_of(row_sum(grad_a_rows.astype(f32)), tensor_pos),
            row_sum(grad_pre.astype(f32)),
            cols_of(row_sum(grad_m.astype(f32)), tensor_pos),
        ]
    )
    grad_vec = xor_sum(grad_vec, "dp")

    def own_piece(start, size):
        return lax.dynamic_slice_in_dim(grad_vec, start + dp_pos * size, size, 0)

    grad_qv_bias = jnp.stack([own_piece(0, piece), own_piece(local_width, piece)])
    grad_proj_bias = own_piece(2 * local_width, piece)
    grad_fc1_bias = own_piece(3 * local_width, n_fc1)
    grad_fc2_bias = own_piece(3 * local_width + hidden, piece)

    attn_grads = attn_grads.astype(f32)
    mlp_grads = mlp_grads.astype(f32)
    return (
        block_out,
        grad_tokens,
        grad_cond,
        attn_grads[:, : 3 * local_width].reshape(depth, 3, local_width),
        grad_qv_bias,
        attn_grads[:, 3 * local_width :].T,
        grad_proj_bias,
        mlp_grads[:, :hidden],
        grad_fc1_bias,
        mlp_grads[:, hidden:].T,
        grad_fc2_bias,
        grad_ada,
        grad_ada_bias,
    )


def solution(mesh):
    placed = (
        P(("dp", "tensor"), None),
        P("dp", None),
        P(("dp", "tensor"), None),
        P("dp", None, "tensor"),
        P(None, ("tensor", "dp")),
        P("tensor", "dp"),
        P(("tensor", "dp")),
        P("dp", "tensor"),
        P(("tensor", "dp")),
        P("tensor", "dp"),
        P(("tensor", "dp")),
        P("dp", None, "tensor"),
        P(None, ("tensor", "dp")),
    )
    return jax.shard_map(
        shards,
        mesh=mesh,
        in_specs=placed,
        out_specs=(
            P(("dp", "tensor"), None),
            P(("dp", "tensor"), None),
            P("dp", None),
            P("dp", None, "tensor"),
            P(None, ("tensor", "dp")),
            P("tensor", "dp"),
            P(("tensor", "dp")),
            P("dp", "tensor"),
            P(("tensor", "dp")),
            P("tensor", "dp"),
            P(("tensor", "dp")),
            P("dp", None, "tensor"),
            P(None, ("tensor", "dp")),
        ),
        check_vma=False,
    )
```

time: 1210 us -> 473 us (0.39)
  waiting for transfers between devices: 725 us -> 205 us
  blocking collectives: 135 us -> 0 us
  matrix products: 181 us -> 94.6 us
  other arithmetic: 108 us -> 34.4 us
  Pallas kernels: 0 us -> 50.7 us
  starting transfers between devices: 1.49 us -> 44.6 us
  local copies, waits for them, and re-layouts: 36.9 us -> 24.6 us
    reduce_scatter x10 -> x2, waiting for transfers between devices: 407 us -> 70.8 us  [the longest x1 70.8 us: shards(): lax.psum_scatter(mlp_grads, 'dp', scatter_dimension=0, tiled=True)]
    all_gather x9 -> x2, waiting for transfers between devices: 217 us -> 8.38 us  [the longest x1 4.7 us: shards(): attn_w = lax.all_gather(attn_shard, 'dp', axis=0, tiled=True)]
    ppermute x0 -> x33, waiting for transfers between devices: none -> 126 us  [the longest x13 80.2 us: shift(): return lax.ppermute(x, axis, [(i, (i + step) % size) for i in range(size)])]
    unnamed x23 -> x4, waiting for transfers between devices: 101 us -> 0.07 us
    dot_general x29 -> x19, matrix products: 181 us -> 94.6 us  [the longest x7 38.5 us: dot_nt(): lax.dot_general(a, b, (((1,), (1,)), ((), ())), preferred_element_type=f32)]
    all_gather x4 -> x0, blocking collectives: 66.3 us -> none  [the longest x1 23.6 us: shards(): lax.all_gather(b_ada, 'dp', axis=1, tiled=True)]
    unnamed x2 -> x0, blocking collectives: 64.3 us -> none
    convert_element_type x21 -> x5, other arithmetic: 54.3 us -> 2.36 us  [the longest x1 1.11 us: shards(): mlp_grads = mlp_grads.astype(f32)]
  transfers between devices with their start and end apart: 21 -> 37, of which waited for: 18 -> 29; matrix products, arithmetic and copies ran while one was open for 14% -> 26% of each run, Pallas kernels for 0% -> 11%
where the time goes in v1:
time: 473 us; the launch traced here: 469 us
  waiting for transfers between devices  205 us (43%)
  matrix products  94.6 us (20%)
  Pallas kernels  50.7 us (11%)
  starting transfers between devices  44.6 us (9%)
  other arithmetic  34.4 us (7%)
  local copies, waits for them, and re-layouts  24.6 us (5%)
  between operations  15.1 us (3%)
    ppermute x13, waiting for transfers between devices, shift(): return lax.ppermute(x, axis, [(i, (i + step) % size) for i in range(size)])  80.2 us
    reduce_scatter x1, waiting for transfers between devices, shards(): lax.psum_scatter(mlp_grads, 'dp', scatter_dimension=0, tiled=True)  70.8 us
    ppermute x20, waiting for transfers between devices, xor_step(): return lax.ppermute(x, axis, [(i, i ^ bit) for i in range(size)])  45.7 us
    dot_general x7, matrix products, dot_nt(): lax.dot_general(a, b, (((1,), (1,)), ((), ())), preferred_element_type=f32)  38.5 us
    dot_general x5, matrix products, dot_nn(): lax.dot_general(a, b, (((1,), (0,)), ((), ())), preferred_element_type=f32)  28.5 us
    pallas_call x1, Pallas kernels, attend_back(): pl.pallas_call(partial(attend_back_kernel, 256), grid=(pairs,), in_specs=...  27.9 us
    dot_general x5, matrix products, dot_tn(): lax.dot_general(a, b, (((0,), (0,)), ((), ())), preferred_element_type=f32)  27.2 us
    ppermute x20, starting transfers between devices, xor_step(): return lax.ppermute(x, axis, [(i, i ^ bit) for i in range(size)])  24 us
  transfers between devices with their start and end apart: 37, of which 29 were waited for; matrix products, arithmetic and copies ran while one was open for 26% of the time, Pallas kernels for 11%

profile of v1, /device:TPU:0, one launch (start us, length us, event | category | flops | bytes accessed | tf_op | source)
XLA Modules:
  0.0 469.0 jit_solution(4814308487526684248)
XLA Ops:
  43.1 4.7 %collective-permute-done.6 = f32[8,3072]{1,0:T(8,128)S(1)} collective-permute-done((f32[8,3072]{1,0:T(8,128)S(1)}, f32[8,3072]{1,0:T(8,128)S(1)}, u32[]{:S(2)}, u32[]{:S(2)}) %collective-permute-start.6) | collective-permute-done | bytes 98336 | tf_op jit(solution)/shard_map/ppermute | solution.py:179
  47.9 4.4 collective-permute-start.7
  68.0 4.7 %all-gather.3.cloned.1.call-done = bf16[1024,2560]{1,0:T(8,128)(2,1)} async-done(((bf16[64,2560]{1,0:T(8,128)(2,1)}), bf16[1024,2560]{1,0:T(8,128)(2,1)}) %all-gather.3.cloned.1.call-update) | async-done | bytes 5242896 | tf_op jit(solution)/shard_map/all_gather | solution.py:250
  72.7 7.1 %add_convert_fusion.q_ref.k_ref.v_ref = bf16[1024,1536]{1,0:T(8,128)(2,1)S(1)} fusion(f32[1536]{0:T(1024)S(1)} %pad_maximum_fusion.17, bf16[1024,2560]{1,0:T(8,128)(2,1)} %all-gather.3.cloned.1.call-done, f32[1024]{0:T(1024)S(1)} %bitcast.118, f32[1024]{0:T(1024)S(1)} %bitcast.102, f32[1024]{0:T(1024)S(1)} %add_rsqrt_fusion.1, ...), kind=kOutput, calls=%fused_computation.6 | convolution fusion | flops 3233808384 | bytes 8411136 | tf_op jit(solution)/shard_map/dot_general | solution.py:25
  79.8 22.8 %attend.1 = (bf16[1024,512]{1,0:T(8,128)(2,1)S(1)}, f32[4,2,1024]{2,1,0:T(2,128)S(1)}) custom-call(bf16[1024,1536]{1,0:T(8,128)(2,1)S(1)} %add_convert_fusion.q_ref.k_ref.v_ref, bf16[1024,1536]{1,0:T(8,128)(2,1)S(1)} %add_convert_fusion.q_ref.k_ref.v_ref, bf16[1024,1536]{1,0:T(8,128)(2,1)S(1)} %add_convert_fusion.q_ref.k_ref.v_ref), custom_call_target="tpu_custom_call" | custom-call | flops 8589934592 | bytes 4194304 | tf_op jit(solution)/shard_map/attend/pallas_call | solution.py:70
  105.2 23.6 %collective-permute-done.12 = bf16[1024,512]{1,0:T(8,128)(2,1)} collective-permute-done((bf16[1024,512]{1,0:T(8,128)(2,1)S(1)}, bf16[1024,512]{1,0:T(8,128)(2,1)}, u32[]{:S(2)}, u32[]{:S(2)}) %collective-permute-start.12) | collective-permute-done | bytes 1048608 | tf_op jit(solution)/shard_map/ppermute | solution.py:174
  130.1 10.7 %fusion.72 = (f32[1024]{0:T(1024)S(1)}, f32[1024,1024]{1,0:T(8,128)S(1)}, f32[1024,1024]{1,0:T(8,128)}, f32[1024,1024]{1,0:T(8,128)}) fusion(f32[1024]{0:T(1024)S(1)} %bitcast.112, bf16[512,1024]{1,0:T(8,128)(2,1)} %copy-done.13, bf16[512,1024]{1,0:T(8,128)(2,1)S(1)} %copy-done.11, f32[1024]{0:T(1024)S(1)} %add_rsqrt_fusion.1, ...), kind=kOutput, calls=%fused_computation.172 | convolution fusion | flops 2164259840 | bytes 18894848 | tf_op jit(solution)/shard_map/dot_general | solution.py:29
  149.0 8.1 %fusion.10 = f32[1024,2048]{1,0:T(8,128)S(1)} fusion(bf16[1024,4096]{1,0:T(8,128)(2,1)} %all-gather.5.cloned.1.call-done, f32[1024,1024]{1,0:T(8,128)} %subtract_multiply_fusion, f32[1024]{0:T(1024)S(1)} %bitcast.116, f32[1024]{0:T(1024)S(1)} %bitcast.108), kind=kOutput, calls=%fused_computation.31 | convolution fusion | flops 4298113024 | bytes 16785408 | tf_op jit(solution)/shard_map/dot_general | solution.py:25
  157.2 9.3 %convert_reduce_fusion = (f32[2048]{0:T(1024)S(1)}, bf16[1024,2048]{1,0:T(8,128)(2,1)S(1)}) fusion(f32[1024,2048]{1,0:T(8,128)S(1)} %fusion.10, f32[2048]{0:T(1024)S(1)} %slice_bitcast_fusion.5, bf16[1024,4096]{1,0:T(8,128)(2,1)S(1)} %copy-done.32, bf16[512,1024]{1,0:T(8,128)(2,1)} %collective-permute-done.14, bf16[512,1024]{1,0:T(8,128)(2,1)S(1)} %copy-done.8, ...), kind=kOutput, calls=%fused_computation.1 | convolution fusion | flops 4345296896 | bytes 18894848 | tf_op jit(solution)/shard_map/dot_general | solution.py:25
  172.4 8.0 %fusion.4 = f32[1024,1024]{1,0:T(8,128)S(1)} fusion(bf16[1024,4096]{1,0:T(8,128)(2,1)S(1)} %copy-done.32, f32[1024,2048]{1,0:T(8,128)} %copy-done.34, f32[2048]{0:T(1024)S(1)} %slice_bitcast_fusion.5), kind=kOutput, calls=%fused_computation.25 | convolution fusion | flops 4315938816 | bytes 16785408 | tf_op jit(solution)/shard_map/dot_general | solution.py:29
  181.5 15.4 %collective-permute-done.15 = bf16[512,1024]{1,0:T(8,128)(2,1)S(1)} collective-permute-done((bf16[512,1024]{1,0:T(8,128)(2,1)S(1)}, bf16[512,1024]{1,0:T(8,128)(2,1)S(1)}, u32[]{:S(2)}, u32[]{:S(2)}) %collective-permute-start.15) | collective-permute-done | bytes 1048608 | tf_op jit(solution)/shard_map/ppermute | solution.py:174
  197.0 4.5 multiply_reduce_fusion.1
  201.5 17.3 %collective-permute-done.13 = bf16[512,1024]{1,0:T(8,128)(2,1)S(1)} collective-permute-done((bf16[512,1024]{1,0:T(8,128)(2,1)S(1)}, bf16[512,1024]{1,0:T(8,128)(2,1)S(1)}, u32[]{:S(2)}, u32[]{:S(2)}) %collective-permute-start.13) | collective-permute-done | bytes 1048608 | tf_op jit(solution)/shard_map/ppermute | solution.py:174
  227.5 12.8 %collective-permute-done.16 = bf16[512,512]{1,0:T(8,128)(2,1)S(1)} collective-permute-done((bf16[512,512]{1,0:T(8,128)(2,1)S(1)}, bf16[512,512]{1,0:T(8,128)(2,1)S(1)}, u32[]{:S(2)}, u32[]{:S(2)}) %collective-permute-start.16) | collective-permute-done | bytes 524320 | tf_op jit(solution)/shard_map/ppermute | solution.py:174
  240.4 27.9 %attend_back.1 = bf16[3,1024,512]{2,1,0:T(8,128)(2,1)S(1)} custom-call(bf16[1024,1536]{1,0:T(8,128)(2,1)} %copy-done.2, bf16[1024,1536]{1,0:T(8,128)(2,1)} %copy-done.2, bf16[1024,1536]{1,0:T(8,128)(2,1)} %copy-done.2, bf16[1024,512]{1,0:T(8,128)(2,1)S(1)} %pad_maximum_fusion.6.do_ref, f32[4,2,1024]{2,1,0:T(2,128)S(1)} %get-tuple-element.16.lse_ref), custom_call_target="tpu_custom_call" | custom-call | flops 21474836480 | bytes 7340032 | tf_op jit(solution)/shard_map/attend_back/pallas_call | solution.py:131
  278.8 10.1 %convolution_convert_fusion.2 = bf16[1024,2048]{1,0:T(8,128)(2,1)} fusion(bf16[1024,2048]{1,0:T(8,128)(2,1)} %copy-done.33, f32[1024,1024]{1,0:T(8,128)} %subtract_multiply_fusion, f32[1024]{0:T(1024)S(1)} %bitcast.117, f32[1024]{0:T(1024)S(1)} %bitcast.111), kind=kOutput, calls=%fused_computation.23 | convolution fusion | flops 4300210176 | bytes 12591104 | tf_op jit(solution)/shard_map/dot_general | solution.py:33
  288.8 10.9 %convolution_convert_fusion.1 = bf16[1024,2048]{1,0:T(8,128)(2,1)} fusion(bf16[512,1024]{1,0:T(8,128)(2,1)} %collective-permute-done.14, bf16[512,1024]{1,0:T(8,128)(2,1)S(1)} %copy-done.9, f32[1024]{0:T(1024)S(1)} %bitcast.100, f32[1024,2048]{1,0:T(8,128)} %copy-done.34, f32[2048]{0:T(1024)S(1)} %slice_bitcast_fusion.5), kind=kOutput, calls=%fused_computation.22 | convolution fusion | flops 4324327424 | bytes 14692352 | tf_op jit(solution)/shard_map/dot_general | solution.py:33
  299.8 7.9 %pad_maximum_fusion = bf16[1024,4096]{1,0:T(8,128)(2,1)} fusion(bf16[1024,2048]{1,0:T(8,128)(2,1)} %convolution_convert_fusion.1, bf16[1024,2048]{1,0:T(8,128)(2,1)} %convolution_convert_fusion.2), kind=kLoop, calls=%fused_computation | loop fusion | flops 16777216 | bytes 16777216 | tf_op jit(solution)/shard_map/concatenate | solution.py:333
  310.0 5.8 %fusion.43 = bf16[512,1024]{1,0:T(8,128)(2,1)} fusion(bf16[1024,2560]{1,0:T(8,128)(2,1)} %all-gather.3.cloned.1.call-done, bf16[1024,1536]{1,0:T(8,128)(2,1)S(1)} %pad_maximum_fusion.2), kind=kOutput, calls=%fused_computation.78 | convolution fusion | flops 1611137024 | bytes 5767168 | tf_op jit(solution)/shard_map/dot_general | solution.py:29
  334.2 4.0 collective-permute-done.17
  338.2 6.9 %multiply_reduce_fusion.2 = (f32[1024]{0:T(1024)S(1)}, f32[512]{0:T(512)S(1)}, f32[512]{0:T(512)S(1)}, f32[1024]{0:T(1024)S(1)}, f32[512,1024]{1,0:T(8,128)}) fusion(f32[1024,1024]{1,0:T(8,128)} %get-tuple-element.92, f32[1024]{0:T(1024)S(1)} %bitcast.104, bf16[512,1024]{1,0:T(8,128)(2,1)} %collective-permute-done.17, ...), kind=kOutput, calls=%fused_computation.62 | convolution fusion | flops 1615328256 | bytes 9977856 | tf_op jit(solution)/shard_map/dot_general | solution.py:29
  359.9 4.2 add_convert_fusion.3
  378.4 4.7 %collective-permute-done.27 = f32[8,16,64]{2,1,0:T(8,128)S(1)} collective-permute-done((f32[8,16,64]{2,1,0:T(8,128)S(1)}, f32[8,16,64]{2,1,0:T(8,128)S(1)}, u32[]{:S(2)}, u32[]{:S(2)}) %collective-permute-start.27) | collective-permute-done | bytes 32800 | tf_op jit(solution)/shard_map/ppermute | solution.py:179
  387.5 70.8 %reduce-scatter.5.cloned.1.call-done = bf16[64,4096]{1,0:T(8,128)(2,1)} async-done(((bf16[1024,4096]{1,0:T(8,128)(2,1)}), bf16[64,4096]{1,0:T(8,128)(2,1)}) %reduce-scatter.5.cloned.1.call-update) | async-done | bytes 524304 | tf_op jit(solution)/shard_map/reduce_scatter | solution.py:336
  (270 shorter events, 147.3 us)
Async XLA Ops:
  7.2 65.5 %all-gather.3.cloned.1.call-start = ((), (), s32[]{:S(2)}) async-start(), calls=%async_computation.2 | async-start | bytes 5570560 | tf_op jit(solution)/shard_map/all_gather | solution.py:250
  7.2 5.5 %collective-permute-start.11 = (bf16[64,512]{1,0:T(8,128)(2,1)}, bf16[64,512]{1,0:T(8,128)(2,1)S(1)}, u32[]{:S(2)}, u32[]{:S(2)}) collective-permute-start(bf16[64,512]{1,0:T(8,128)(2,1)} %bitcast.95), channel_id=1, source_target_pairs={{0,1},{1,0},{2,3},{3,2},{4,5},{5,4},{6,7},{7,6},{8,9},{9,8},{10,11... | collective-permute-start | bytes 196616 | tf_op jit(solution)/shard_map/ppermute | solution.py:174
  14.3 134.7 %all-gather.5.cloned.1.call-start = ((), (), s32[]{:S(2)}) async-start(), calls=%async_computation.3 | async-start | bytes 8912896 | tf_op jit(solution)/shard_map/all_gather | solution.py:251
  16.2 367.9 %reduce-scatter.3.cloned.1.call-start = ((), (), s32[]{:S(2)}) async-start(), calls=%async_computation.4 | async-start | bytes 4456448 | tf_op jit(solution)/shard_map/reduce_scatter | solution.py:354
  34.6 5.8 %collective-permute-start.5 = (bf16[8,1920]{1,0:T(8,128)(2,1)S(1)}, bf16[8,1920]{1,0:T(8,128)(2,1)S(1)}, u32[]{:S(2)}, u32[]{:S(2)}) collective-permute-start(bf16[8,1920]{1,0:T(8,128)(2,1)S(1)} %pad_maximum_fusion.12), channel_id=1, source_target_pairs={{0,16},{2,18},{4,20},{6,22},{8,24},{10,26},{12,28},{14,30},{16,0},... | collective-permute-start | bytes 92168 | tf_op jit(solution)/shard_map/ppermute | solution.py:179
  37.9 29.0 %collective-permute-start = (bf16[512,1024]{1,0:T(8,128)(2,1)}, bf16[512,1024]{1,0:T(8,128)(2,1)S(1)}, u32[]{:S(2)}, u32[]{:S(2)}) collective-permute-start(bf16[512,1024]{1,0:T(8,128)(2,1)} %param.13), channel_id=1, source_target_pairs={{0,1},{1,0},{2,3},{3,2},{4,5},{5,4},{6,7},{7,6},{8,9},{9,8},{10,11... | collective-permute-start | bytes 3145736 | tf_op jit(solution)/shard_map/ppermute | solution.py:174
  40.8 7.0 %collective-permute-start.6 = (f32[8,3072]{1,0:T(8,128)S(1)}, f32[8,3072]{1,0:T(8,128)S(1)}, u32[]{:S(2)}, u32[]{:S(2)}) collective-permute-start(f32[8,3072]{1,0:T(8,128)S(1)} %slice.226), channel_id=1, source_target_pairs={{0,16},{2,18},{4,20},{6,22},{8,24},{10,26},{12,28},{14,30},{16,0},... | collective-permute-start | bytes 294920 | tf_op jit(solution)/shard_map/ppermute | solution.py:179
  47.9 8.5 %collective-permute-start.7 = (f32[4,3072]{1,0:T(4,128)S(1)}, f32[4,3072]{1,0:T(4,128)S(1)}, u32[]{:S(2)}, u32[]{:S(2)}) collective-permute-start(f32[4,3072]{1,0:T(4,128)S(1)} %slice.228), channel_id=1, source_target_pairs={{0,8},{2,10},{4,12},{6,14},{8,0},{10,2},{12,4},{14,6},{16,24},{18,... | collective-permute-start | bytes 147464 | tf_op jit(solution)/shard_map/ppermute | solution.py:179
  56.4 4.4 collective-permute-start.8
  62.1 4.7 %collective-permute-start.10 = (f32[6,512]{1,0:T(8,128)S(1)}, f32[6,512]{1,0:T(8,128)S(1)}, u32[]{:S(2)}, u32[]{:S(2)}) collective-permute-start(f32[6,512]{1,0:T(8,128)S(1)} %add.230), channel_id=1, source_target_pairs={{0,1},{1,0},{2,3},{3,2},{4,5},{5,4},{6,7},{7,6},{8,9},{9,8},{10,11... | collective-permute-start | bytes 36872 | tf_op jit(solution)/shard_map/ppermute | solution.py:174
  102.6 26.2 %collective-permute-start.12 = (bf16[1024,512]{1,0:T(8,128)(2,1)S(1)}, bf16[1024,512]{1,0:T(8,128)(2,1)}, u32[]{:S(2)}, u32[]{:S(2)}) collective-permute-start(bf16[1024,512]{1,0:T(8,128)(2,1)S(1)} %get-tuple-element.15), channel_id=1, source_target_pairs={{0,1},{1,0},{2,3},{3,2},{4,5},{5,4},{6,7},{7,6},{8,9},{9,8},{10,11... | collective-permute-start | bytes 3145736 | tf_op jit(solution)/shard_map/ppermute | solution.py:174
  104.1 53.0 %collective-permute-start.14 = (bf16[512,1024]{1,0:T(8,128)(2,1)S(1)}, bf16[512,1024]{1,0:T(8,128)(2,1)}, u32[]{:S(2)}, u32[]{:S(2)}) collective-permute-start(bf16[512,1024]{1,0:T(8,128)(2,1)S(1)} %copy-done.8), channel_id=1, source_target_pairs={{0,1},{1,0},{2,3},{3,2},{4,5},{5,4},{6,7},{7,6},{8,9},{9,8},{10,11... | collective-permute-start | bytes 3145736 | tf_op jit(solution)/shard_map/ppermute | solution.py:174
  170.9 26.1 %collective-permute-start.15 = (bf16[512,1024]{1,0:T(8,128)(2,1)S(1)}, bf16[512,1024]{1,0:T(8,128)(2,1)S(1)}, u32[]{:S(2)}, u32[]{:S(2)}) collective-permute-start(bf16[512,1024]{1,0:T(8,128)(2,1)S(1)} %fusion.48), channel_id=1, source_target_pairs={{0,1},{1,0},{2,3},{3,2},{4,5},{5,4},{6,7},{7,6},{8,9},{9,8},{10,11... | collective-permute-start | bytes 3145736 | tf_op jit(solution)/shard_map/ppermute | solution.py:174
  180.6 38.2 %collective-permute-start.13 = (bf16[512,1024]{1,0:T(8,128)(2,1)S(1)}, bf16[512,1024]{1,0:T(8,128)(2,1)S(1)}, u32[]{:S(2)}, u32[]{:S(2)}) collective-permute-start(bf16[512,1024]{1,0:T(8,128)(2,1)S(1)} %slice.353), channel_id=1, source_target_pairs={{0,1},{1,0},{2,3},{3,2},{4,5},{5,4},{6,7},{7,6},{8,9},{9,8},{10,11... | collective-permute-start | bytes 3145736 | tf_op jit(solution)/shard_map/ppermute | solution.py:174
  225.4 14.9 %collective-permute-start.16 = (bf16[512,512]{1,0:T(8,128)(2,1)S(1)}, bf16[512,512]{1,0:T(8,128)(2,1)S(1)}, u32[]{:S(2)}, u32[]{:S(2)}) collective-permute-start(bf16[512,512]{1,0:T(8,128)(2,1)S(1)} %get-tuple-element.96), channel_id=1, source_target_pairs={{0,1},{1,0},{2,3},{3,2},{4,5},{5,4},{6,7},{7,6},{8,9},{9,8},{10,11... | collective-permute-start | bytes 1572872 | tf_op jit(solution)/shard_map/ppermute | solution.py:174
  226.9 47.8 %collective-permute-start.28 = (bf16[512,1024]{1,0:T(8,128)(2,1)S(1)}, bf16[512,1024]{1,0:T(8,128)(2,1)S(1)}, u32[]{:S(2)}, u32[]{:S(2)}) collective-permute-start(bf16[512,1024]{1,0:T(8,128)(2,1)S(1)} %multiply_convert_fusion.3), channel_id=1, source_target_pairs={{0,1},{1,0},{2,3},{3,2},{4,5},{5,4},{6,7},{7,6},{8,9},{9,8},{10,11... | collective-permute-start | bytes 3145736 | tf_op jit(solution)/shard_map/ppermute | solution.py:174
  278.7 179.6 %reduce-scatter.5.cloned.1.call-start = ((), (), s32[]{:S(2)}) async-start(), calls=%async_computation.5 | async-start | bytes 8912896 | tf_op jit(solution)/shard_map/reduce_scatter | solution.py:336
  315.8 22.4 %collective-permute-start.17 = (bf16[512,1024]{1,0:T(8,128)(2,1)}, bf16[512,1024]{1,0:T(8,128)(2,1)}, u32[]{:S(2)}, u32[]{:S(2)}) collective-permute-start(bf16[512,1024]{1,0:T(8,128)(2,1)} %fusion.43), channel_id=1, source_target_pairs={{0,1},{1,0},{2,3},{3,2},{4,5},{5,4},{6,7},{7,6},{8,9},{9,8},{10,11... | collective-permute-start | bytes 3145736 | tf_op jit(solution)/shard_map/ppermute | solution.py:174
  324.8 4.7 %collective-permute-start.31 = (f32[4096]{0:T(1024)S(1)}, f32[4096]{0:T(1024)S(1)}, u32[]{:S(2)}, u32[]{:S(2)}) collective-permute-start(f32[4096]{0:T(1024)S(1)} %add.268), channel_id=1, source_target_pairs={{0,8},{2,10},{4,12},{6,14},{8,0},{10,2},{12,4},{14,6},{16,24},{18,... | collective-permute-start | bytes 49160 | tf_op jit(solution)/shard_map/ppermute | solution.py:179
  329.5 4.6 collective-permute-start.32
  354.1 3.9 collective-permute-start.21
  358.0 6.0 %collective-permute-start.22 = (bf16[8,3072]{1,0:T(8,128)(2,1)S(1)}, bf16[8,3072]{1,0:T(8,128)(2,1)S(1)}, u32[]{:S(2)}, u32[]{:S(2)}) collective-permute-start(bf16[8,3072]{1,0:T(8,128)(2,1)S(1)} %pad_maximum_fusion.10), channel_id=1, source_target_pairs={{0,16},{2,18},{4,20},{6,22},{8,24},{10,26},{12,28},{14,30},{16,0},... | collective-permute-start | bytes 147464 | tf_op jit(solution)/shard_map/ppermute | solution.py:179
  373.4 3.9 collective-permute-start.26
  377.3 5.8 %collective-permute-start.27 = (f32[8,16,64]{2,1,0:T(8,128)S(1)}, f32[8,16,64]{2,1,0:T(8,128)S(1)}, u32[]{:S(2)}, u32[]{:S(2)}) collective-permute-start(f32[8,16,64]{2,1,0:T(8,128)S(1)} %pad_maximum_fusion.9), channel_id=1, source_target_pairs={{0,16},{2,18},{4,20},{6,22},{8,24},{10,26},{12,28},{14,30},{16,0},... | collective-permute-start | bytes 98312 | tf_op jit(solution)/shard_map/ppermute | solution.py:179
  (50 other events, 904.9 us)
Sparse Core Ops, SparseCore 0:
  14.4 58.2 all-gather.2
  75.4 73.5 all-gather.4
  278.8 71.2 reduce-scatter.2
  354.6 103.6 reduce-scatter.4

commit v2 on v1

v2 whole, which is shorter than its diff:
```python
import math
from functools import partial

import jax
import jax.numpy as jnp
from jax import lax
from jax.experimental import pallas as pl
from jax.experimental.pallas import tpu as pltpu
from jax.sharding import PartitionSpec as P

HEAD_DIM = 64
LEN = 1024
PAIR = 2 * HEAD_DIM

norm_eps = 1e-06
highest = lax.Precision.HIGHEST
f32 = jnp.float32
bf16 = jnp.bfloat16

score_scale = HEAD_DIM ** (-0.5)
log2_scale = score_scale * math.log2(math.e)


MIB = 1024 * 1024


def dot_nn(a, b):
    return lax.dot_general(a, b, (((1,), (0,)), ((), ())), preferred_element_type=f32)


def dot_nt(a, b):
    return lax.dot_general(a, b, (((1,), (1,)), ((), ())), preferred_element_type=f32)


def dot_tn(a, b):
    return lax.dot_general(a, b, (((0,), (0,)), ((), ())), preferred_element_type=f32)


def head_masks():
    lane = lax.broadcasted_iota(jnp.int32, (1, PAIR), 1)
    return [(lane < HEAD_DIM), (lane >= HEAD_DIM)]


def attend_kernel(step_rows, q_ref, k_ref, v_ref, o_ref, lse_ref):
    rows = q_ref.shape[0]
    masks = head_masks()
    keys = k_ref[...]
    values_t = v_ref[...].astype(f32).T.astype(bf16)
    sub = lax.broadcasted_iota(jnp.int32, (PAIR, 1), 0)
    for start in range(0, rows, step_rows):
        queries = q_ref[start : start + step_rows, :]
        out_t = []
        for head in range(2):
            q_head = jnp.where(masks[head], queries, jnp.zeros_like(queries))
            scores = dot_nt(keys, q_head) * log2_scale
            peak = jnp.max(scores, 0, keepdims=True)
            terms = jnp.exp2(scores - peak)
            total = jnp.sum(terms, 0, keepdims=True)
            out_t.append(dot_nn(values_t, terms.astype(bf16)) * (1.0 / total))
            lse_ref[0, head : head + 1, start : start + step_rows] = peak + jnp.log2(total)
        joined = jnp.where(sub < HEAD_DIM, out_t[0], out_t[1])
        o_ref[start : start + step_rows, :] = joined.T.astype(bf16)


def attend(qkv, local_width):
    rows = qkv.shape[0]
    pairs = local_width // PAIR
    heads = local_width // HEAD_DIM
    spec = [
        pl.BlockSpec((rows, PAIR), partial(lambda part, i: (0, part * pairs + i), part))
        for part in range(3)
    ]
    return pl.pallas_call(
        partial(attend_kernel, 256),
        grid=(pairs,),
        in_specs=spec,
        out_specs=[
            pl.BlockSpec((rows, PAIR), lambda i: (0, i)),
            pl.BlockSpec((1, 2, rows), lambda i: (i, 0, 0)),
        ],
        out_shape=[
            jax.ShapeDtypeStruct((rows, local_width), bf16),
            jax.ShapeDtypeStruct((pairs, 2, rows), f32),
        ],
        compiler_params=pltpu.CompilerParams(vmem_limit_bytes=28 * MIB),
        cost_estimate=pl.CostEstimate(
            flops=4 * heads * rows * rows * 256,
            bytes_accessed=rows * local_width * 8,
            transcendentals=heads * rows * rows,
        ),
        name="attend",
    )(qkv, qkv, qkv)


def attend_back_kernel(step_rows, q_ref, k_ref, v_ref, do_ref, lse_ref, dqkv_ref):
    rows = q_ref.shape[0]
    masks = head_masks()
    keys = k_ref[...]
    values = v_ref[...]
    sub = lax.broadcasted_iota(jnp.int32, (PAIR, 1), 0)
    keys_t = keys.astype(f32).T.astype(bf16)
    d_keys = jnp.zeros((rows, PAIR), f32)
    d_values = jnp.zeros((rows, PAIR), f32)
    for start in range(0, rows, step_rows):
        queries = q_ref[start : start + step_rows, :]
        d_out = do_ref[start : start + step_rows, :]
        dq_t = []
        for head in range(2):
            q_head = jnp.where(masks[head], queries, jnp.zeros_like(queries))
            do_head = jnp.where(masks[head], d_out, jnp.zeros_like(d_out))
            lse = lse_ref[0, head : head + 1, start : start + step_rows]
            probs = jnp.exp2(dot_nt(keys, q_head) * log2_scale - lse)
            d_probs = dot_nt(values, do_head)
            weighted = probs * d_probs
            row_dot = jnp.sum(weighted, 0, keepdims=True)
            d_scores = (weighted - probs * row_dot).astype(bf16)
            d_values = d_values + dot_nn(probs.astype(bf16), do_head)
            d_keys = d_keys + dot_nn(d_scores, q_head)
            dq_t.append(dot_nn(keys_t, d_scores))
        joined = jnp.where(sub < HEAD_DIM, dq_t[0], dq_t[1])
        dqkv_ref[0, start : start + step_rows, :] = (joined.T * score_scale).astype(bf16)
    dqkv_ref[1] = (d_keys * score_scale).astype(bf16)
    dqkv_ref[2] = d_values.astype(bf16)


def attend_back(qkv, grad_heads, lse, local_width):
    rows = qkv.shape[0]
    pairs = local_width // PAIR
    heads = local_width // HEAD_DIM
    spec = [
        pl.BlockSpec((rows, PAIR), partial(lambda part, i: (0, part * pairs + i), part))
        for part in range(3)
    ]
    return pl.pallas_call(
        partial(attend_back_kernel, 256),
        grid=(pairs,),
        in_specs=spec
        + [
            pl.BlockSpec((rows, PAIR), lambda i: (0, i)),
            pl.BlockSpec((1, 2, rows), lambda i: (i, 0, 0)),
        ],
        out_specs=pl.BlockSpec((3, rows, PAIR), lambda i: (0, 0, i)),
        out_shape=jax.ShapeDtypeStruct((3, rows, local_width), bf16),
        compiler_params=pltpu.CompilerParams(vmem_limit_bytes=28 * MIB),
        cost_estimate=pl.CostEstimate(
            flops=10 * heads * rows * rows * 256,
            bytes_accessed=rows * local_width * 14,
            transcendentals=heads * rows * rows,
        ),
        name="attend_back",
    )(qkv, qkv, qkv, grad_heads, lse)


def normalize(values):
    mean = jnp.mean(values, -1, keepdims=True)
    centred = values - mean
    rstd = lax.rsqrt(jnp.mean(centred * centred, -1, keepdims=True) + norm_eps)
    return (centred * rstd, mean, rstd)


def norm_back(grad_n, normed, rstd):
    first = jnp.mean(grad_n, -1, keepdims=True)
    second = jnp.mean(grad_n * normed, -1, keepdims=True)
    return rstd * (grad_n - first - normed * second)


def gelu_both(v):
    c = math.sqrt(2.0 / math.pi)
    sq = v * v
    half = 0.5 + 0.5 * jnp.tanh(v * (c + c * 0.044715 * sq))
    act = v * half
    slope = half + act * (1.0 - half) * (2 * c + 6 * c * 0.044715 * sq)
    return act, slope


def full_spec(shape):
    return pl.BlockSpec(shape, lambda *_: (0,) * len(shape))


def mlp_kernel(
    own_rows, step_rows, h_ref, dm_ref, w1_ref, w2_ref, b1_ref,
    act_ref, dpre_ref, db_ref, own_ref, rest_ref, acc_ref,
):
    j = pl.program_id(0)

    @pl.when(j == 0)
    def _():
        acc_ref[...] = jnp.zeros_like(acc_ref)

    rows = h_ref.shape[0]
    w1, w2, b1 = w1_ref[...], w2_ref[...], b1_ref[...]
    total = jnp.zeros((1, w1.shape[1]), f32)
    for start in range(0, rows, step_rows):
        part = slice(start, start + step_rows)
        pre = dot_nn(h_ref[part, :], w1) + b1
        d_act = dot_nn(dm_ref[part, :], w2)
        act, slope = gelu_both(pre)
        d_pre = d_act * slope
        d_low = d_pre.astype(bf16)
        act_ref[part, :] = act.astype(bf16)
        dpre_ref[part, :] = d_low
        total = total + jnp.sum(d_pre, 0, keepdims=True)
        acc_ref[part, :] += dot_nt(d_low, w1)
    db_ref[...] = total

    @pl.when(j == pl.num_programs(0) - 1)
    def _():
        own_ref[...] = acc_ref[:own_rows, :]
        rest_ref[...] = acc_ref[own_rows:, :].astype(bf16)


def mlp_both(hidden_two, grad_m, mlp_w, bias, own_rows):
    rows, width = hidden_two.shape
    hidden = mlp_w.shape[1] // 2
    block = min(512, hidden)
    steps = hidden // block
    return pl.pallas_call(
        partial(mlp_kernel, own_rows, 256),
        grid=(steps,),
        in_specs=[
            full_spec((rows, width)),
            full_spec((rows, width)),
            pl.BlockSpec((width, block), lambda j: (0, j)),
            pl.BlockSpec((width, block), lambda j: (0, steps + j)),
            pl.BlockSpec((1, block), lambda j: (0, j)),
        ],
        out_specs=[
            pl.BlockSpec((rows, block), lambda j: (0, j)),
            pl.BlockSpec((rows, block), lambda j: (0, j)),
            pl.BlockSpec((1, block), lambda j: (0, j)),
            full_spec((own_rows, width)),
            full_spec((rows - own_rows, width)),
        ],
        out_shape=[
            jax.ShapeDtypeStruct((rows, hidden), bf16),
            jax.ShapeDtypeStruct((rows, hidden), bf16),
            jax.ShapeDtypeStruct((1, hidden), f32),
            jax.ShapeDtypeStruct((own_rows, width), f32),
            jax.ShapeDtypeStruct((rows - own_rows, width), bf16),
        ],
        scratch_shapes=[pltpu.VMEM((rows, width), f32)],
        compiler_params=pltpu.CompilerParams(vmem_limit_bytes=48 * MIB),
        cost_estimate=pl.CostEstimate(
            flops=6 * rows * width * hidden,
            bytes_accessed=4 * rows * hidden + 6 * width * hidden + 8 * rows * width,
            transcendentals=rows * hidden,
        ),
        name="mlp_both",
    )(hidden_two, grad_m, mlp_w, mlp_w, bias)


def transpose_low(value):
    return value.astype(f32).T.astype(bf16)


def mlp_grads_kernel(own_rows, half, h_ref, dm_ref, dpre_ref, act_ref, w2_ref, cot_ref, grad_ref, own_ref, rest_ref, sum_ref, h_t, dm_t, acc_ref):
    j = pl.program_id(0)

    @pl.when(j == 0)
    def _():
        h_t[...] = transpose_low(h_ref[...])
        dm_t[...] = transpose_low(dm_ref[...])
        acc_ref[...] = jnp.zeros_like(acc_ref)

    @pl.when(j < half)
    def _():
        grad_ref[...] = dot_nn(h_t[...], dpre_ref[...]).astype(bf16)

    @pl.when(j >= half)
    def _():
        grad_ref[...] = dot_nn(dm_t[...], act_ref[...]).astype(bf16)
        acc_ref[...] += dot_nt(act_ref[...], w2_ref[...])

    @pl.when(j == 2 * half - 1)
    def _():
        own_ref[...] = acc_ref[:own_rows, :]
        rest_ref[...] = acc_ref[own_rows:, :].astype(bf16)
        sum_ref[...] = jnp.sum(acc_ref[...] * cot_ref[...].astype(f32), 0, keepdims=True)


def mlp_weight_grads(hidden_two, grad_m, grad_pre, activ, mlp_w, cot_all, own_rows):
    rows, width = hidden_two.shape
    hidden = mlp_w.shape[1] // 2
    block = min(512, hidden)
    half = hidden // block
    return pl.pallas_call(
        partial(mlp_grads_kernel, own_rows, half),
        grid=(2 * half,),
        in_specs=[
            full_spec((rows, width)),
            full_spec((rows, width)),
            pl.BlockSpec((rows, block), lambda j: (0, jnp.minimum(j, half - 1))),
            pl.BlockSpec((rows, block), lambda j: (0, jnp.maximum(j - half, 0))),
            pl.BlockSpec((width, block), lambda j: (0, half + jnp.maximum(j - half, 0))),
            full_spec((rows, width)),
        ],
        out_specs=[
            pl.BlockSpec((width, block), lambda j: (0, j)),
            full_spec((own_rows, width)),
            full_spec((rows - own_rows, width)),
            full_spec((1, width)),
        ],
        out_shape=[
            jax.ShapeDtypeStruct((width, 2 * hidden), bf16),
            jax.ShapeDtypeStruct((own_rows, width), f32),
            jax.ShapeDtypeStruct((rows - own_rows, width), bf16),
            jax.ShapeDtypeStruct((1, width), f32),
        ],
        scratch_shapes=[
            pltpu.VMEM((width, rows), bf16),
            pltpu.VMEM((width, rows), bf16),
            pltpu.VMEM((rows, width), f32),
        ],
        compiler_params=pltpu.CompilerParams(vmem_limit_bytes=48 * MIB),
        cost_estimate=pl.CostEstimate(
            flops=6 * rows * width * hidden,
            bytes_accessed=4 * rows * hidden + 6 * width * hidden + 8 * rows * width,
            transcendentals=0,
        ),
        name="mlp_weight_grads",
    )(hidden_two, grad_m, grad_pre, activ, mlp_w, cot_all)


def middle_kernel(own_steps, pieces, *refs):
    heads = [ref[...] for ref in refs[:pieces]]
    w_ref, x_ref, cot_ref, mod_ref = refs[pieces : pieces + 4]
    h_ref, dm_ref, sum_ref, a_ref, x1_ref, mean_ref, rstd_ref = refs[pieces + 4 :]
    i = pl.program_id(0)
    branch = dot_nt(jnp.concatenate(heads, 1), w_ref[...]) + mod_ref[6:7, :]
    middle = x_ref[...].astype(f32) + mod_ref[2:3, :] * branch
    normed, mean, rstd = normalize(middle)
    h_ref[...] = (normed * (1.0 + mod_ref[4:5, :]) + mod_ref[3:4, :]).astype(bf16)
    low = (mod_ref[5:6, :] * cot_ref[...].astype(f32)).astype(bf16)
    dm_ref[...] = low
    total = jnp.sum(low.astype(f32), 0, keepdims=True)

    @pl.when(i == 0)
    def _():
        sum_ref[...] = total

    @pl.when(i > 0)
    def _():
        sum_ref[...] += total

    @pl.when(i < own_steps)
    def _():
        a_ref[...] = branch
        x1_ref[...] = middle
        mean_ref[...] = mean
        rstd_ref[...] = rstd


def middle_part(heads, weight, x_all, cot_all, modul, own_rows):
    rows, width = x_all.shape
    block = min(256, own_rows)
    steps, own_steps = rows // block, own_rows // block
    specs, arrays = [], []
    for s, parts in enumerate(heads):
        for part in parts:
            specs.append(
                pl.BlockSpec(
                    (block, part.shape[1]),
                    partial(lambda back, i: (lax.rem(i - back + steps, steps), 0), s * own_steps),
                )
            )
            arrays.append(part)
    row_spec = pl.BlockSpec((block, width), lambda i: (i, 0))
    own_spec = pl.BlockSpec((block, width), lambda i: (jnp.minimum(i, own_steps - 1), 0))
    one_spec = pl.BlockSpec((block, 1), lambda i: (jnp.minimum(i, own_steps - 1), 0))
    return pl.pallas_call(
        partial(middle_kernel, own_steps, len(arrays)),
        grid=(steps,),
        in_specs=specs
        + [full_spec((width, width)), row_spec, row_spec, full_spec(modul.shape)],
        out_specs=[row_spec, row_spec, full_spec((1, width)), own_spec, own_spec, one_spec, one_spec],
        out_shape=[
            jax.ShapeDtypeStruct((rows, width), bf16),
            jax.ShapeDtypeStruct((rows, width), bf16),
            jax.ShapeDtypeStruct((1, width), f32),
            jax.ShapeDtypeStruct((own_rows, width), f32),
            jax.ShapeDtypeStruct((own_rows, width), f32),
            jax.ShapeDtypeStruct((own_rows, 1), f32),
            jax.ShapeDtypeStruct((own_rows, 1), f32),
        ],
        compiler_params=pltpu.CompilerParams(vmem_limit_bytes=40 * MIB),
        cost_estimate=pl.CostEstimate(
            flops=2 * rows * width * width,
            bytes_accessed=12 * rows * width + 8 * own_rows * width,
            transcendentals=rows,
        ),
        name="middle_part",
    )(*arrays, weight, x_all, cot_all, modul)


def middle_back_kernel(others, pieces, own_ref, *refs):
    arrived = refs[:others]
    cot_ref, x1_ref, a_ref, mean_ref, rstd_ref, mod_ref, w_ref = refs[others : others + 7]
    mid_ref, da_ref, sums_ref = refs[others + 7 : others + 10]
    head_refs = refs[others + 10 :]
    grad_h = own_ref[...]
    for ref in arrived:
        grad_h = grad_h + ref[...].astype(f32)
    normed = (x1_ref[...] - mean_ref[...]) * rstd_ref[...]
    grad_mid = cot_ref[...].astype(f32) + norm_back(
        grad_h * (1.0 + mod_ref[4:5, :]), normed, rstd_ref[...]
    )
    grad_a = (mod_ref[2:3, :] * grad_mid).astype(bf16)
    mid_ref[...] = grad_mid
    da_ref[...] = grad_a
    sums = jnp.concatenate(
        [
            jnp.sum(grad_mid * a_ref[...], 0, keepdims=True),
            jnp.sum(grad_h, 0, keepdims=True),
            jnp.sum(grad_h * normed, 0, keepdims=True),
        ]
    )
    i = pl.program_id(0)

    @pl.when(i == 0)
    def _():
        sums_ref[...] = sums

    @pl.when(i > 0)
    def _():
        sums_ref[...] += sums

    grad_heads = dot_nn(grad_a, w_ref[...]).astype(bf16)
    columns = head_refs[0].shape[1]
    for p in range(pieces):
        head_refs[p][...] = grad_heads[:, p * columns : (p + 1) * columns]


def middle_back(own, arrived, cot, x1, branch, mean, rstd, modul, weight, columns):
    rows, width = own.shape
    block = min(256, rows)
    pieces = width // columns
    row_spec = pl.BlockSpec((block, width), lambda i: (i, 0))
    one_spec = pl.BlockSpec((block, 1), lambda i: (i, 0))
    return pl.pallas_call(
        partial(middle_back_kernel, len(arrived), pieces),
        grid=(rows // block,),
        in_specs=[row_spec] * (len(arrived) + 4)
        + [one_spec, one_spec, full_spec(modul.shape), full_spec((width, width))],
        out_specs=[row_spec, row_spec, full_spec((3, width))]
        + [pl.BlockSpec((block, columns), lambda i: (i, 0))] * pieces,
        out_shape=[
            jax.ShapeDtypeStruct((rows, width), f32),
            jax.ShapeDtypeStruct((rows, width), bf16),
            jax.ShapeDtypeStruct((3, width), f32),
        ]
        + [jax.ShapeDtypeStruct((rows, columns), bf16)] * pieces,
        compiler_params=pltpu.CompilerParams(vmem_limit_bytes=40 * MIB),
        cost_estimate=pl.CostEstimate(
            flops=2 * rows * width * width, bytes_accessed=28 * rows * width, transcendentals=0
        ),
        name="middle_back",
    )(own, *arrived, cot, x1, branch, mean, rstd, modul, weight)


def col_grads_kernel(count, depth, arrays, core_ref, left_ref, *refs):
    keep_ref, send_ref = refs[arrays:]
    left_t = transpose_low(left_ref[...])
    core = core_ref[0]
    at = 0
    for ref in refs[:arrays]:
        for p in range(ref.shape[0]):
            columns = slice(at, at + ref.shape[2])
            result = dot_nn(left_t, ref[p])
            for i in range(count // 2):
                low = result[2 * i * depth : (2 * i + 1) * depth]
                high = result[(2 * i + 1) * depth : (2 * i + 2) * depth]
                rows = slice(i * depth, (i + 1) * depth)
                keep_ref[rows, columns] = jnp.where(core == 0, low, high).astype(bf16)
                send_ref[rows, columns] = jnp.where(core == 0, high, low).astype(bf16)
            at += ref.shape[2]


def col_grads(left, rights, core, depth):
    rows, width = left.shape
    columns = sum(right.shape[0] * right.shape[2] for right in rights)
    out = jax.ShapeDtypeStruct((width // 2, columns), bf16)
    vmem = pl.BlockSpec(memory_space=pltpu.VMEM)
    return pl.pallas_call(
        partial(col_grads_kernel, width // depth, depth, len(rights)),
        in_specs=[pl.BlockSpec(memory_space=pltpu.SMEM)] + [vmem] * (1 + len(rights)),
        out_specs=[vmem, vmem],
        out_shape=[out, out],
        compiler_params=pltpu.CompilerParams(vmem_limit_bytes=40 * MIB),
        cost_estimate=pl.CostEstimate(
            flops=2 * rows * width * columns,
            bytes_accessed=2 * rows * width + 4 * rows * columns,
            transcendentals=0,
        ),
        name="col_grads",
    )(core, left, *rights)


def hidden_back_kernel(own_rows, groups, *refs):
    x_ref = refs[0]
    grads = refs[1 : 1 + groups]
    weights = refs[1 + groups : 1 + 2 * groups]
    own_ref, rest_ref, sums_ref, acc_ref = refs[1 + 2 * groups :]
    j = pl.program_id(0)
    part = dot_nt(grads[0][0], weights[0][...])
    for g in range(1, groups):
        part = part + dot_nt(grads[g][0], weights[g][...])

    @pl.when(j == 0)
    def _():
        acc_ref[...] = part

    @pl.when(j > 0)
    def _():
        acc_ref[...] += part

    @pl.when(j == pl.num_programs(0) - 1)
    def _():
        total = acc_ref[...]
        normed, _, _ = normalize(x_ref[...].astype(f32))
        own_ref[...] = total[:own_rows]
        rest_ref[...] = total[own_rows:].astype(bf16)
        sums_ref[0:1, :] = jnp.sum(total, 0, keepdims=True)
        sums_ref[1:2, :] = jnp.sum(total * normed, 0, keepdims=True)


def hidden_back(x_all, grads, weight, first, own_rows):
    rows, width = x_all.shape
    groups = len(grads)
    columns = grads[0].shape[2]
    return pl.pallas_call(
        partial(hidden_back_kernel, own_rows, groups),
        grid=(3,),
        in_specs=[full_spec((rows, width))]
        + [pl.BlockSpec((1, rows, columns), lambda j: (j, 0, 0))] * groups
        + [
            pl.BlockSpec((width, columns), partial(lambda at, j: (0, at + j), first // columns + 3 * g))
            for g in range(groups)
        ],
        out_specs=[
            full_spec((own_rows, width)),
            full_spec((rows - own_rows, width)),
            full_spec((2, width)),
        ],
        out_shape=[
            jax.ShapeDtypeStruct((own_rows, width), f32),
            jax.ShapeDtypeStruct((rows - own_rows, width), bf16),
            jax.ShapeDtypeStruct((2, width), f32),
        ],
        scratch_shapes=[pltpu.VMEM((rows, width), f32)],
        compiler_params=pltpu.CompilerParams(vmem_limit_bytes=40 * MIB),
        cost_estimate=pl.CostEstimate(
            flops=6 * rows * width * columns * groups,
            bytes_accessed=4 * rows * width + 12 * rows * columns * groups,
            transcendentals=0,
        ),
        name="hidden_back",
    )(x_all, *grads, *([weight] * groups))


def shift(x, axis, step):
    size = lax.axis_size(axis)
    return lax.ppermute(x, axis, [(i, (i + step) % size) for i in range(size)])


def xor_step(x, axis, bit):
    size = lax.axis_size(axis)
    return lax.ppermute(x, axis, [(i, i ^ bit) for i in range(size)])


def bits_of(side_last):
    size = lax.axis_size("dp")
    bits = [1 << k for k in range(size.bit_length() - 1)]
    return bits[:1] + bits[2:] + bits[1:2] if side_last else bits


def xor_of(side_last):
    bits = bits_of(side_last)
    place = jnp.arange(1 << len(bits), dtype=jnp.int32)
    return sum(((place >> k) & 1) * bit for k, bit in enumerate(bits))


def xor_gather(x, side_last):
    out = x[None]
    for bit in bits_of(side_last):
        out = jnp.concatenate([out, xor_step(out, "dp", bit)], 0)
    return out


def xor_scatter_sum(x, side_last):
    half = x.shape[0] // 2
    for bit in reversed(bits_of(side_last)):
        x = x[:half] + xor_step(x[half:], "dp", bit)
        half //= 2
    return x[0]


def xor_sum(x, side_last):
    for bit in bits_of(side_last):
        x = x + xor_step(x, "dp", bit)
    return x


def sort_xor(x, side_last):
    size = lax.axis_size("dp")
    me = lax.axis_index("dp")
    order = jnp.arange(size, dtype=jnp.int32)
    pick = ((order[:, None] ^ me) == xor_of(side_last)[None, :]).astype(f32)
    flat = x.reshape(size, -1).astype(f32)
    return jnp.dot(pick, flat, precision=highest).reshape(x.shape)


def rel_gather(x, axis):
    return [x] + [shift(x, axis, s) for s in range(1, lax.axis_size(axis))]


def sort_rel(parts, axis):
    size = lax.axis_size(axis)
    me = lax.axis_index(axis)
    out = []
    for target in range(size):
        value = jnp.zeros_like(parts[0])
        for s in range(size):
            value = jnp.where(lax.rem(me - s + size, size) == target, parts[s], value)
        out.append(value)
    return out


def together(run, work, *args):
    shapes = jax.eval_shape(work, *args)
    empty = lambda *_: jax.tree.map(lambda v: jnp.zeros(v.shape, v.dtype), shapes)
    return lax.cond(run, work, empty, *args)


def dp_place():
    size, me = lax.axis_size("dp"), lax.axis_index("dp")
    return size // 4, me // 4, lax.rem(me // 2, 2), lax.rem(me, 2)


def after(value, *others):
    return lax.optimization_barrier((value,) + others)[0]


def far_shift(x, step):
    size = lax.axis_size("dp")
    return lax.ppermute(x, "dp", [(i, (i + 4 * step) % size) for i in range(size)])


def add_low(keep, arrived):
    return (keep.astype(f32) + arrived.astype(f32)).astype(bf16)


def side_split(total, depth):
    far_size, _, side, _ = dp_place()
    total = total.reshape(far_size, 2, depth, total.shape[1])
    keep = lax.dynamic_index_in_dim(total, side, 1, keepdims=False)
    return keep, lax.dynamic_index_in_dim(total, 1 - side, 1, keepdims=False)


def far_split(total):
    far_size, far, _, _ = dp_place()
    rows = [
        lax.dynamic_index_in_dim(total, lax.rem(far + s, far_size), 0, keepdims=False)
        for s in range(far_size)
    ]
    return rows[0], rows[1:]


def shards(
    tokens, cond, cotangent, w_qkv, b_qv, w_proj, b_proj, w_fc1, b_fc1, w_fc2, b_fc2, w_ada, b_ada
):
    tensor_size = lax.axis_size("tensor")
    dp_size = lax.axis_size("dp")
    tensor_pos = lax.axis_index("tensor")
    dp_pos = lax.axis_index("dp")
    row_count, width = tokens.shape
    group_rows = row_count * tensor_size
    depth = w_qkv.shape[0]
    local_width = w_qkv.shape[2]
    hidden = w_fc1.shape[1]
    pairs = local_width // PAIR
    groups = 2 if pairs % 2 == 0 else 1
    group_width = local_width // groups
    assert cond.shape[0] == 1 and group_rows == LEN

    def row_sum(v):
        return jnp.sum(v, 0, dtype=f32)

    def cols_of(values, owner):
        return lax.dynamic_slice_in_dim(values, owner * local_width, local_width, values.ndim - 1)

    proj_parts = rel_gather(w_proj.T, "tensor")
    qkv_parts = [
        w_qkv[:, :, g * group_width : (g + 1) * group_width].reshape(depth, 3 * group_width)
        for g in range(groups)
    ]
    attn_w = lax.all_gather(jnp.concatenate(proj_parts + qkv_parts, 1), "dp", axis=0, tiled=True)
    mlp_w = lax.all_gather(jnp.concatenate([w_fc1, w_fc2.T], 1), "dp", axis=0, tiled=True)
    tok_parts = rel_gather(tokens, "tensor")
    cot_all = jnp.concatenate(rel_gather(after(cotangent, *tok_parts), "tensor"), 0)
    core_one = lax.rem(dp_pos, 2).astype(jnp.int32).reshape(1)

    vectors = jnp.concatenate([b_qv.reshape(-1), b_fc1])
    packed = xor_gather(jnp.concatenate([cond.reshape(-1), vectors]), True)
    cond_all = packed[:, :width]
    own_vec = sort_xor(packed[:, width:], True)
    piece = b_proj.shape[0]
    n_fc1 = b_fc1.shape[0]
    qv_bias = own_vec[:, : 2 * piece].reshape(dp_size, 2, piece).transpose(1, 0, 2)
    qv_bias = qv_bias.reshape(2, local_width)
    fc1_bias = own_vec[:, 2 * piece :].reshape(1, hidden)

    silu_all = jax.nn.silu(cond_all.astype(f32)).astype(bf16)
    silu_own = lax.dynamic_slice(silu_all, (0, dp_pos * depth), (dp_size, depth))
    ada_flat = w_ada.reshape(depth, 6 * local_width)
    biases = jnp.concatenate([b_ada, b_proj[None], b_fc2[None]]).astype(f32)
    lane = lax.broadcasted_iota(jnp.int32, (1, local_width), 1)
    biases = jnp.where(lane // piece == dp_pos, jnp.tile(biases, (1, dp_size)), 0.0)
    mod_part = jnp.pad(dot_nn(silu_own, ada_flat), ((0, 0), (0, 2 * local_width)))
    mod_part = mod_part + biases.reshape(1, 8 * local_width)
    mod_half = xor_scatter_sum(mod_part, True).reshape(8, local_width)
    modul = jnp.concatenate(sort_rel(rel_gather(mod_half, "tensor"), "tensor"), 1)
    shift_one, scale_one, gate_one, shift_two, scale_two, gate_two, proj_bias, fc2_bias = [
        modul[k : k + 1] for k in range(8)
    ]

    x_all = jnp.concatenate(tok_parts, 0)
    inputs = x_all.astype(f32)
    normed_one, mean_one, rstd_one = normalize(inputs)
    hidden_one = (normed_one * (1.0 + scale_one) + shift_one).astype(bf16)
    hidden_one = lax.optimization_barrier(hidden_one)
    qkv, heads_out, lse, heads_other = [], [], [], []
    for g in range(groups):
        cols = slice(g * group_width, (g + 1) * group_width)
        bias = jnp.concatenate([qv_bias[0, cols], jnp.zeros((group_width,), f32), qv_bias[1, cols]])
        left = hidden_one if g == 0 else after(hidden_one, heads_out[-1])
        at = width + 3 * group_width * g
        qkv.append((dot_nn(left, attn_w[:, at : at + 3 * group_width]) + bias).astype(bf16))
        out, log_total = attend(qkv[g], group_width)
        heads_out.append(out)
        lse.append(log_total)
        heads_other.append([shift(out, "tensor", s) for s in range(1, tensor_size)])
    heads_rel = [heads_out] + [[v[s - 1] for v in heads_other] for s in range(1, tensor_size)]
    hidden_two, grad_m, dm_sum, branch_attn, middle, mean_two, rstd_two = middle_part(
        heads_rel, attn_w, x_all, cot_all, modul, row_count
    )

    activ, grad_pre, fc1_sum, own_two, rest_two = mlp_both(
        hidden_two, grad_m, mlp_w, fc1_bias, row_count
    )

    def owners_sum(own, rest):
        arrived = [
            shift(rest[(s - 1) * row_count : s * row_count], "tensor", -s)
            for s in range(1, tensor_size)
        ]
        return own, arrived

    def add_up(own, arrived):
        for part in arrived:
            own = own + part.astype(f32)
        return own

    run = dp_pos >= 0

    def weight_part(rest_two, *args):
        arrived = owners_sum(None, rest_two)[1]
        return arrived, mlp_weight_grads(*args, row_count)

    arrived_two, (mlp_grads, own_mlp, rest_mlp, mlp_sum) = together(
        run, weight_part, rest_two, hidden_two, grad_m, grad_pre, activ, mlp_w, cot_all
    )
    mlp_grads = lax.psum_scatter(mlp_grads, "dp", scatter_dimension=0, tiled=True)

    grad_out = cotangent.astype(f32)
    grad_mid, grad_a, sums_two, *grad_pieces = middle_back(
        own_two, arrived_two, cotangent, middle, branch_attn, mean_two, rstd_two, modul, attn_w, group_width
    )

    def heads_of(pieces, g):
        parts = [pieces[g]]
        for j in range(1, tensor_size):
            s = tensor_size - j
            parts.append(shift(pieces[s * groups + g], "tensor", -s))
        return jnp.concatenate(parts, 0)

    last = groups - 1
    grad_heads = heads_of(grad_pieces, 0)
    dqkv, early = [], []
    if last:

        def first_group(pieces, heads, qkv_g, lse_g, left):
            moved = heads_of(pieces, 1)
            grads = attend_back(qkv_g, heads, lse_g, group_width)
            return moved, grads, col_grads(left, [grads], core_one, depth)

        grad_heads, grads, early = together(
            run, first_group, grad_pieces, grad_heads, qkv[0], lse[0], hidden_one
        )
        dqkv.append(grads)

    def last_group(grad_a, early, heads, qkv_g, lse_g, before, x_all):
        grad_a_rows = jnp.concatenate(rel_gather(grad_a, "tensor"), 0)
        if early:
            early = add_low(early[0], xor_step(early[1], "dp", 1))
        grads = attend_back(qkv_g, heads, lse_g, group_width)
        back = hidden_back(x_all, before + [grads], attn_w, width, row_count)
        return grad_a_rows, early, grads, back

    grad_a_rows, early, grads, (own_one, rest_one, sums_one) = together(
        run, last_group, grad_a, early, grad_heads, qkv[last], lse[last], dqkv, x_all
    )
    dqkv = dqkv + [grads]

    grad_mod = jnp.concatenate([sums_one, sums_two, mlp_sum + fc2_bias * row_sum(grad_out)[None]])
    grad_mod_own = cols_of(grad_mod, tensor_pos)
    for s in range(1, tensor_size):
        owner = lax.rem(tensor_pos - s + tensor_size, tensor_size)
        grad_mod_own = grad_mod_own + shift(cols_of(grad_mod, owner), "tensor", -s)
    grad_mod_own = grad_mod_own.astype(bf16).reshape(6 * local_width)
    late = [
        jnp.concatenate(pair, 1)
        for pair in zip(
            col_grads(hidden_one, [dqkv[last]], core_one, depth),
            col_grads(grad_a_rows, [out[None] for out in heads_out], core_one, depth),
        )
    ]
    grad_vec = jnp.concatenate(
        [row_sum(d[0].astype(f32)) for d in dqkv]
        + [row_sum(d[2].astype(f32)) for d in dqkv]
        + [
            cols_of(row_sum(grad_a_rows.astype(f32)), tensor_pos),
            fc1_sum.reshape(-1),
            cols_of(dm_sum[0], tensor_pos),
        ]
    )

    late = add_low(late[0], xor_step(late[1], "dp", 1))
    total = jnp.concatenate([early, late], 1) if last else late
    side_keep, side_send = side_split(total, depth)

    def side_part(rest_one, side_keep, side_send, grad_mod_own, grad_vec):
        arrived = owners_sum(None, rest_one)[1]
        side = xor_step(side_send, "dp", 2)

        def small(grad_mod_own, grad_vec):
            grad_mod_all = xor_gather(grad_mod_own, True)
            silu_part = dot_nt(grad_mod_all, ada_flat)
            return grad_mod_all, silu_part, xor_sum(grad_vec, True)

        out = together(run, small, grad_mod_own, grad_vec)
        return arrived, far_split(add_low(side_keep, side)), out

    arrived_one, (far_own, far_sends), (grad_mod_all, silu_part, grad_vec) = together(
        run, side_part, rest_one, side_keep, side_send, grad_mod_own, grad_vec
    )

    def far_part(far_own, far_sends, rest_mlp, own_mlp, silu_part, own_one, arrived_one, grad_mod_all):
        arrived_mlp = owners_sum(None, rest_mlp)[1]
        far_arrived = [far_shift(part, s + 1) for s, part in enumerate(far_sends)]

        def small(silu_part, own_one, arrived_one, grad_mod_all):
            grad_hidden_one = add_up(own_one, arrived_one)
            n1, r1 = normed_one[:row_count], rstd_one[:row_count]
            grad_tokens = grad_mid + norm_back(grad_hidden_one * (1.0 + scale_one), n1, r1)
            grad_ada = dot_tn(silu_own, grad_mod_all)
            ada_sum = jnp.sum(grad_mod_all, 0, dtype=f32)
            return grad_tokens.astype(bf16), xor_gather(silu_part, False), grad_ada, ada_sum

        out = together(run, small, silu_part, own_one, arrived_one, grad_mod_all)
        attn_grads = add_up(far_own.astype(f32), far_arrived)
        branch_mlp = add_up(own_mlp, arrived_mlp) + fc2_bias
        block_out = (middle + gate_two * branch_mlp).astype(bf16)
        return block_out, attn_grads, out

    block_out, attn_grads, (grad_tokens, silu_all, grad_ada, ada_sum) = together(
        run, far_part, far_own, far_sends, rest_mlp, own_mlp, silu_part, own_one, arrived_one, grad_mod_all
    )
    grad_ada = grad_ada.reshape(depth, 6, local_width)
    ada_sum = ada_sum.reshape(6, local_width)
    grad_ada_bias = lax.dynamic_slice_in_dim(ada_sum, dp_pos * piece, piece, 1)
    mine = (xor_of(False)[:, None] == xor_of(True)[None, :]).astype(f32)
    silu_rows = sort_xor(jnp.sum(silu_all * mine[:, :, None], 1), False).reshape(1, width)
    grad_silu = silu_rows
    for s in range(1, tensor_size):
        grad_silu = grad_silu + shift(silu_rows, "tensor", s)
    _, silu_back = jax.vjp(jax.nn.silu, cond.astype(f32))
    grad_cond = silu_back(grad_silu)[0]
    grad_qkv = attn_grads[:, : 3 * local_width].reshape(depth, groups, 3, group_width)
    grad_qkv = grad_qkv.transpose(0, 2, 1, 3).reshape(depth, 3, local_width)
    grad_proj = attn_grads[:, 3 * local_width :]

    def own_piece(start, size):
        return lax.dynamic_slice_in_dim(grad_vec, start + dp_pos * size, size, 0)

    grad_qv_bias = jnp.stack([own_piece(0, piece), own_piece(local_width, piece)])
    grad_proj_bias = own_piece(2 * local_width, piece)
    grad_fc1_bias = own_piece(3 * local_width, n_fc1)
    grad_fc2_bias = own_piece(3 * local_width + hidden, piece)

    mlp_grads = mlp_grads.astype(f32)
    return (
        block_out,
        grad_tokens,
        grad_cond,
        grad_qkv,
        grad_qv_bias,
        grad_proj.T,
        grad_proj_bias,
        mlp_grads[:, :hidden],
        grad_fc1_bias,
        mlp_grads[:, hidden:].T,
        grad_fc2_bias,
        grad_ada,
        grad_ada_bias,
    )


def solution(mesh):
    placed = (
        P(("dp", "tensor"), None),
        P("dp", None),
        P(("dp", "tensor"), None),
        P("dp", None, "tensor"),
        P(None, ("tensor", "dp")),
        P("tensor", "dp"),
        P(("tensor", "dp")),
        P("dp", "tensor"),
        P(("tensor", "dp")),
        P("tensor", "dp"),
        P(("tensor", "dp")),
        P("dp", None, "tensor"),
        P(None, ("tensor", "dp")),
    )
    return jax.shard_map(
        shards,
        mesh=mesh,
        in_specs=placed,
        out_specs=(
            P(("dp", "tensor"), None),
            P(("dp", "tensor"), None),
            P("dp", None),
            P("dp", None, "tensor"),
            P(None, ("tensor", "dp")),
            P("tensor", "dp"),
            P(("tensor", "dp")),
            P("dp", "tensor"),
            P(("tensor", "dp")),
            P("tensor", "dp"),
            P(("tensor", "dp")),
            P("dp", None, "tensor"),
            P(None, ("tensor", "dp")),
        ),
        check_vma=False,
    )
```

time: 473 us -> 388 us (0.82)
  waiting for transfers between devices: 205 us -> 96.8 us
  matrix products: 94.6 us -> 11.5 us
  Pallas kernels: 50.7 us -> 132 us
  local copies, waits for them, and re-layouts: 24.6 us -> 42.8 us
    pallas_call x0 -> x8, Pallas kernels: none -> 78.6 us  [the longest x1 22.8 us: mlp_weight_grads(): pl.pallas_call(partial(mlp_grads_kernel, own_rows, half), grid=(2 * half,...]
    reduce_scatter x1, waiting for transfers between devices: 70.8 us -> 0.01 us  [shards(): lax.psum_scatter(mlp_grads, 'dp', scatter_dimension=0, tiled=True)]
    ppermute x13 -> x14, waiting for transfers between devices: 80.2 us -> 31.8 us  [shift(): return lax.ppermute(x, axis, [(i, (i + step) % size) for i in range(size)])]
    dot_general x7 -> x1, matrix products: 38.5 us -> 1.7 us  [dot_nt(): lax.dot_general(a, b, (((1,), (1,)), ((), ())), preferred_element_type=f32)]
    dot_general x5 -> x1, matrix products: 27.2 us -> 2.05 us  [dot_tn(): lax.dot_general(a, b, (((0,), (0,)), ((), ())), preferred_element_type=f32)]
    dot_general x5 -> x3, matrix products: 28.5 us -> 7.39 us  [dot_nn(): lax.dot_general(a, b, (((1,), (0,)), ((), ())), preferred_element_type=f32)]
    all_gather x2, waiting for transfers between devices: 8.38 us -> 20 us  [the longest x1 14.1 us: shards(): lax.all_gather(jnp.concatenate(proj_parts + qkv_parts, 1), 'dp', axis=0,...]
    concatenate x18 -> x19, other arithmetic: 16.5 us -> 7.73 us  [the longest x9 2.33 us: xor_gather(): out = jnp.concatenate([out, xor_step(out, 'dp', bit)], 0)]
  transfers between devices with their start and end apart: 37 -> 43, of which waited for: 29 -> 25; matrix products, arithmetic and copies ran while one was open for 26% -> 19% of each run, Pallas kernels for 11% -> 29%
where the time goes in v2:
time: 388 us; the launch traced here: 382 us
  Pallas kernels  132 us (34%)
  waiting for transfers between devices  96.8 us (25%)
  starting transfers between devices  46.7 us (12%)
  local copies, waits for them, and re-layouts  42.8 us (11%)
  other arithmetic  37.6 us (10%)
  between operations  14.7 us (4%)
  matrix products  11.5 us (3%)
    ppermute x23, waiting for transfers between devices, xor_step(): return lax.ppermute(x, axis, [(i, i ^ bit) for i in range(size)])  44.9 us
    ppermute x14, waiting for transfers between devices, shift(): return lax.ppermute(x, axis, [(i, (i + step) % size) for i in range(size)])  31.8 us
    pallas_call x2, Pallas kernels, attend_back(): pl.pallas_call(partial(attend_back_kernel, 256), grid=(pairs,), in_specs=...  29 us
    pallas_call x2, Pallas kernels, attend(): pl.pallas_call(partial(attend_kernel, 256), grid=(pairs,), in_specs=spec,...  24.1 us
    pallas_call x1, Pallas kernels, mlp_weight_grads(): pl.pallas_call(partial(mlp_grads_kernel, own_rows, half), grid=(2 * half,...  22.8 us
    ppermute x23, starting transfers between devices, xor_step(): return lax.ppermute(x, axis, [(i, i ^ bit) for i in range(size)])  22.6 us
    pallas_call x1, Pallas kernels, mlp_both(): pl.pallas_call(partial(mlp_kernel, own_rows, 256), grid=(steps,), in_spec...  22.3 us
    ppermute x14, starting transfers between devices, shift(): return lax.ppermute(x, axis, [(i, (i + step) % size) for i in range(size)])  19.7 us
  transfers between devices with their start and end apart: 43, of which 25 were waited for; matrix products, arithmetic and copies ran while one was open for 19% of the time, Pallas kernels for 29%

profile of v2, /device:TPU:0, one launch (start us, length us, event | category | flops | bytes accessed | tf_op | source)
XLA Modules:
  0.0 382.2 jit_solution(14211743835672436202)
XLA Ops:
  59.2 14.1 %all-gather.3.cloned.1.call-done.refs_4_.refs_7_ = bf16[1024,2560]{1,0:T(8,128)(2,1)} async-done(((bf16[64,2560]{1,0:T(8,128)(2,1)}), bf16[1024,2560]{1,0:T(8,128)(2,1)}) %all-gather.3.cloned.1.call-update) | async-done | bytes 5242896 | tf_op jit(solution)/shard_map/all_gather | solution.py:696
  77.2 12.2 %attend.2 = (bf16[1024,256]{1,0:T(8,128)(2,1)S(1)}, f32[2,2,1024]{2,1,0:T(2,128)}) custom-call(bf16[1024,768]{1,0:T(8,128)(2,1)S(1)} %add_convert_fusion.5.q_ref.k_ref.v_ref, bf16[1024,768]{1,0:T(8,128)(2,1)S(1)} %add_convert_fusion.5.q_ref.k_ref.v_ref, bf16[1024,768]{1,0:T(8,128)(2,1)S(1)} %add_convert_fusion.5.q_ref.k_ref.v_ref), custom_call_target="tpu_custom_call" | custom-call | flops 4294967296 | bytes 2097152 | tf_op jit(solution)/shard_map/attend/pallas_call | solution.py:73
  92.8 12.0 %attend.3 = (bf16[1024,256]{1,0:T(8,128)(2,1)S(1)}, f32[2,2,1024]{2,1,0:T(2,128)}) custom-call(bf16[1024,768]{1,0:T(8,128)(2,1)S(1)} %add_convert_fusion.4.q_ref.k_ref.v_ref, bf16[1024,768]{1,0:T(8,128)(2,1)S(1)} %add_convert_fusion.4.q_ref.k_ref.v_ref, bf16[1024,768]{1,0:T(8,128)(2,1)S(1)} %add_convert_fusion.4.q_ref.k_ref.v_ref), custom_call_target="tpu_custom_call" | custom-call | flops 4294967296 | bytes 2097152 | tf_op jit(solution)/shard_map/attend/pallas_call | solution.py:73
  108.5 11.1 %collective-permute-done.34.refs_3_ = bf16[1024,256]{1,0:T(8,128)(2,1)S(1)} collective-permute-done((bf16[1024,256]{1,0:T(8,128)(2,1)S(1)}, bf16[1024,256]{1,0:T(8,128)(2,1)S(1)}, u32[]{:S(2)}, u32[]{:S(2)}) %collective-permute-start.34) | collective-permute-done | bytes 524320 | tf_op jit(solution)/shard_map/ppermute | solution.py:562
  120.3 9.8 %collective-permute-done.33.refs_2_ = bf16[1024,256]{1,0:T(8,128)(2,1)S(1)} collective-permute-done((bf16[1024,256]{1,0:T(8,128)(2,1)S(1)}, bf16[1024,256]{1,0:T(8,128)(2,1)S(1)}, u32[]{:S(2)}, u32[]{:S(2)}) %collective-permute-start.33) | collective-permute-done | bytes 524320 | tf_op jit(solution)/shard_map/ppermute | solution.py:562
  134.0 9.0 %middle_part.1 = (bf16[1024,1024]{1,0:T(8,128)(2,1)}, bf16[1024,1024]{1,0:T(8,128)(2,1)}, f32[1,1024]{1,0:T(1,128)S(1)}, f32[512,1024]{1,0:T(8,128)S(1)}, f32[51...) custom-call(bf16[1024,256]{1,0:T(8,128)(2,1)S(1)} %copy-done.4, bf16[1024,256]{1,0:T(8,128)(2,1)S(1)} %copy-done.7, ...), custom_call_target="tpu_custom_call" | custom-call | flops 2147483648 | bytes 16777216 | tf_op jit(solution)/shard_map/middle_part/pallas_call | solution.py:370
  143.7 5.9 %all-gather.5.cloned.1.call-done.w1_ref.w2_ref = bf16[1024,4096]{1,0:T(8,128)(2,1)} async-done(((bf16[64,4096]{1,0:T(8,128)(2,1)}), bf16[1024,4096]{1,0:T(8,128)(2,1)}) %all-gather.5.cloned.1.call-update) | async-done | bytes 8388624 | tf_op jit(solution)/shard_map/all_gather | solution.py:697
  149.6 22.3 %mlp_both.1 = (bf16[1024,2048]{1,0:T(8,128)(2,1)}, bf16[1024,2048]{1,0:T(8,128)(2,1)}, f32[1,2048]{1,0:T(1,128)S(1)}, f32[512,1024]{1,0:T(8,128)S(1)}, bf16[512,1024]{1,0:T(8,128)(2,1)}) custom-call(bf16[1024,1024]{1,0:T(8,128)(2,1)} %get-tuple-element.332.h_ref, bf16[1024,1024]{1,0:T(8,128)(2,1)} %get-tuple-element.333.dm_ref, ...), custom_call_target="tpu_custom_call" | custom-call | flops 12884901888 | bytes 29360128 | tf_op jit(solution)/shard_map/mlp_both/pallas_call | solution.py:217
  173.3 25.6 %conditional.7 = (bf16[512,1024]{1,0:T(8,128)(2,1)}, bf16[1024,4096]{1,0:T(8,128)(2,1)}, f32[512,1024]{1,0:T(8,128)}, bf16[512,1024]{1,0:T(8,128)(2,1)}, f32[1,1024]{1,0:T(1,128)S(1)}) conditional(s32[]{:T(128)} %convert_element_type.138, () %tuple.80, (bf16[512,1024]{1,0:T(8,128)(2,1)}, bf16[1024,1024]{1,0:T(8,128)(2,1)}, ...), branch_computations={%region_2.3_spmd, %region_3.4_spmd} | conditional | flops 12884901888 | bytes 33554512 | solution.py:631
  174.7 22.8 %mlp_weight_grads.1 = (bf16[1024,4096]{1,0:T(8,128)(2,1)}, f32[512,1024]{1,0:T(8,128)}, bf16[512,1024]{1,0:T(8,128)(2,1)}, f32[1,1024]{1,0:T(1,128)S(1)}) custom-call(bf16[1024,1024]{1,0:T(8,128)(2,1)} %get-tuple-element.180.h_ref, bf16[1024,1024]{1,0:T(8,128)(2,1)} %get-tuple-element.181.dm_ref, bf16[1024,2048]{1,0:T(8,128)(2,1)} %get-tuple-element.182.dpre_ref, ...), custom_call_target="tpu_custom_call" | custom-call | flops 12884901888 | bytes 29360128 | tf_op jit(solution)/shard_map/cond/branch_1_fun/mlp_weight_grads/pallas_call | solution.py:286
  202.4 6.7 %middle_back.1 = (f32[512,1024]{1,0:T(8,128)}, bf16[512,1024]{1,0:T(8,128)(2,1)}, f32[3,1024]{1,0:T(4,128)S(1)}, bf16[512,256]{1,0:T(8,128)(2,1)S(1)}, bf16[512,...) custom-call(f32[512,1024]{1,0:T(8,128)S(1)} %copy-done.2, ...), custom_call_target="tpu_custom_call" | custom-call | flops 1073741824 | bytes 14680064 | tf_op jit(solution)/shard_map/middle_back/pallas_call | solution.py:439
  211.3 5.8 %collective-permute-done.36 = bf16[512,256]{1,0:T(8,128)(2,1)S(1)} collective-permute-done((bf16[512,256]{1,0:T(8,128)(2,1)S(1)}, bf16[512,256]{1,0:T(8,128)(2,1)S(1)}, u32[]{:S(2)}, u32[]{:S(2)}) %collective-permute-start.36) | collective-permute-done | bytes 262176 | tf_op jit(solution)/shard_map/ppermute | solution.py:562
  217.2 20.3 %conditional.8 = (bf16[1024,256]{1,0:T(8,128)(2,1)S(1)}, bf16[3,1024,256]{2,1,0:T(8,128)(2,1)}, bf16[512,768]{1,0:T(8,128)(2,1)}, bf16[512,768]{1,0:T(8,128)(2,1)}) conditional(s32[]{:T(128)} %convert_element_type.138, () %tuple.86, (bf16[512,256]{1,0:T(8,128)(2,1)S(1)}, bf16[512,256]{1,0:T(8,128)(2,1)S(1)}, bf16[1024,768]{1,0:T(8,128)(2,1)S(1)}, ...), branch_computations={%region_4.5_spmd, %region_5.6_spmd} | conditional | flops 12349079552 | bytes 11010120 | solution.py:631
  218.8 14.3 %attend_back.2.refs_0_ = bf16[3,1024,256]{2,1,0:T(8,128)(2,1)} custom-call(bf16[1024,768]{1,0:T(8,128)(2,1)S(1)} %get-tuple-element.192.q_ref.k_ref.v_ref, bf16[1024,768]{1,0:T(8,128)(2,1)S(1)} %get-tuple-element.192.q_ref.k_ref.v_ref, bf16[1024,768]{1,0:T(8,128)(2,1)S(1)} %get-tuple-element.192.q_ref.k_ref.v_ref, ...), custom_call_target="tpu_custom_call" | custom-call | flops 10737418240 | bytes 3670016 | tf_op jit(solution)/shard_map/cond/branch_1_fun/attend_back/pallas_call | solution.py:134
  233.0 4.4 %col_grads.3 = (bf16[512,768]{1,0:T(8,128)(2,1)}, bf16[512,768]{1,0:T(8,128)(2,1)}) custom-call(s32[1]{0:T(128)} %get-tuple-element.195.core_ref, bf16[1024,1024]{1,0:T(8,128)(2,1)S(1)} %get-tuple-element.196.left_ref, bf16[3,1024,256]{2,1,0:T(8,128)(2,1)} %attend_back.2.refs_0_), custom_call_target="tpu_custom_call" | custom-call | flops 1610612736 | bytes 5242880 | tf_op jit(solution)/shard_map/cond/branch_1_fun/col_grads/pallas_call | solution.py:483
  238.4 27.4 %conditional.9 = (bf16[1024,1024]{1,0:T(8,128)(2,1)S(1)}, bf16[512,768]{1,0:T(8,128)(2,1)S(1)}, bf16[3,1024,256]{2,1,0:T(8,128)(2,1)S(1)}, f32[512,1024]{1,0:T(8...) conditional(s32[]{:T(128)} %convert_element_type.138, () %tuple.85, (bf16[512,1024]{1,0:T(8,128)(2,1)}, ...), branch_computations={%region_6.7_spmd, %region_7.8_spmd} | conditional | flops 13964410880 | bytes 63701280 | solution.py:631
  239.0 14.8 %attend_back.3.refs_2_ = bf16[3,1024,256]{2,1,0:T(8,128)(2,1)S(1)} custom-call(bf16[1024,768]{1,0:T(8,128)(2,1)} %get-tuple-element.202.q_ref.k_ref.v_ref, bf16[1024,768]{1,0:T(8,128)(2,1)} %get-tuple-element.202.q_ref.k_ref.v_ref, bf16[1024,768]{1,0:T(8,128)(2,1)} %get-tuple-element.202.q_ref.k_ref.v_ref, bf16[1024,256]{1,0:T(8,128)(2,1)} %get-tuple-element.203.do_ref, ...), custom_call_target="tpu_custom_call" | custom-call | flops 10737418240 | bytes 3670016 | tf_op jit(solution)/shard_map/cond/branch_1_fun/attend_back/pallas_call | solution.py:134
  253.8 10.1 %hidden_back.1 = (f32[512,1024]{1,0:T(8,128)}, bf16[512,1024]{1,0:T(8,128)(2,1)}, f32[2,1024]{1,0:T(2,128)S(1)}) custom-call(bf16[1024,1024]{1,0:T(8,128)(2,1)S(1)} %get-tuple-element.205.refs_0_, bf16[3,1024,256]{2,1,0:T(8,128)(2,1)} %get-tuple-element.206.refs_1_, bf16[3,1024,256]{2,1,0:T(8,128)(2,1)S(1)} %attend_back.3.refs_2_, ...), custom_call_target="tpu_custom_call" | custom-call | flops 3221225472 | bytes 10485760 | tf_op jit(solution)/shard_map/cond/branch_1_fun/hidden_back/pallas_call | solution.py:530
  275.8 42.3 %conditional.10 = (bf16[512,1024]{1,0:T(8,128)(2,1)}, bf16[64,2048]{1,0:T(8,128)(2,1)}, bf16[64,2048]{1,0:T(8,128)(2,1)}, bf16[64,2048]{1,0:T(8,128)(2,1)}, bf16...) conditional(s32[]{:T(128)} %convert_element_type.138, () %tuple.84, ...), branch_computations={%region_14.15_spmd, %region_15.18_spmd} | conditional | flops 8699981 | bytes 17696204 | solution.py:631
  278.5 36.7 %conditional = (bf16[16,3072]{1,0:T(8,128)(2,1)}, f32[16,64]{1,0:T(8,128)}, f32[4096]{0:T(1024)}) conditional(s32[]{:T(128)} %convert_element_type.106, () %tuple.56, (bf16[6,512]{1,0:T(8,128)(2,1)S(1)}, bf16[64,3072]{1,0:T(8,128)(2,1)S(1)}, f32[4096]{0:T(1024)}) %tuple.146), branch_computations={%region_16.16_spmd, %region_17.17_spmd} | conditional | flops 6602752 | bytes 1901000 | solution.py:631
  294.3 4.3 %collective-permute-done.10 = f32[4096]{0:T(1024)S(1)} collective-permute-done((f32[4096]{0:T(1024)S(1)}, f32[4096]{0:T(1024)S(1)}, u32[]{:S(2)}, u32[]{:S(2)}) %collective-permute-start.10) | collective-permute-done | bytes 16416 | tf_op jit(solution)/shard_map/cond/branch_1_fun/cond/branch_1_fun/ppermute | solution.py:567
  299.2 10.9 %collective-permute-done.11 = f32[4096]{0:T(1024)S(1)} collective-permute-done((f32[4096]{0:T(1024)S(1)}, f32[4096]{0:T(1024)S(1)}, u32[]{:S(2)}, u32[]{:S(2)}) %collective-permute-start.11) | collective-permute-done | bytes 16416 | tf_op jit(solution)/shard_map/cond/branch_1_fun/cond/branch_1_fun/ppermute | solution.py:567
  318.2 42.2 %conditional.11 = (bf16[512,1024]{1,0:T(8,128)(2,1)}, f32[64,2048]{1,0:T(8,128)}, bf16[512,1024]{1,0:T(8,128)(2,1)}, f32[16,16,64]{2,1,0:T(8,128)}, f32[6,512]{1,0:T(8,128)}, /*index=5*/f32[64,6,512]{2,0,1:T(8,128)}) conditional(s32[]{:T(128)} %convert_element_type.138, () %tuple.79, (f32[8,1024]{1,0:T(8,128)}, bf16[512,1024]{1,0:T(8,128)(2,1)}, ...), branch_computations={%region_18.19_spmd, %region_19.25_spmd} | conditional | flops 18352128 | bytes 58806832 | solution.py:631
  323.0 29.8 %conditional.1 = (bf16[512,1024]{1,0:T(8,128)(2,1)}, f32[16,16,64]{2,1,0:T(8,128)}, f32[64,6,512]{2,1,0:T(8,128)S(1)}, f32[6,512]{1,0:T(8,128)}) conditional(s32[]{:T(128)} %convert_element_type.116, () %tuple.62, (f32[1024]{0:T(1024)}, bf16[512,1024]{1,0:T(8,128)(2,1)}, f32[512,1024]{1,0:T(8,128)S(1)}, f32[1,1024]{1,0:T(1,128)}, ...), branch_computations={%region_20.20_spmd, %region_21.24_spmd} | conditional | flops 14288896 | bytes 33607900 | solution.py:631
  (346 shorter events, 176.8 us)
Async XLA Ops:
  7.3 66.1 %all-gather.3.cloned.1.call-start = ((), (), s32[]{:S(2)}) async-start(), calls=%async_computation.1 | async-start | bytes 5570560 | tf_op jit(solution)/shard_map/all_gather | solution.py:696
  14.4 135.2 %all-gather.5.cloned.1.call-start = ((), (), s32[]{:S(2)}) async-start(), calls=%async_computation.2 | async-start | bytes 8912896 | tf_op jit(solution)/shard_map/all_gather | solution.py:697
  16.3 356.3 %reduce-scatter.2.cloned.1.call-start = ((), (), s32[]{:S(2)}) async-start(), calls=%async_computation.3 | async-start | bytes 8912896 | tf_op jit(solution)/shard_map/reduce_scatter | solution.py:772
  16.6 34.9 %collective-permute-start.31 = (bf16[512,1024]{1,0:T(8,128)(2,1)}, bf16[512,1024]{1,0:T(8,128)(2,1)}, u32[]{:S(2)}, u32[]{:S(2)}) collective-permute-start(bf16[512,1024]{1,0:T(8,128)(2,1)} %param.27), channel_id=1, source_target_pairs={{0,1},{1,0},{2,3},{3,2},{4,5},{5,4},{6,7},{7,6},{8,9},{9,8},{10,11... | collective-permute-start | bytes 3145736 | tf_op jit(solution)/shard_map/ppermute | solution.py:562
  57.7 49.3 %collective-permute-start.35 = (bf16[512,1024]{1,0:T(8,128)(2,1)S(1)}, bf16[512,1024]{1,0:T(8,128)(2,1)}, u32[]{:S(2)}, u32[]{:S(2)}) collective-permute-start(bf16[512,1024]{1,0:T(8,128)(2,1)S(1)} %copy-done), channel_id=1, source_target_pairs={{0,1},{1,0},{2,3},{3,2},{4,5},{5,4},{6,7},{7,6},{8,9},{9,8},{10,11... | collective-permute-start | bytes 3145736 | tf_op jit(solution)/shard_map/ppermute | solution.py:562
  104.8 14.8 %collective-permute-start.34 = (bf16[1024,256]{1,0:T(8,128)(2,1)S(1)}, bf16[1024,256]{1,0:T(8,128)(2,1)S(1)}, u32[]{:S(2)}, u32[]{:S(2)}) collective-permute-start(bf16[1024,256]{1,0:T(8,128)(2,1)S(1)} %get-tuple-element.330.refs_1_), channel_id=1, source_target_pairs={{0,1},{1,0},{2,3},{3,2},{4,5},{5,4},{6,7},{7,6},{8,9},{9,8},{10,11... | collective-permute-start | bytes 1572872 | tf_op jit(solution)/shard_map/ppermute | solution.py:562
  106.3 23.9 %collective-permute-start.33 = (bf16[1024,256]{1,0:T(8,128)(2,1)S(1)}, bf16[1024,256]{1,0:T(8,128)(2,1)S(1)}, u32[]{:S(2)}, u32[]{:S(2)}) collective-permute-start(bf16[1024,256]{1,0:T(8,128)(2,1)S(1)} %get-tuple-element.328.refs_0_), channel_id=1, source_target_pairs={{0,1},{1,0},{2,3},{3,2},{4,5},{5,4},{6,7},{7,6},{8,9},{9,8},{10,11... | collective-permute-start | bytes 1572872 | tf_op jit(solution)/shard_map/ppermute | solution.py:562
  173.3 25.6 %collective-permute-start = (bf16[512,1024]{1,0:T(8,128)(2,1)}, bf16[512,1024]{1,0:T(8,128)(2,1)}, u32[]{:S(2)}, u32[]{:S(2)}) collective-permute-start(bf16[512,1024]{1,0:T(8,128)(2,1)} %get-tuple-element.179), channel_id=1, source_target_pairs={{0,1},{1,0},{2,3},{3,2},{4,5},{5,4},{6,7},{7,6},{8,9},{9,8},{10,11... | collective-permute-start | bytes 3145736 | tf_op jit(solution)/shard_map/cond/branch_1_fun/ppermute | solution.py:562
  209.1 8.0 %collective-permute-start.36 = (bf16[512,256]{1,0:T(8,128)(2,1)S(1)}, bf16[512,256]{1,0:T(8,128)(2,1)S(1)}, u32[]{:S(2)}, u32[]{:S(2)}) collective-permute-start(bf16[512,256]{1,0:T(8,128)(2,1)S(1)} %get-tuple-element.349), channel_id=1, source_target_pairs={{0,1},{1,0},{2,3},{3,2},{4,5},{5,4},{6,7},{7,6},{8,9},{9,8},{10,11... | collective-permute-start | bytes 786440 | tf_op jit(solution)/shard_map/ppermute | solution.py:562
  217.2 20.3 %collective-permute-start.1 = (bf16[512,256]{1,0:T(8,128)(2,1)S(1)}, bf16[512,256]{1,0:T(8,128)(2,1)S(1)}, u32[]{:S(2)}, u32[]{:S(2)}) collective-permute-start(bf16[512,256]{1,0:T(8,128)(2,1)S(1)} %get-tuple-element.191), channel_id=1, source_target_pairs={{0,1},{1,0},{2,3},{3,2},{4,5},{5,4},{6,7},{7,6},{8,9},{9,8},{10,11... | collective-permute-start | bytes 786440 | tf_op jit(solution)/shard_map/cond/branch_1_fun/ppermute | solution.py:562
  238.4 25.8 %collective-permute-start.2 = (bf16[512,1024]{1,0:T(8,128)(2,1)}, bf16[512,1024]{1,0:T(8,128)(2,1)S(1)}, u32[]{:S(2)}, u32[]{:S(2)}) collective-permute-start(bf16[512,1024]{1,0:T(8,128)(2,1)} %get-tuple-element.199), channel_id=1, source_target_pairs={{0,1},{1,0},{2,3},{3,2},{4,5},{5,4},{6,7},{7,6},{8,9},{9,8},{10,11... | collective-permute-start | bytes 3145736 | tf_op jit(solution)/shard_map/cond/branch_1_fun/ppermute | solution.py:562
  239.0 25.0 %collective-permute-start.3 = (bf16[512,768]{1,0:T(8,128)(2,1)}, bf16[512,768]{1,0:T(8,128)(2,1)S(1)}, u32[]{:S(2)}, u32[]{:S(2)}) collective-permute-start(bf16[512,768]{1,0:T(8,128)(2,1)} %get-tuple-element.201), channel_id=1, source_target_pairs={{0,2},{2,0},{4,6},{6,4},{8,10},{10,8},{12,14},{14,12},{16,18},{18,... | collective-permute-start | bytes 2359304 | tf_op jit(solution)/shard_map/cond/branch_1_fun/ppermute | solution.py:567
  265.9 7.2 %collective-permute-start.38 = (f32[6,512]{1,0:T(8,128)S(1)}, f32[6,512]{1,0:T(8,128)S(1)}, u32[]{:S(2)}, u32[]{:S(2)}) collective-permute-start(f32[6,512]{1,0:T(8,128)S(1)} %constant_dynamic-slice_fusion.1), channel_id=1, source_target_pairs={{0,1},{1,0},{2,3},{3,2},{4,5},{5,4},{6,7},{7,6},{8,9},{9,8},{10,11... | collective-permute-start | bytes 36872 | tf_op jit(solution)/shard_map/ppermute | solution.py:562
  277.8 37.5 %collective-permute-start.13 = (bf16[4,64,2048]{2,1,0:T(8,128)(2,1)S(1)}, bf16[4,64,2048]{2,1,0:T(8,128)(2,1)}, u32[]{:S(2)}, u32[]{:S(2)}) collective-permute-start(bf16[4,64,2048]{2,1,0:T(8,128)(2,1)S(1)} %dynamic-slice_bitcast_fusion), channel_id=1, source_target_pairs={{0,4},{2,6},{4,0},{6,2},{8,12},{10,14},{12,8},{14,10},{16,20},{18,... | collective-permute-start | bytes 3145736 | tf_op jit(solution)/shard_map/cond/branch_1_fun/ppermute | solution.py:567
  277.9 40.3 %collective-permute-start.12 = (bf16[512,1024]{1,0:T(8,128)(2,1)}, bf16[512,1024]{1,0:T(8,128)(2,1)}, u32[]{:S(2)}, u32[]{:S(2)}) collective-permute-start(bf16[512,1024]{1,0:T(8,128)(2,1)} %get-tuple-element.214), channel_id=1, source_target_pairs={{0,1},{1,0},{2,3},{3,2},{4,5},{5,4},{6,7},{7,6},{8,9},{9,8},{10,11... | collective-permute-start | bytes 3145736 | tf_op jit(solution)/shard_map/cond/branch_1_fun/ppermute | solution.py:562
  285.0 6.4 %collective-permute-start.6 = (bf16[4,3072]{1,0:T(4,128)(2,1)S(1)}, bf16[4,3072]{1,0:T(4,128)(2,1)S(1)}, u32[]{:S(2)}, u32[]{:S(2)}) collective-permute-start(bf16[4,3072]{1,0:T(4,128)(2,1)S(1)} %pad_maximum_fusion.3), channel_id=1, source_target_pairs={{0,16},{2,18},{4,20},{6,22},{8,24},{10,26},{12,28},{14,30},{16,0},... | collective-permute-start | bytes 73736 | tf_op jit(solution)/shard_map/cond/branch_1_fun/cond/branch_1_fun/ppermute | solution.py:567
  291.4 19.3 %collective-permute-start.7 = (bf16[8,3072]{1,0:T(8,128)(2,1)S(1)}, bf16[8,3072]{1,0:T(8,128)(2,1)}, u32[]{:S(2)}, u32[]{:S(2)}) collective-permute-start(bf16[8,3072]{1,0:T(8,128)(2,1)S(1)} %pad_maximum_fusion.2), channel_id=1, source_target_pairs={{0,4},{2,6},{4,0},{6,2},{8,12},{10,14},{12,8},{14,10},{16,20},{18,... | collective-permute-start | bytes 147464 | tf_op jit(solution)/shard_map/cond/branch_1_fun/cond/branch_1_fun/ppermute | solution.py:567
  298.6 11.5 %collective-permute-start.11 = (f32[4096]{0:T(1024)S(1)}, f32[4096]{0:T(1024)S(1)}, u32[]{:S(2)}, u32[]{:S(2)}) collective-permute-start(f32[4096]{0:T(1024)S(1)} %add.234), channel_id=1, source_target_pairs={{0,4},{2,6},{4,0},{6,2},{8,12},{10,14},{12,8},{14,10},{16,20},{18,... | collective-permute-start | bytes 49160 | tf_op jit(solution)/shard_map/cond/branch_1_fun/cond/branch_1_fun/ppermute | solution.py:567
  318.2 38.7 %collective-permute-start.18 = (bf16[512,1024]{1,0:T(8,128)(2,1)}, bf16[512,1024]{1,0:T(8,128)(2,1)}, u32[]{:S(2)}, u32[]{:S(2)}) collective-permute-start(bf16[512,1024]{1,0:T(8,128)(2,1)} %get-tuple-element.237), channel_id=1, source_target_pairs={{0,1},{1,0},{2,3},{3,2},{4,5},{5,4},{6,7},{7,6},{8,9},{9,8},{10,11... | collective-permute-start | bytes 3145736 | tf_op jit(solution)/shard_map/cond/branch_1_fun/ppermute | solution.py:562
  318.8 36.1 %collective-permute-start.19 = (bf16[64,2048]{1,0:T(8,128)(2,1)}, bf16[64,2048]{1,0:T(8,128)(2,1)S(1)}, u32[]{:S(2)}, u32[]{:S(2)}) collective-permute-start(bf16[64,2048]{1,0:T(8,128)(2,1)} %get-tuple-element.240), channel_id=1, source_target_pairs={{0,8},{2,10},{4,12},{6,14},{8,16},{10,18},{12,20},{14,22},{16,24},... | collective-permute-start | bytes 786440 | tf_op jit(solution)/shard_map/cond/branch_1_fun/ppermute | solution.py:645
  319.3 35.6 %collective-permute-start.20 = (bf16[64,2048]{1,0:T(8,128)(2,1)}, bf16[64,2048]{1,0:T(8,128)(2,1)}, u32[]{:S(2)}, u32[]{:S(2)}) collective-permute-start(bf16[64,2048]{1,0:T(8,128)(2,1)} %get-tuple-element.241), channel_id=1, source_target_pairs={{0,16},{2,18},{4,20},{6,22},{8,24},{10,26},{12,28},{14,30},{16,0},... | collective-permute-start | bytes 786440 | tf_op jit(solution)/shard_map/cond/branch_1_fun/ppermute | solution.py:645
  320.7 34.2 %collective-permute-start.21 = (bf16[64,2048]{1,0:T(8,128)(2,1)}, bf16[64,2048]{1,0:T(8,128)(2,1)}, u32[]{:S(2)}, u32[]{:S(2)}) collective-permute-start(bf16[64,2048]{1,0:T(8,128)(2,1)} %get-tuple-element.242), channel_id=1, source_target_pairs={{0,24},{2,26},{4,28},{6,30},{8,0},{10,2},{12,4},{14,6},{16,8},{18,... | collective-permute-start | bytes 786440 | tf_op jit(solution)/shard_map/cond/branch_1_fun/ppermute | solution.py:645
  323.0 13.9 %collective-permute-start.14 = (f32[1,16,64]{2,1,0:T(8,128)}, f32[1,16,64]{2,1,0:T(8,128)S(1)}, u32[]{:S(2)}, u32[]{:S(2)}) collective-permute-start(f32[1,16,64]{2,1,0:T(8,128)} %bitcast.8), channel_id=1, source_target_pairs={{0,2},{2,0},{4,6},{6,4},{8,10},{10,8},{12,14},{14,12},{16,18},{18,... | collective-permute-start | bytes 12296 | tf_op jit(solution)/shard_map/cond/branch_1_fun/cond/branch_1_fun/ppermute | solution.py:567
  361.8 10.2 %collective-permute-start.39 = (f32[1,1024]{1,0:T(1,128)S(1)}, f32[1,1024]{1,0:T(1,128)S(1)}, u32[]{:S(2)}, u32[]{:S(2)}) collective-permute-start(f32[1,1024]{1,0:T(1,128)S(1)} %reshape.298), channel_id=1, source_target_pairs={{0,1},{1,0},{2,3},{3,2},{4,5},{5,4},{6,7},{7,6},{8,9},{9,8},{10,11... | collective-permute-start | bytes 12296 | tf_op jit(solution)/shard_map/ppermute | solution.py:562
  (82 other events, 898.3 us)
Sparse Core Ops, SparseCore 0:
  14.5 58.8 all-gather.2
  76.1 73.4 all-gather.4
  199.0 107.7 reduce-scatter.1

commit v3 on v2

--- a/solution.py
+++ b/solution.py
@@ -47,19 +47,28 @@
     keys = k_ref[...]
     values_t = v_ref[...].astype(f32).T.astype(bf16)
     sub = lax.broadcasted_iota(jnp.int32, (PAIR, 1), 0)
-    for start in range(0, rows, step_rows):
+    tasks = [(start, head) for start in range(0, rows, step_rows) for head in range(2)]
+
+    def products(task):
+        start, head = task
         queries = q_ref[start : start + step_rows, :]
-        out_t = []
-        for head in range(2):
-            q_head = jnp.where(masks[head], queries, jnp.zeros_like(queries))
-            scores = dot_nt(keys, q_head) * log2_scale
-            peak = jnp.max(scores, 0, keepdims=True)
-            terms = jnp.exp2(scores - peak)
-            total = jnp.sum(terms, 0, keepdims=True)
-            out_t.append(dot_nn(values_t, terms.astype(bf16)) * (1.0 / total))
-            lse_ref[0, head : head + 1, start : start + step_rows] = peak + jnp.log2(total)
-        joined = jnp.where(sub < HEAD_DIM, out_t[0], out_t[1])
-        o_ref[start : start + step_rows, :] = joined.T.astype(bf16)
+        return dot_nt(keys, jnp.where(masks[head], queries, jnp.zeros_like(queries)))
+
+    ahead = products(tasks[0])
+    out_t = []
+    for t, (start, head) in enumerate(tasks):
+        scores = ahead * log2_scale
+        if t + 1 < len(tasks):
+            ahead = products(tasks[t + 1])
+        peak = jnp.max(scores, 0, keepdims=True)
+        terms = jnp.exp2(scores - peak)
+        total = jnp.sum(terms, 0, keepdims=True)
+        out_t.append(dot_nn(values_t, terms.astype(bf16)) * (1.0 / total))
+        lse_ref[0, head : head + 1, start : start + step_rows] = peak + jnp.log2(total)
+        if head:
+            joined = jnp.where(sub < HEAD_DIM, out_t[0], out_t[1])
+            o_ref[start : start + step_rows, :] = joined.T.astype(bf16)
+            out_t = []
 
 
 def attend(qkv, local_width):
@@ -71,7 +80,7 @@
         for part in range(3)
     ]
     return pl.pallas_call(
-        partial(attend_kernel, 256),
+        partial(attend_kernel, min(512, rows)),
         grid=(pairs,),
         in_specs=spec,
         out_specs=[
@@ -82,7 +91,7 @@
             jax.ShapeDtypeStruct((rows, local_width), bf16),
             jax.ShapeDtypeStruct((pairs, 2, rows), f32),
         ],
-        compiler_params=pltpu.CompilerParams(vmem_limit_bytes=28 * MIB),
+        compiler_params=pltpu.CompilerParams(vmem_limit_bytes=40 * MIB),
         cost_estimate=pl.CostEstimate(
             flops=4 * heads * rows * rows * 256,
             bytes_accessed=rows * local_width * 8,
@@ -101,24 +110,34 @@
     keys_t = keys.astype(f32).T.astype(bf16)
     d_keys = jnp.zeros((rows, PAIR), f32)
     d_values = jnp.zeros((rows, PAIR), f32)
-    for start in range(0, rows, step_rows):
+    tasks = [(start, head) for start in range(0, rows, step_rows) for head in range(2)]
+
+    def products(task):
+        start, head = task
         queries = q_ref[start : start + step_rows, :]
         d_out = do_ref[start : start + step_rows, :]
-        dq_t = []
-        for head in range(2):
-            q_head = jnp.where(masks[head], queries, jnp.zeros_like(queries))
-            do_head = jnp.where(masks[head], d_out, jnp.zeros_like(d_out))
-            lse = lse_ref[0, head : head + 1, start : start + step_rows]
-            probs = jnp.exp2(dot_nt(keys, q_head) * log2_scale - lse)
-            d_probs = dot_nt(values, do_head)
-            weighted = probs * d_probs
-            row_dot = jnp.sum(weighted, 0, keepdims=True)
-            d_scores = (weighted - probs * row_dot).astype(bf16)
-            d_values = d_values + dot_nn(probs.astype(bf16), do_head)
-            d_keys = d_keys + dot_nn(d_scores, q_head)
-            dq_t.append(dot_nn(keys_t, d_scores))
-        joined = jnp.where(sub < HEAD_DIM, dq_t[0], dq_t[1])
-        dqkv_ref[0, start : start + step_rows, :] = (joined.T * score_scale).astype(bf16)
+        q_head = jnp.where(masks[head], queries, jnp.zeros_like(queries))
+        do_head = jnp.where(masks[head], d_out, jnp.zeros_like(d_out))
+        return q_head, do_head, dot_nt(keys, q_head), dot_nt(values, do_head)
+
+    ahead = products(tasks[0])
+    dq_t = []
+    for t, (start, head) in enumerate(tasks):
+        q_head, do_head, scores, d_probs = ahead
+        if t + 1 < len(tasks):
+            ahead = products(tasks[t + 1])
+        lse = lse_ref[0, head : head + 1, start : start + step_rows]
+        probs = jnp.exp2(scores * log2_scale - lse)
+        weighted = probs * d_probs
+        row_dot = jnp.sum(weighted, 0, keepdims=True)
+        d_scores = (weighted - probs * row_dot).astype(bf16)
+        d_values = d_values + dot_nn(probs.astype(bf16), do_head)
+        d_keys = d_keys + dot_nn(d_scores, q_head)
+        dq_t.append(dot_nn(keys_t, d_scores))
+        if head:
+            joined = jnp.where(sub < HEAD_DIM, dq_t[0], dq_t[1])
+            dqkv_ref[0, start : start + step_rows, :] = (joined.T * score_scale).astype(bf16)
+            dq_t = []
     dqkv_ref[1] = (d_keys * score_scale).astype(bf16)
     dqkv_ref[2] = d_values.astype(bf16)
 
@@ -215,7 +234,7 @@
     block = min(512, hidden)
     steps = hidden // block
     return pl.pallas_call(
-        partial(mlp_kernel, own_rows, 256),
+        partial(mlp_kernel, own_rows, rows),
         grid=(steps,),
         in_specs=[
             full_spec((rows, width)),
@@ -495,50 +514,46 @@
     )(core, left, *rights)
 
 
-def hidden_back_kernel(own_rows, groups, *refs):
-    x_ref = refs[0]
-    grads = refs[1 : 1 + groups]
-    weights = refs[1 + groups : 1 + 2 * groups]
-    own_ref, rest_ref, sums_ref, acc_ref = refs[1 + 2 * groups :]
-    j = pl.program_id(0)
-    part = dot_nt(grads[0][0], weights[0][...])
-    for g in range(1, groups):
-        part = part + dot_nt(grads[g][0], weights[g][...])
-
-    @pl.when(j == 0)
-    def _():
-        acc_ref[...] = part
-
-    @pl.when(j > 0)
-    def _():
-        acc_ref[...] += part
-
-    @pl.when(j == pl.num_programs(0) - 1)
-    def _():
-        total = acc_ref[...]
-        normed, _, _ = normalize(x_ref[...].astype(f32))
-        own_ref[...] = total[:own_rows]
-        rest_ref[...] = total[own_rows:].astype(bf16)
-        sums_ref[0:1, :] = jnp.sum(total, 0, keepdims=True)
-        sums_ref[1:2, :] = jnp.sum(total * normed, 0, keepdims=True)
+def hidden_back_kernel(own_steps, first, x_ref, w_ref, *refs):
+    own_ref, rest_ref, sums_ref = refs[-3:]
+    pieces = [ref[p] for ref in refs[:-3] for p in range(3)]
+    total = dot_nt(jnp.concatenate(pieces, 1), w_ref[:, first:])
+    normed, _, _ = normalize(x_ref[...].astype(f32))
+    sums = jnp.concatenate(
+        [jnp.sum(total, 0, keepdims=True), jnp.sum(total * normed, 0, keepdims=True)]
+    )
+    i = pl.program_id(0)
+
+    @pl.when(i == 0)
+    def _():
+        sums_ref[...] = sums
+
+    @pl.when(i > 0)
+    def _():
+        sums_ref[...] += sums
+
+    @pl.when(i < own_steps)
+    def _():
+        own_ref[...] = total
+
+    @pl.when(i >= own_steps)
+    def _():
+        rest_ref[...] = total.astype(bf16)
 
 
 def hidden_back(x_all, grads, weight, first, own_rows):
     rows, width = x_all.shape
-    groups = len(grads)
     columns = grads[0].shape[2]
+    block = min(256, own_rows)
+    own_steps = own_rows // block
     return pl.pallas_call(
-        partial(hidden_back_kernel, own_rows, groups),
-        grid=(3,),
-        in_specs=[full_spec((rows, width))]
-        + [pl.BlockSpec((1, rows, columns), lambda j: (j, 0, 0))] * groups
-        + [
-            pl.BlockSpec((width, columns), partial(lambda at, j: (0, at + j), first // columns + 3 * g))
-            for g in range(groups)
-        ],
+        partial(hidden_back_kernel, own_steps, first),
+        grid=(rows // block,),
+        in_specs=[pl.BlockSpec((block, width), lambda i: (i, 0)), full_spec(weight.shape)]
+        + [pl.BlockSpec((3, block, columns), lambda i: (0, i, 0))] * len(grads),
         out_specs=[
-            full_spec((own_rows, width)),
-            full_spec((rows - own_rows, width)),
+            pl.BlockSpec((block, width), lambda i: (jnp.minimum(i, own_steps - 1), 0)),
+            pl.BlockSpec((block, width), lambda i: (jnp.maximum(i - own_steps, 0), 0)),
             full_spec((2, width)),
         ],
         out_shape=[
@@ -546,15 +561,14 @@
             jax.ShapeDtypeStruct((rows - own_rows, width), bf16),
             jax.ShapeDtypeStruct((2, width), f32),
         ],
-        scratch_shapes=[pltpu.VMEM((rows, width), f32)],
         compiler_params=pltpu.CompilerParams(vmem_limit_bytes=40 * MIB),
         cost_estimate=pl.CostEstimate(
-            flops=6 * rows * width * columns * groups,
-            bytes_accessed=4 * rows * width + 12 * rows * columns * groups,
+            flops=6 * rows * width * columns * len(grads),
+            bytes_accessed=4 * rows * width + 12 * rows * columns * len(grads),
             transcendentals=0,
         ),
         name="hidden_back",
-    )(x_all, *grads, *([weight] * groups))
+    )(x_all, weight, *grads)
 
 
 def shift(x, axis, step):
@@ -580,8 +594,11 @@
 
 
 def xor_gather(x, side_last):
-    out = x[None]
-    for bit in bits_of(side_last):
+    return widen(x[None], bits_of(side_last))
+
+
+def widen(out, bits):
+    for bit in bits:
         out = jnp.concatenate([out, xor_step(out, "dp", bit)], 0)
     return out
 
@@ -688,15 +705,14 @@
     def cols_of(values, owner):
         return lax.dynamic_slice_in_dim(values, owner * local_width, local_width, values.ndim - 1)
 
-    proj_parts = rel_gather(w_proj.T, "tensor")
+    run = dp_pos >= 0
     qkv_parts = [
         w_qkv[:, :, g * group_width : (g + 1) * group_width].reshape(depth, 3 * group_width)
         for g in range(groups)
     ]
-    attn_w = lax.all_gather(jnp.concatenate(proj_parts + qkv_parts, 1), "dp", axis=0, tiled=True)
+    attn_w = lax.all_gather(jnp.concatenate([w_proj.T] + qkv_parts, 1), "dp", axis=0, tiled=True)
     mlp_w = lax.all_gather(jnp.concatenate([w_fc1, w_fc2.T], 1), "dp", axis=0, tiled=True)
-    tok_parts = rel_gather(tokens, "tensor")
-    cot_all = jnp.concatenate(rel_gather(after(cotangent, *tok_parts), "tensor"), 0)
+    x_all = jnp.concatenate(rel_gather(tokens, "tensor"), 0)
     core_one = lax.rem(dp_pos, 2).astype(jnp.int32).reshape(1)
 
     vectors = jnp.concatenate([b_qv.reshape(-1), b_fc1])
@@ -723,25 +739,40 @@
         modul[k : k + 1] for k in range(8)
     ]
 
-    x_all = jnp.concatenate(tok_parts, 0)
-    inputs = x_all.astype(f32)
-    normed_one, mean_one, rstd_one = normalize(inputs)
-    hidden_one = (normed_one * (1.0 + scale_one) + shift_one).astype(bf16)
-    hidden_one = lax.optimization_barrier(hidden_one)
-    qkv, heads_out, lse, heads_other = [], [], [], []
-    for g in range(groups):
+    def first_rows(cotangent, x_all, shift_one, scale_one):
+        moved = rel_gather(cotangent, "tensor")[1:]
+        normed, _, rstd = normalize(x_all.astype(f32))
+        return moved, (normed * (1.0 + scale_one) + shift_one).astype(bf16)
+
+    cot_parts, hidden_one = together(run, first_rows, cotangent, x_all, shift_one, scale_one)
+    cot_all = jnp.concatenate([cotangent] + cot_parts, 0)
+    normed_one, _, rstd_one = normalize(tokens.astype(f32))
+
+    def attend_group(g, moving, hidden_one, attn_w, qv_bias):
+        moved = rel_gather(moving, "tensor")[1:]
         cols = slice(g * group_width, (g + 1) * group_width)
         bias = jnp.concatenate([qv_bias[0, cols], jnp.zeros((group_width,), f32), qv_bias[1, cols]])
-        left = hidden_one if g == 0 else after(hidden_one, heads_out[-1])
-        at = width + 3 * group_width * g
-        qkv.append((dot_nn(left, attn_w[:, at : at + 3 * group_width]) + bias).astype(bf16))
-        out, log_total = attend(qkv[g], group_width)
+        at = local_width + 3 * group_width * g
+        weight = attn_w[:, at : at + 3 * group_width]
+        qkv = (dot_nn(hidden_one, weight) + bias).astype(bf16)
+        return moved, qkv, attend(qkv, group_width)
+
+    qkv, heads_out, lse, moved = [], [], [], []
+    for g in range(groups):
+        moving = heads_out[g - 1] if g else attn_w[:, :local_width]
+        parts, qkv_g, (out, log_total) = together(
+            run, partial(attend_group, g), moving, hidden_one, attn_w, qv_bias
+        )
+        qkv.append(qkv_g)
         heads_out.append(out)
         lse.append(log_total)
-        heads_other.append([shift(out, "tensor", s) for s in range(1, tensor_size)])
+        moved.append(parts)
+    moved.append(rel_gather(heads_out[-1], "tensor")[1:])
+    proj_w = jnp.concatenate([attn_w[:, :local_width]] + moved[0], 1)
+    heads_other = moved[1:]
     heads_rel = [heads_out] + [[v[s - 1] for v in heads_other] for s in range(1, tensor_size)]
     hidden_two, grad_m, dm_sum, branch_attn, middle, mean_two, rstd_two = middle_part(
-        heads_rel, attn_w, x_all, cot_all, modul, row_count
+        heads_rel, proj_w, x_all, cot_all, modul, row_count
     )
 
     activ, grad_pre, fc1_sum, own_two, rest_two = mlp_both(
@@ -760,8 +791,6 @@
             own = own + part.astype(f32)
         return own
 
-    run = dp_pos >= 0
-
     def weight_part(rest_two, *args):
         arrived = owners_sum(None, rest_two)[1]
         return arrived, mlp_weight_grads(*args, row_count)
@@ -773,7 +802,7 @@
 
     grad_out = cotangent.astype(f32)
     grad_mid, grad_a, sums_two, *grad_pieces = middle_back(
-        own_two, arrived_two, cotangent, middle, branch_attn, mean_two, rstd_two, modul, attn_w, group_width
+        own_two, arrived_two, cotangent, middle, branch_attn, mean_two, rstd_two, modul, proj_w, group_width
     )
 
     def heads_of(pieces, g):
@@ -803,7 +832,7 @@
         if early:
             early = add_low(early[0], xor_step(early[1], "dp", 1))
         grads = attend_back(qkv_g, heads, lse_g, group_width)
-        back = hidden_back(x_all, before + [grads], attn_w, width, row_count)
+        back = hidden_back(x_all, before + [grads], attn_w, local_width, row_count)
         return grad_a_rows, early, grads, back
 
     grad_a_rows, early, grads, (own_one, rest_one, sums_one) = together(
@@ -854,32 +883,60 @@
         run, side_part, rest_one, side_keep, side_send, grad_mod_own, grad_vec
     )
 
-    def far_part(far_own, far_sends, rest_mlp, own_mlp, silu_part, own_one, arrived_one, grad_mod_all):
+    def own_piece(values, start, size):
+        return lax.dynamic_slice_in_dim(values, start + dp_pos * size, size, 0)
+
+    def far_part(far_own, far_sends, rest_mlp, own_mlp, *args):
         arrived_mlp = owners_sum(None, rest_mlp)[1]
         far_arrived = [far_shift(part, s + 1) for s, part in enumerate(far_sends)]
 
-        def small(silu_part, own_one, arrived_one, grad_mod_all):
+        def small(silu_part, *values):
+            near = widen(silu_part[None], bits_of(False)[:2])
+            near, own_one, arrived_one, grad_mod_all, grad_vec, mlp_grads = lax.optimization_barrier(
+                (near,) + values
+            )
+            silu_all = widen(near, bits_of(False)[2:])
             grad_hidden_one = add_up(own_one, arrived_one)
-            n1, r1 = normed_one[:row_count], rstd_one[:row_count]
-            grad_tokens = grad_mid + norm_back(grad_hidden_one * (1.0 + scale_one), n1, r1)
-            grad_ada = dot_tn(silu_own, grad_mod_all)
-            ada_sum = jnp.sum(grad_mod_all, 0, dtype=f32)
-            return grad_tokens.astype(bf16), xor_gather(silu_part, False), grad_ada, ada_sum
-
-        out = together(run, small, silu_part, own_one, arrived_one, grad_mod_all)
+            grad_tokens = grad_mid + norm_back(
+                grad_hidden_one * (1.0 + scale_one), normed_one, rstd_one
+            )
+            grad_ada = dot_tn(silu_own, grad_mod_all).reshape(depth, 6, local_width)
+            ada_sum = jnp.sum(grad_mod_all, 0, dtype=f32).reshape(6, local_width)
+            vectors = (
+                lax.dynamic_slice_in_dim(ada_sum, dp_pos * piece, piece, 1),
+                jnp.stack([own_piece(grad_vec, 0, piece), own_piece(grad_vec, local_width, piece)]),
+                own_piece(grad_vec, 2 * local_width, piece),
+                own_piece(grad_vec, 3 * local_width, n_fc1),
+                own_piece(grad_vec, 3 * local_width + hidden, piece),
+            )
+            mlp_grads = mlp_grads.astype(f32)
+            mlp_grads = (mlp_grads[:, :hidden], mlp_grads[:, hidden:].T)
+            mine = (xor_of(False)[:, None] == xor_of(True)[None, :]).astype(f32)
+            silu_rows = sort_xor(jnp.sum(silu_all * mine[:, :, None], 1), False)
+            return grad_tokens.astype(bf16), silu_rows.reshape(1, width), grad_ada, vectors, mlp_grads
+
+        out = together(run, small, *args)
         attn_grads = add_up(far_own.astype(f32), far_arrived)
         branch_mlp = add_up(own_mlp, arrived_mlp) + fc2_bias
         block_out = (middle + gate_two * branch_mlp).astype(bf16)
         return block_out, attn_grads, out
 
-    block_out, attn_grads, (grad_tokens, silu_all, grad_ada, ada_sum) = together(
-        run, far_part, far_own, far_sends, rest_mlp, own_mlp, silu_part, own_one, arrived_one, grad_mod_all
-    )
-    grad_ada = grad_ada.reshape(depth, 6, local_width)
-    ada_sum = ada_sum.reshape(6, local_width)
-    grad_ada_bias = lax.dynamic_slice_in_dim(ada_sum, dp_pos * piece, piece, 1)
-    mine = (xor_of(False)[:, None] == xor_of(True)[None, :]).astype(f32)
-    silu_rows = sort_xor(jnp.sum(silu_all * mine[:, :, None], 1), False).reshape(1, width)
+    block_out, attn_grads, out = together(
+        run,
+        far_part,
+        far_own,
+        far_sends,
+        rest_mlp,
+        own_mlp,
+        silu_part,
+        own_one,
+        arrived_one,
+        grad_mod_all,
+        grad_vec,
+        mlp_grads,
+    )
+    grad_tokens, silu_rows, grad_ada, vectors, (grad_fc1, grad_fc2) = out
+    grad_ada_bias, grad_qv_bias, grad_proj_bias, grad_fc1_bias, grad_fc2_bias = vectors
     grad_silu = silu_rows
     for s in range(1, tensor_size):
         grad_silu = grad_silu + shift(silu_rows, "tensor", s)
@@ -887,28 +944,17 @@
     grad_cond = silu_back(grad_silu)[0]
     grad_qkv = attn_grads[:, : 3 * local_width].reshape(depth, groups, 3, group_width)
     grad_qkv = grad_qkv.transpose(0, 2, 1, 3).reshape(depth, 3, local_width)
-    grad_proj = attn_grads[:, 3 * local_width :]
-
-    def own_piece(start, size):
-        return lax.dynamic_slice_in_dim(grad_vec, start + dp_pos * size, size, 0)
-
-    grad_qv_bias = jnp.stack([own_piece(0, piece), own_piece(local_width, piece)])
-    grad_proj_bias = own_piece(2 * local_width, piece)
-    grad_fc1_bias = own_piece(3 * local_width, n_fc1)
-    grad_fc2_bias = own_piece(3 * local_width + hidden, piece)
-
-    mlp_grads = mlp_grads.astype(f32)
     return (
         block_out,
         grad_tokens,
         grad_cond,
         grad_qkv,
         grad_qv_bias,
-        grad_proj.T,
+        attn_grads[:, 3 * local_width :].T,
         grad_proj_bias,
-        mlp_grads[:, :hidden],
+        grad_fc1,
         grad_fc1_bias,
-        mlp_grads[:, hidden:].T,
+        grad_fc2,
         grad_fc2_bias,
         grad_ada,
         grad_ada_bias,

time: 388 us -> 363 us (0.936)
  waiting for transfers between devices: 96.8 us -> 84.5 us
  Pallas kernels: 132 us -> 120 us
  local copies, waits for them, and re-layouts: 42.8 us -> 34.1 us
  other arithmetic: 37.6 us -> 41.6 us
    all_gather x1, waiting for transfers between devices: 14.1 us -> 0.01 us  [shards(): lax.all_gather(jnp.concatenate([w_proj.T] + qkv_parts, 1), 'dp', axis=0,...]
    ppermute x14, waiting for transfers between devices: 31.8 us -> 45.2 us  [shift(): return lax.ppermute(x, axis, [(i, (i + step) % size) for i in range(size)])]
    pallas_call x4, Pallas kernels: 56.5 us -> 44.6 us  [the longest x1 19.8 us: mlp_both(): pl.pallas_call(partial(mlp_kernel, own_rows, rows), grid=(steps,), in_spe...]
    ppermute x23, waiting for transfers between devices: 44.9 us -> 38.2 us  [xor_step(): return lax.ppermute(x, axis, [(i, i ^ bit) for i in range(size)])]
    unnamed x109 -> x58, local copies, waits for them, and re-layouts: 12.9 us -> 7.44 us
    all_gather x1, waiting for transfers between devices: 5.88 us -> 0.97 us  [shards(): lax.all_gather(jnp.concatenate([w_fc1, w_fc2.T], 1), 'dp', axis=0, tiled=...]
    convert_element_type x2 -> x4, other arithmetic: 1.85 us -> 5.95 us  [the longest x1 3.72 us: first_rows(): return (moved, (normed * (1.0 + scale_one) + shift_one).astype(bf16))]
    cond x34 -> x35, local copies, waits for them, and re-layouts: 7.89 us -> 4.97 us
  transfers between devices with their start and end apart: 43 -> 43, of which waited for: 25 -> 24; matrix products, arithmetic and copies ran while one was open for 19% -> 21% of each run, Pallas kernels for 29% -> 28%
where the time goes in v3:
time: 363 us; the launch traced here: 357 us
  Pallas kernels  120 us (33%)
  waiting for transfers between devices  84.5 us (23%)
  starting transfers between devices  47.3 us (13%)
  other arithmetic  41.6 us (11%)
  local copies, waits for them, and re-layouts  34.1 us (9%)
  matrix products  14.7 us (4%)
  between operations  14.6 us (4%)
    ppermute x14, waiting for transfers between devices, shift(): return lax.ppermute(x, axis, [(i, (i + step) % size) for i in range(size)])  45.2 us
    ppermute x23, waiting for transfers between devices, xor_step(): return lax.ppermute(x, axis, [(i, i ^ bit) for i in range(size)])  38.2 us
    pallas_call x2, Pallas kernels, attend_back(): pl.pallas_call(partial(attend_back_kernel, 256), grid=(pairs,), in_specs=...  26.6 us
    ppermute x23, starting transfers between devices, xor_step(): return lax.ppermute(x, axis, [(i, i ^ bit) for i in range(size)])  24.2 us
    pallas_call x1, Pallas kernels, mlp_weight_grads(): pl.pallas_call(partial(mlp_grads_kernel, own_rows, half), grid=(2 * half,...  22.8 us
    pallas_call x1, Pallas kernels, mlp_both(): pl.pallas_call(partial(mlp_kernel, own_rows, rows), grid=(steps,), in_spe...  19.8 us
    ppermute x14, starting transfers between devices, shift(): return lax.ppermute(x, axis, [(i, (i + step) % size) for i in range(size)])  17.7 us
    pallas_call x2, Pallas kernels, attend(): pl.pallas_call(partial(attend_kernel, min(512, rows)), grid=(pairs,), in_...  16.5 us
  transfers between devices with their start and end apart: 43, of which 24 were waited for; matrix products, arithmetic and copies ran while one was open for 21% of the time, Pallas kernels for 28%

profile of v3, /device:TPU:0, one launch (start us, length us, event | category | flops | bytes accessed | tf_op | source)
XLA Modules:
  0.0 356.6 jit_solution(17755098491877835411)
XLA Ops:
  45.3 12.3 %collective-permute-done.33 = f32[8,512]{1,0:T(8,128)S(1)} collective-permute-done((f32[8,512]{1,0:T(8,128)S(1)}, f32[8,512]{1,0:T(8,128)S(1)}, u32[]{:S(2)}, u32[]{:S(2)}) %collective-permute-start.33) | collective-permute-done | bytes 16416 | tf_op jit(solution)/shard_map/ppermute | solution.py:576
  58.8 21.9 %conditional.10 = (bf16[512,1024]{1,0:T(8,128)(2,1)}, bf16[1024,1024]{1,0:T(8,128)(2,1)}) conditional(s32[]{:T(128)} %convert_element_type.144, () %tuple.109, (bf16[512,1024]{1,0:T(8,128)(2,1)S(1)}, bf16[1024,1024]{1,0:T(8,128)(2,1)}, f32[1,1024]{1,0:T(1,128)S(1)}, f32[8,1024]{1,0:T(8,128)S(1)}) %tuple.173), branch_computations={%region_0.1_spmd, %region_1.4_spmd} | conditional | flops 12584960 | bytes 12644408 | solution.py:648
  68.2 12.4 %collective-permute-done.1 = bf16[512,1024]{1,0:T(8,128)(2,1)} collective-permute-done((bf16[512,1024]{1,0:T(8,128)(2,1)S(1)}, bf16[512,1024]{1,0:T(8,128)(2,1)}, u32[]{:S(2)}, u32[]{:S(2)}) %collective-permute-start.1) | collective-permute-done | bytes 1048608 | tf_op jit(solution)/shard_map/cond/branch_1_fun/ppermute | solution.py:576
  81.9 23.2 %conditional.11 = (bf16[1024,512]{1,0:T(8,128)(2,1)}, bf16[1024,768]{1,0:T(8,128)(2,1)}, bf16[1024,256]{1,0:T(8,128)(2,1)}, f32[2,2,1024]{2,1,0:T(2,128)S(1)}) conditional(s32[]{:T(128)} %convert_element_type.144, () %tuple.108, (bf16[1024,512]{1,0:T(8,128)(2,1)S(1)}, bf16[1024,2048]{1,0:T(8,128)(2,1)}, bf16[1024,1024]{1,0:T(8,128)(2,1)}, ...), branch_computations={%region_4.5_spmd, %region_5.6_spmd} | conditional | flops 5907154432 | bytes 11548748 | solution.py:648
  88.6 8.4 %attend.2 = (bf16[1024,256]{1,0:T(8,128)(2,1)}, f32[2,2,1024]{2,1,0:T(2,128)S(1)}) custom-call(bf16[1024,768]{1,0:T(8,128)(2,1)} %add_convert_fusion.q_ref.k_ref.v_ref, bf16[1024,768]{1,0:T(8,128)(2,1)} %add_convert_fusion.q_ref.k_ref.v_ref, bf16[1024,768]{1,0:T(8,128)(2,1)} %add_convert_fusion.q_ref.k_ref.v_ref), custom_call_target="tpu_custom_call" | custom-call | flops 4294967296 | bytes 2097152 | tf_op jit(solution)/shard_map/cond/branch_1_fun/attend/pallas_call | solution.py:82
  97.0 8.1 %collective-permute-done.5 = bf16[1024,512]{1,0:T(8,128)(2,1)} collective-permute-done((bf16[1024,512]{1,0:T(8,128)(2,1)S(1)}, bf16[1024,512]{1,0:T(8,128)(2,1)}, u32[]{:S(2)}, u32[]{:S(2)}) %collective-permute-start.5) | collective-permute-done | bytes 1048608 | tf_op jit(solution)/shard_map/cond/branch_1_fun/ppermute | solution.py:576
  105.1 15.8 %conditional.12 = (bf16[1024,256]{1,0:T(8,128)(2,1)}, bf16[1024,768]{1,0:T(8,128)(2,1)}, bf16[1024,256]{1,0:T(8,128)(2,1)}, f32[2,2,1024]{2,1,0:T(2,128)S(1)}, bf16[1,1024,256]{2,1,0:T(8,128)(2,1)S(1)}) conditional(s32[]{:T(128)} %convert_element_type.144, () %tuple.112, (bf16[1024,256]{1,0:T(8,128)(2,1)}, bf16[1024,2048]{1,0:T(8,128)(2,1)}, ...), branch_computations={%region_6.7_spmd, %region_7.8_spmd} | conditional | flops 5907154432 | bytes 10500180 | solution.py:648
  111.7 8.1 %attend.3 = (bf16[1024,256]{1,0:T(8,128)(2,1)}, f32[2,2,1024]{2,1,0:T(2,128)S(1)}) custom-call(bf16[1024,768]{1,0:T(8,128)(2,1)} %add_convert_fusion.1.q_ref.k_ref.v_ref, bf16[1024,768]{1,0:T(8,128)(2,1)} %add_convert_fusion.1.q_ref.k_ref.v_ref, bf16[1024,768]{1,0:T(8,128)(2,1)} %add_convert_fusion.1.q_ref.k_ref.v_ref), custom_call_target="tpu_custom_call" | custom-call | flops 4294967296 | bytes 2097152 | tf_op jit(solution)/shard_map/cond/branch_1_fun/attend/pallas_call | solution.py:82
  125.1 5.2 %collective-permute-done.35.refs_3_ = bf16[1024,256]{1,0:T(8,128)(2,1)S(1)} collective-permute-done((bf16[1024,256]{1,0:T(8,128)(2,1)}, bf16[1024,256]{1,0:T(8,128)(2,1)S(1)}, u32[]{:S(2)}, u32[]{:S(2)}) %collective-permute-start.35) | collective-permute-done | bytes 524320 | tf_op jit(solution)/shard_map/ppermute | solution.py:576
  130.3 8.9 %middle_part.1 = (bf16[1024,1024]{1,0:T(8,128)(2,1)}, bf16[1024,1024]{1,0:T(8,128)(2,1)}, f32[1,1024]{1,0:T(1,128)S(1)}, f32[512,1024]{1,0:T(8,128)S(1)}, f32[51...) custom-call(bf16[1024,256]{1,0:T(8,128)(2,1)} %get-tuple-element.433.refs_0_, ...), custom_call_target="tpu_custom_call" | custom-call | flops 2147483648 | bytes 16777216 | tf_op jit(solution)/shard_map/middle_part/pallas_call | solution.py:389
  141.6 19.8 %mlp_both.1 = (bf16[1024,2048]{1,0:T(8,128)(2,1)}, bf16[1024,2048]{1,0:T(8,128)(2,1)}, f32[1,2048]{1,0:T(1,128)S(1)}, f32[512,1024]{1,0:T(8,128)S(1)}, bf16[512,1024]{1,0:T(8,128)(2,1)}) custom-call(bf16[1024,1024]{1,0:T(8,128)(2,1)} %get-tuple-element.438.h_ref, bf16[1024,1024]{1,0:T(8,128)(2,1)} %get-tuple-element.439.dm_ref, ...), custom_call_target="tpu_custom_call" | custom-call | flops 12884901888 | bytes 29360128 | tf_op jit(solution)/shard_map/mlp_both/pallas_call | solution.py:236
  162.8 25.6 %conditional.13 = (bf16[512,1024]{1,0:T(8,128)(2,1)}, bf16[1024,4096]{1,0:T(8,128)(2,1)}, f32[512,1024]{1,0:T(8,128)}, bf16[512,1024]{1,0:T(8,128)(2,1)}, f32[1,1024]{1,0:T(1,128)S(1)}) conditional(s32[]{:T(128)} %convert_element_type.144, () %tuple.107, (bf16[512,1024]{1,0:T(8,128)(2,1)}, bf16[1024,1024]{1,0:T(8,128)(2,1)}, ...), branch_computations={%region_8.9_spmd, %region_9.10_spmd} | conditional | flops 12884901888 | bytes 33554512 | solution.py:648
  164.3 22.8 %mlp_weight_grads.1 = (bf16[1024,4096]{1,0:T(8,128)(2,1)}, f32[512,1024]{1,0:T(8,128)}, bf16[512,1024]{1,0:T(8,128)(2,1)}, f32[1,1024]{1,0:T(1,128)S(1)}) custom-call(bf16[1024,1024]{1,0:T(8,128)(2,1)} %get-tuple-element.257.h_ref, bf16[1024,1024]{1,0:T(8,128)(2,1)} %get-tuple-element.258.dm_ref, bf16[1024,2048]{1,0:T(8,128)(2,1)} %get-tuple-element.259.dpre_ref, ...), custom_call_target="tpu_custom_call" | custom-call | flops 12884901888 | bytes 29360128 | tf_op jit(solution)/shard_map/cond/branch_1_fun/mlp_weight_grads/pallas_call | solution.py:305
  193.3 5.5 %middle_back.1 = (f32[512,1024]{1,0:T(8,128)}, bf16[512,1024]{1,0:T(8,128)(2,1)}, f32[3,1024]{1,0:T(4,128)S(1)}, bf16[512,256]{1,0:T(8,128)(2,1)S(1)}, bf16[512,...) custom-call(f32[512,1024]{1,0:T(8,128)S(1)} %copy-done.3, ...), custom_call_target="tpu_custom_call" | custom-call | flops 1073741824 | bytes 14680064 | tf_op jit(solution)/shard_map/middle_back/pallas_call | solution.py:458
  206.1 20.2 %conditional.14 = (bf16[1024,256]{1,0:T(8,128)(2,1)S(1)}, bf16[3,1024,256]{2,1,0:T(8,128)(2,1)}, bf16[512,768]{1,0:T(8,128)(2,1)}, bf16[512,768]{1,0:T(8,128)(2,1)}) conditional(s32[]{:T(128)} %convert_element_type.144, () %tuple.117, (bf16[512,256]{1,0:T(8,128)(2,1)S(1)}, bf16[512,256]{1,0:T(8,128)(2,1)S(1)}, bf16[1024,768]{1,0:T(8,128)(2,1)}, ...), branch_computations={%region_10.11_spmd, %region_11.12_spmd} | conditional | flops 12349079552 | bytes 11010120 | solution.py:648
  207.6 13.5 %attend_back.2.refs_0_ = bf16[3,1024,256]{2,1,0:T(8,128)(2,1)} custom-call(bf16[1024,768]{1,0:T(8,128)(2,1)} %get-tuple-element.269.q_ref.k_ref.v_ref, bf16[1024,768]{1,0:T(8,128)(2,1)} %get-tuple-element.269.q_ref.k_ref.v_ref, bf16[1024,768]{1,0:T(8,128)(2,1)} %get-tuple-element.269.q_ref.k_ref.v_ref, bf16[1024,256]{1,0:T(8,128)(2,1)S(1)} %get-tuple-element.270.do_ref, ...), custom_call_target="tpu_custom_call" | custom-call | flops 10737418240 | bytes 3670016 | tf_op jit(solution)/shard_map/cond/branch_1_fun/attend_back/pallas_call | solution.py:153
  226.3 23.6 %conditional.15 = (bf16[1024,1024]{1,0:T(8,128)(2,1)S(1)}, bf16[512,768]{1,0:T(8,128)(2,1)S(1)}, bf16[3,1024,256]{2,1,0:T(8,128)(2,1)}, f32[512,1024]{1,0:T(8,12...) conditional(s32[]{:T(128)} %convert_element_type.144, () %tuple.116, (bf16[512,1024]{1,0:T(8,128)(2,1)}, ...), branch_computations={%region_12.13_spmd, %region_13.14_spmd} | conditional | flops 13964410880 | bytes 60555532 | solution.py:648
  227.1 13.0 %attend_back.3.refs_1_ = bf16[3,1024,256]{2,1,0:T(8,128)(2,1)S(1)} custom-call(bf16[1024,768]{1,0:T(8,128)(2,1)} %get-tuple-element.279.q_ref.k_ref.v_ref, bf16[1024,768]{1,0:T(8,128)(2,1)} %get-tuple-element.279.q_ref.k_ref.v_ref, bf16[1024,768]{1,0:T(8,128)(2,1)} %get-tuple-element.279.q_ref.k_ref.v_ref, bf16[1024,256]{1,0:T(8,128)(2,1)} %copy-done.20, ...), custom_call_target="tpu_custom_call" | custom-call | flops 10737418240 | bytes 3670016 | tf_op jit(solution)/shard_map/cond/branch_1_fun/attend_back/pallas_call | solution.py:153
  240.2 8.3 %hidden_back.1 = (f32[512,1024]{1,0:T(8,128)}, bf16[512,1024]{1,0:T(8,128)(2,1)}, f32[2,1024]{1,0:T(2,128)S(1)}) custom-call(bf16[1024,1024]{1,0:T(8,128)(2,1)} %get-tuple-element.282.x_ref, bf16[1024,2048]{1,0:T(8,128)(2,1)S(1)} %copy-done.23, bf16[3,1024,256]{2,1,0:T(8,128)(2,1)} %get-tuple-element.284.refs_0_, bf16[3,1024,256]{2,1,0:T(8,128)(2,1)S(1)} %attend_back.3.refs_1_), custom_call_target="tpu_custom_call" | custom-call | flops 3221225472 | bytes 10485760 | tf_op jit(solution)/shard_map/cond/branch_1_fun/hidden_back/pallas_call | solution.py:549
  262.6 42.5 %conditional.16 = (bf16[512,1024]{1,0:T(8,128)(2,1)}, bf16[64,2048]{1,0:T(8,128)(2,1)}, bf16[64,2048]{1,0:T(8,128)(2,1)}, bf16[64,2048]{1,0:T(8,128)(2,1)}, bf16...) conditional(s32[]{:T(128)} %convert_element_type.144, () %tuple.115, ...), branch_computations={%region_20.21_spmd, %region_21.24_spmd} | conditional | flops 8699981 | bytes 17696204 | solution.py:648
  266.8 35.3 %conditional = (bf16[16,3072]{1,0:T(8,128)(2,1)}, f32[16,64]{1,0:T(8,128)}, f32[4096]{0:T(1024)}) conditional(s32[]{:T(128)} %convert_element_type.115, () %tuple.78, (bf16[6,512]{1,0:T(8,128)(2,1)S(1)}, bf16[64,3072]{1,0:T(8,128)(2,1)S(1)}, f32[4096]{0:T(1024)}) %tuple.178), branch_computations={%region_22.22_spmd, %region_23.23_spmd} | conditional | flops 6602752 | bytes 1901000 | solution.py:648
  287.0 9.9 %collective-permute-done.14 = f32[4096]{0:T(1024)S(1)} collective-permute-done((f32[4096]{0:T(1024)S(1)}, f32[4096]{0:T(1024)S(1)}, u32[]{:S(2)}, u32[]{:S(2)}) %collective-permute-start.14) | collective-permute-done | bytes 16416 | tf_op jit(solution)/shard_map/cond/branch_1_fun/cond/branch_1_fun/ppermute | solution.py:581
  305.1 38.2 %conditional.17 = (bf16[512,1024]{1,0:T(8,128)(2,1)}, f32[64,2048]{1,0:T(8,128)}, bf16[512,1024]{1,0:T(8,128)(2,1)}, f32[1,1024]{1,0:T(1,128)}, f32[6,32]{1,0:T(...) conditional(s32[]{:T(128)} %convert_element_type.144, ...), branch_computations={%region_25.26_spmd, %region_26.0_spmd} | conditional | flops 23052948 | bytes 68689384 | solution.py:648
  311.3 24.4 %conditional.1 = (bf16[512,1024]{1,0:T(8,128)(2,1)}, f32[1,1024]{1,0:T(1,128)}, f32[64,6,512]{2,1,0:T(8,128)S(1)}, f32[6,32]{1,0:T(8,128)}, f32[2,32]{1,0:T(2,12...) conditional(s32[]{:T(128)} %convert_element_type.127, () %tuple.85, ...), branch_computations={%region_27.27_spmd, %region_28.34_spmd} | conditional | flops 18989716 | bytes 43490388 | solution.py:648
  (308 shorter events, 185.3 us)
Async XLA Ops:
  7.3 73.4 %all-gather.3.cloned.1.call-start = ((), (), s32[]{:S(2)}) async-start(), calls=%async_computation.1 | async-start | bytes 4456448 | tf_op jit(solution)/shard_map/all_gather | solution.py:713
  9.9 131.6 %all-gather.5.cloned.1.call-start = ((), (), s32[]{:S(2)}) async-start(), calls=%async_computation.2 | async-start | bytes 8912896 | tf_op jit(solution)/shard_map/all_gather | solution.py:714
  11.9 293.2 %reduce-scatter.2.cloned.1.call-start = ((), (), s32[]{:S(2)}) async-start(), calls=%async_computation.3 | async-start | bytes 8912896 | tf_op jit(solution)/shard_map/reduce_scatter | solution.py:801
  35.2 22.5 %collective-permute-start.34 = (bf16[512,1024]{1,0:T(8,128)(2,1)S(1)}, bf16[512,1024]{1,0:T(8,128)(2,1)S(1)}, u32[]{:S(2)}, u32[]{:S(2)}) collective-permute-start(bf16[512,1024]{1,0:T(8,128)(2,1)S(1)} %copy-done.17), channel_id=1, source_target_pairs={{0,1},{1,0},{2,3},{3,2},{4,5},{5,4},{6,7},{7,6},{8,9},{9,8},{10,11... | collective-permute-start | bytes 3145736 | tf_op jit(solution)/shard_map/ppermute | solution.py:576
  43.2 14.4 %collective-permute-start.33 = (f32[8,512]{1,0:T(8,128)S(1)}, f32[8,512]{1,0:T(8,128)S(1)}, u32[]{:S(2)}, u32[]{:S(2)}) collective-permute-start(f32[8,512]{1,0:T(8,128)S(1)} %reshape_squeeze.3), channel_id=1, source_target_pairs={{0,1},{1,0},{2,3},{3,2},{4,5},{5,4},{6,7},{7,6},{8,9},{9,8},{10,11... | collective-permute-start | bytes 49160 | tf_op jit(solution)/shard_map/ppermute | solution.py:576
  58.8 21.9 %collective-permute-start.1 = (bf16[512,1024]{1,0:T(8,128)(2,1)S(1)}, bf16[512,1024]{1,0:T(8,128)(2,1)}, u32[]{:S(2)}, u32[]{:S(2)}) collective-permute-start(bf16[512,1024]{1,0:T(8,128)(2,1)S(1)} %get-tuple-element.240), channel_id=1, source_target_pairs={{0,1},{1,0},{2,3},{3,2},{4,5},{5,4},{6,7},{7,6},{8,9},{9,8},{10,11... | collective-permute-start | bytes 3145736 | tf_op jit(solution)/shard_map/cond/branch_1_fun/ppermute | solution.py:576
  81.9 23.2 %collective-permute-start.5 = (bf16[1024,512]{1,0:T(8,128)(2,1)S(1)}, bf16[1024,512]{1,0:T(8,128)(2,1)}, u32[]{:S(2)}, u32[]{:S(2)}) collective-permute-start(bf16[1024,512]{1,0:T(8,128)(2,1)S(1)} %get-tuple-element.244), channel_id=1, source_target_pairs={{0,1},{1,0},{2,3},{3,2},{4,5},{5,4},{6,7},{7,6},{8,9},{9,8},{10,11... | collective-permute-start | bytes 3145736 | tf_op jit(solution)/shard_map/cond/branch_1_fun/ppermute | solution.py:576
  105.1 15.8 %collective-permute-start.6 = (bf16[1024,256]{1,0:T(8,128)(2,1)}, bf16[1024,256]{1,0:T(8,128)(2,1)}, u32[]{:S(2)}, u32[]{:S(2)}) collective-permute-start(bf16[1024,256]{1,0:T(8,128)(2,1)} %get-tuple-element.250), channel_id=1, source_target_pairs={{0,1},{1,0},{2,3},{3,2},{4,5},{5,4},{6,7},{7,6},{8,9},{9,8},{10,11... | collective-permute-start | bytes 1572872 | tf_op jit(solution)/shard_map/cond/branch_1_fun/ppermute | solution.py:576
  120.9 9.4 %collective-permute-start.35 = (bf16[1024,256]{1,0:T(8,128)(2,1)}, bf16[1024,256]{1,0:T(8,128)(2,1)S(1)}, u32[]{:S(2)}, u32[]{:S(2)}) collective-permute-start(bf16[1024,256]{1,0:T(8,128)(2,1)} %get-tuple-element.434.refs_1_), channel_id=1, source_target_pairs={{0,1},{1,0},{2,3},{3,2},{4,5},{5,4},{6,7},{7,6},{8,9},{9,8},{10,11... | collective-permute-start | bytes 1572872 | tf_op jit(solution)/shard_map/ppermute | solution.py:576
  162.8 25.6 %collective-permute-start = (bf16[512,1024]{1,0:T(8,128)(2,1)}, bf16[512,1024]{1,0:T(8,128)(2,1)}, u32[]{:S(2)}, u32[]{:S(2)}) collective-permute-start(bf16[512,1024]{1,0:T(8,128)(2,1)} %get-tuple-element.256), channel_id=1, source_target_pairs={{0,1},{1,0},{2,3},{3,2},{4,5},{5,4},{6,7},{7,6},{8,9},{9,8},{10,11... | collective-permute-start | bytes 3145736 | tf_op jit(solution)/shard_map/cond/branch_1_fun/ppermute | solution.py:576
  198.8 7.2 %collective-permute-start.36 = (bf16[512,256]{1,0:T(8,128)(2,1)S(1)}, bf16[512,256]{1,0:T(8,128)(2,1)S(1)}, u32[]{:S(2)}, u32[]{:S(2)}) collective-permute-start(bf16[512,256]{1,0:T(8,128)(2,1)S(1)} %get-tuple-element.456), channel_id=1, source_target_pairs={{0,1},{1,0},{2,3},{3,2},{4,5},{5,4},{6,7},{7,6},{8,9},{9,8},{10,11... | collective-permute-start | bytes 786440 | tf_op jit(solution)/shard_map/ppermute | solution.py:576
  206.1 20.2 %collective-permute-start.2 = (bf16[512,256]{1,0:T(8,128)(2,1)S(1)}, bf16[512,256]{1,0:T(8,128)(2,1)S(1)}, u32[]{:S(2)}, u32[]{:S(2)}) collective-permute-start(bf16[512,256]{1,0:T(8,128)(2,1)S(1)} %get-tuple-element.268), channel_id=1, source_target_pairs={{0,1},{1,0},{2,3},{3,2},{4,5},{5,4},{6,7},{7,6},{8,9},{9,8},{10,11... | collective-permute-start | bytes 786440 | tf_op jit(solution)/shard_map/cond/branch_1_fun/ppermute | solution.py:576
  226.3 23.1 %collective-permute-start.3 = (bf16[512,1024]{1,0:T(8,128)(2,1)}, bf16[512,1024]{1,0:T(8,128)(2,1)S(1)}, u32[]{:S(2)}, u32[]{:S(2)}) collective-permute-start(bf16[512,1024]{1,0:T(8,128)(2,1)} %get-tuple-element.276), channel_id=1, source_target_pairs={{0,1},{1,0},{2,3},{3,2},{4,5},{5,4},{6,7},{7,6},{8,9},{9,8},{10,11... | collective-permute-start | bytes 3145736 | tf_op jit(solution)/shard_map/cond/branch_1_fun/ppermute | solution.py:576
  226.9 21.6 %collective-permute-start.4 = (bf16[512,768]{1,0:T(8,128)(2,1)}, bf16[512,768]{1,0:T(8,128)(2,1)S(1)}, u32[]{:S(2)}, u32[]{:S(2)}) collective-permute-start(bf16[512,768]{1,0:T(8,128)(2,1)} %get-tuple-element.278), channel_id=1, source_target_pairs={{0,2},{2,0},{4,6},{6,4},{8,10},{10,8},{12,14},{14,12},{16,18},{18,... | collective-permute-start | bytes 2359304 | tf_op jit(solution)/shard_map/cond/branch_1_fun/ppermute | solution.py:581
  250.0 9.9 %collective-permute-start.38 = (f32[6,512]{1,0:T(8,128)S(1)}, f32[6,512]{1,0:T(8,128)S(1)}, u32[]{:S(2)}, u32[]{:S(2)}) collective-permute-start(f32[6,512]{1,0:T(8,128)S(1)} %constant_dynamic-slice_fusion.1), channel_id=1, source_target_pairs={{0,1},{1,0},{2,3},{3,2},{4,5},{5,4},{6,7},{7,6},{8,9},{9,8},{10,11... | collective-permute-start | bytes 36872 | tf_op jit(solution)/shard_map/ppermute | solution.py:576
  264.6 37.5 %collective-permute-start.16 = (bf16[4,64,2048]{2,1,0:T(8,128)(2,1)S(1)}, bf16[4,64,2048]{2,1,0:T(8,128)(2,1)}, u32[]{:S(2)}, u32[]{:S(2)}) collective-permute-start(bf16[4,64,2048]{2,1,0:T(8,128)(2,1)S(1)} %dynamic-slice_bitcast_fusion), channel_id=1, source_target_pairs={{0,4},{2,6},{4,0},{6,2},{8,12},{10,14},{12,8},{14,10},{16,20},{18,... | collective-permute-start | bytes 3145736 | tf_op jit(solution)/shard_map/cond/branch_1_fun/ppermute | solution.py:581
  265.9 39.2 %collective-permute-start.15 = (bf16[512,1024]{1,0:T(8,128)(2,1)}, bf16[512,1024]{1,0:T(8,128)(2,1)}, u32[]{:S(2)}, u32[]{:S(2)}) collective-permute-start(bf16[512,1024]{1,0:T(8,128)(2,1)} %get-tuple-element.291), channel_id=1, source_target_pairs={{0,1},{1,0},{2,3},{3,2},{4,5},{5,4},{6,7},{7,6},{8,9},{9,8},{10,11... | collective-permute-start | bytes 3145736 | tf_op jit(solution)/shard_map/cond/branch_1_fun/ppermute | solution.py:576
  279.5 18.0 %collective-permute-start.10 = (bf16[8,3072]{1,0:T(8,128)(2,1)S(1)}, bf16[8,3072]{1,0:T(8,128)(2,1)}, u32[]{:S(2)}, u32[]{:S(2)}) collective-permute-start(bf16[8,3072]{1,0:T(8,128)(2,1)S(1)} %pad_maximum_fusion.4), channel_id=1, source_target_pairs={{0,4},{2,6},{4,0},{6,2},{8,12},{10,14},{12,8},{14,10},{16,20},{18,... | collective-permute-start | bytes 147464 | tf_op jit(solution)/shard_map/cond/branch_1_fun/cond/branch_1_fun/ppermute | solution.py:581
  285.3 11.6 %collective-permute-start.14 = (f32[4096]{0:T(1024)S(1)}, f32[4096]{0:T(1024)S(1)}, u32[]{:S(2)}, u32[]{:S(2)}) collective-permute-start(f32[4096]{0:T(1024)S(1)} %add.267), channel_id=1, source_target_pairs={{0,4},{2,6},{4,0},{6,2},{8,12},{10,14},{12,8},{14,10},{16,20},{18,... | collective-permute-start | bytes 49160 | tf_op jit(solution)/shard_map/cond/branch_1_fun/cond/branch_1_fun/ppermute | solution.py:581
  305.1 34.8 %collective-permute-start.21 = (bf16[512,1024]{1,0:T(8,128)(2,1)}, bf16[512,1024]{1,0:T(8,128)(2,1)}, u32[]{:S(2)}, u32[]{:S(2)}) collective-permute-start(bf16[512,1024]{1,0:T(8,128)(2,1)} %get-tuple-element.322), channel_id=1, source_target_pairs={{0,1},{1,0},{2,3},{3,2},{4,5},{5,4},{6,7},{7,6},{8,9},{9,8},{10,11... | collective-permute-start | bytes 3145736 | tf_op jit(solution)/shard_map/cond/branch_1_fun/ppermute | solution.py:576
  306.0 31.8 %collective-permute-start.22 = (bf16[64,2048]{1,0:T(8,128)(2,1)}, bf16[64,2048]{1,0:T(8,128)(2,1)S(1)}, u32[]{:S(2)}, u32[]{:S(2)}) collective-permute-start(bf16[64,2048]{1,0:T(8,128)(2,1)} %get-tuple-element.325), channel_id=1, source_target_pairs={{0,8},{2,10},{4,12},{6,14},{8,16},{10,18},{12,20},{14,22},{16,24},... | collective-permute-start | bytes 786440 | tf_op jit(solution)/shard_map/cond/branch_1_fun/ppermute | solution.py:662
  307.4 30.4 %collective-permute-start.23 = (bf16[64,2048]{1,0:T(8,128)(2,1)}, bf16[64,2048]{1,0:T(8,128)(2,1)}, u32[]{:S(2)}, u32[]{:S(2)}) collective-permute-start(bf16[64,2048]{1,0:T(8,128)(2,1)} %get-tuple-element.326), channel_id=1, source_target_pairs={{0,16},{2,18},{4,20},{6,22},{8,24},{10,26},{12,28},{14,30},{16,0},... | collective-permute-start | bytes 786440 | tf_op jit(solution)/shard_map/cond/branch_1_fun/ppermute | solution.py:662
  308.1 29.7 %collective-permute-start.24 = (bf16[64,2048]{1,0:T(8,128)(2,1)}, bf16[64,2048]{1,0:T(8,128)(2,1)}, u32[]{:S(2)}, u32[]{:S(2)}) collective-permute-start(bf16[64,2048]{1,0:T(8,128)(2,1)} %get-tuple-element.327), channel_id=1, source_target_pairs={{0,24},{2,26},{4,28},{6,30},{8,0},{10,2},{12,4},{14,6},{16,8},{18,... | collective-permute-start | bytes 786440 | tf_op jit(solution)/shard_map/cond/branch_1_fun/ppermute | solution.py:662
  317.8 11.3 %collective-permute-start.19 = (f32[4,16,64]{2,1,0:T(8,128)S(1)}, f32[4,16,64]{2,1,0:T(8,128)S(1)}, u32[]{:S(2)}, u32[]{:S(2)}) collective-permute-start(f32[4,16,64]{2,1,0:T(8,128)S(1)} %pad_maximum_fusion.8), channel_id=1, source_target_pairs={{0,8},{2,10},{4,12},{6,14},{8,0},{10,2},{12,4},{14,6},{16,24},{18,... | collective-permute-start | bytes 49160 | tf_op jit(solution)/shard_map/cond/branch_1_fun/cond/branch_1_fun/ppermute | solution.py:581
  (59 other events, 517.1 us)
Sparse Core Ops, SparseCore 0:
  10.8 54.4 all-gather.2
  68.1 73.4 all-gather.4
  188.6 107.6 reduce-scatter.1

commit v4 on v3

--- a/solution.py
+++ b/solution.py
@@ -272,7 +272,7 @@
     return value.astype(f32).T.astype(bf16)
 
 
-def mlp_grads_kernel(own_rows, half, h_ref, dm_ref, dpre_ref, act_ref, w2_ref, cot_ref, grad_ref, own_ref, rest_ref, sum_ref, h_t, dm_t, acc_ref):
+def mlp_grads_kernel(own_rows, half, h_ref, dm_ref, dpre_ref, act_ref, w2_ref, cot_ref, bias_ref, grad_ref, own_ref, rest_ref, sum_ref, h_t, dm_t, acc_ref):
     j = pl.program_id(0)
 
     @pl.when(j == 0)
@@ -294,10 +294,12 @@
     def _():
         own_ref[...] = acc_ref[:own_rows, :]
         rest_ref[...] = acc_ref[own_rows:, :].astype(bf16)
-        sum_ref[...] = jnp.sum(acc_ref[...] * cot_ref[...].astype(f32), 0, keepdims=True)
-
-
-def mlp_weight_grads(hidden_two, grad_m, grad_pre, activ, mlp_w, cot_all, own_rows):
+        cot = cot_ref[...].astype(f32)
+        total = jnp.sum(acc_ref[...] * cot, 0, keepdims=True)
+        sum_ref[...] = total + bias_ref[...] * jnp.sum(cot[:own_rows], 0, keepdims=True)
+
+
+def mlp_weight_grads(hidden_two, grad_m, grad_pre, activ, mlp_w, cot_all, bias, own_rows):
     rows, width = hidden_two.shape
     hidden = mlp_w.shape[1] // 2
     block = min(512, hidden)
@@ -312,6 +314,7 @@
             pl.BlockSpec((rows, block), lambda j: (0, jnp.maximum(j - half, 0))),
             pl.BlockSpec((width, block), lambda j: (0, half + jnp.maximum(j - half, 0))),
             full_spec((rows, width)),
+            full_spec((1, width)),
         ],
         out_specs=[
             pl.BlockSpec((width, block), lambda j: (0, j)),
@@ -337,7 +340,7 @@
             transcendentals=0,
         ),
         name="mlp_weight_grads",
-    )(hidden_two, grad_m, grad_pre, activ, mlp_w, cot_all)
+    )(hidden_two, grad_m, grad_pre, activ, mlp_w, cot_all, bias)
 
 
 def middle_kernel(own_steps, pieces, *refs):
@@ -431,6 +434,7 @@
             jnp.sum(grad_mid * a_ref[...], 0, keepdims=True),
             jnp.sum(grad_h, 0, keepdims=True),
             jnp.sum(grad_h * normed, 0, keepdims=True),
+            jnp.sum(grad_a.astype(f32), 0, keepdims=True),
         ]
     )
     i = pl.program_id(0)
@@ -460,12 +464,12 @@
         grid=(rows // block,),
         in_specs=[row_spec] * (len(arrived) + 4)
         + [one_spec, one_spec, full_spec(modul.shape), full_spec((width, width))],
-        out_specs=[row_spec, row_spec, full_spec((3, width))]
+        out_specs=[row_spec, row_spec, full_spec((4, width))]
         + [pl.BlockSpec((block, columns), lambda i: (i, 0))] * pieces,
         out_shape=[
             jax.ShapeDtypeStruct((rows, width), f32),
             jax.ShapeDtypeStruct((rows, width), bf16),
-            jax.ShapeDtypeStruct((3, width), f32),
+            jax.ShapeDtypeStruct((4, width), f32),
         ]
         + [jax.ShapeDtypeStruct((rows, columns), bf16)] * pieces,
         compiler_params=pltpu.CompilerParams(vmem_limit_bytes=40 * MIB),
@@ -796,11 +800,10 @@
         return arrived, mlp_weight_grads(*args, row_count)
 
     arrived_two, (mlp_grads, own_mlp, rest_mlp, mlp_sum) = together(
-        run, weight_part, rest_two, hidden_two, grad_m, grad_pre, activ, mlp_w, cot_all
+        run, weight_part, rest_two, hidden_two, grad_m, grad_pre, activ, mlp_w, cot_all, fc2_bias
     )
     mlp_grads = lax.psum_scatter(mlp_grads, "dp", scatter_dimension=0, tiled=True)
 
-    grad_out = cotangent.astype(f32)
     grad_mid, grad_a, sums_two, *grad_pieces = middle_back(
         own_two, arrived_two, cotangent, middle, branch_attn, mean_two, rstd_two, modul, proj_w, group_width
     )
@@ -840,12 +843,13 @@
     )
     dqkv = dqkv + [grads]
 
-    grad_mod = jnp.concatenate([sums_one, sums_two, mlp_sum + fc2_bias * row_sum(grad_out)[None]])
+    grad_mod = jnp.concatenate([sums_one, sums_two[:3], mlp_sum, sums_two[3:]])
     grad_mod_own = cols_of(grad_mod, tensor_pos)
     for s in range(1, tensor_size):
         owner = lax.rem(tensor_pos - s + tensor_size, tensor_size)
         grad_mod_own = grad_mod_own + shift(cols_of(grad_mod, owner), "tensor", -s)
-    grad_mod_own = grad_mod_own.astype(bf16).reshape(6 * local_width)
+    grad_a_sum = grad_mod_own[6]
+    grad_mod_own = grad_mod_own[:6].astype(bf16).reshape(6 * local_width)
     late = [
         jnp.concatenate(pair, 1)
         for pair in zip(
@@ -857,7 +861,7 @@
         [row_sum(d[0].astype(f32)) for d in dqkv]
         + [row_sum(d[2].astype(f32)) for d in dqkv]
         + [
-            cols_of(row_sum(grad_a_rows.astype(f32)), tensor_pos),
+            grad_a_sum,
             fc1_sum.reshape(-1),
             cols_of(dm_sum[0], tensor_pos),
         ]

time: 363 us -> 362 us (level)
  transfers between devices with their start and end apart: 43 -> 43, of which waited for: 24 -> 25; matrix products, arithmetic and copies ran while one was open for 21% -> 20% of each run, Pallas kernels for 28% -> 28%
where the time goes in v4:
time: 362 us; the launch traced here: 355 us
  Pallas kernels  119 us (33%)
  waiting for transfers between devices  86 us (24%)
  starting transfers between devices  48.4 us (13%)
  other arithmetic  40.8 us (11%)
  local copies, waits for them, and re-layouts  31.9 us (9%)
  between operations  14.6 us (4%)
  matrix products  13.7 us (4%)
    ppermute x14, waiting for transfers between devices, shift(): return lax.ppermute(x, axis, [(i, (i + step) % size) for i in range(size)])  45.6 us
    ppermute x23, waiting for transfers between devices, xor_step(): return lax.ppermute(x, axis, [(i, i ^ bit) for i in range(size)])  40.3 us
    ppermute x23, starting transfers between devices, xor_step(): return lax.ppermute(x, axis, [(i, i ^ bit) for i in range(size)])  26.8 us
    pallas_call x2, Pallas kernels, attend_back(): pl.pallas_call(partial(attend_back_kernel, 256), grid=(pairs,), in_specs=...  26.6 us
    pallas_call x1, Pallas kernels, mlp_weight_grads(): pl.pallas_call(partial(mlp_grads_kernel, own_rows, half), grid=(2 * half,...  22.9 us
    pallas_call x1, Pallas kernels, mlp_both(): pl.pallas_call(partial(mlp_kernel, own_rows, rows), grid=(steps,), in_spe...  19.8 us
    ppermute x14, starting transfers between devices, shift(): return lax.ppermute(x, axis, [(i, (i + step) % size) for i in range(size)])  16.7 us
    pallas_call x2, Pallas kernels, attend(): pl.pallas_call(partial(attend_kernel, min(512, rows)), grid=(pairs,), in_...  16.6 us
  transfers between devices with their start and end apart: 43, of which 25 were waited for; matrix products, arithmetic and copies ran while one was open for 20% of the time, Pallas kernels for 28%

profile of v4, /device:TPU:0, one launch (start us, length us, event | category | flops | bytes accessed | tf_op | source)
XLA Modules:
  0.0 355.2 jit_solution(9795707760967183199)
XLA Ops:
  46.5 11.3 %collective-permute-done.33 = f32[8,512]{1,0:T(8,128)S(1)} collective-permute-done((f32[8,512]{1,0:T(8,128)S(1)}, f32[8,512]{1,0:T(8,128)S(1)}, u32[]{:S(2)}, u32[]{:S(2)}) %collective-permute-start.33) | collective-permute-done | bytes 16416 | tf_op jit(solution)/shard_map/ppermute | solution.py:580
  59.0 21.9 %conditional.10 = (bf16[512,1024]{1,0:T(8,128)(2,1)}, bf16[1024,1024]{1,0:T(8,128)(2,1)}) conditional(s32[]{:T(128)} %convert_element_type.136, () %tuple.109, (bf16[512,1024]{1,0:T(8,128)(2,1)S(1)}, bf16[1024,1024]{1,0:T(8,128)(2,1)}, f32[1,1024]{1,0:T(1,128)S(1)}, f32[8,1024]{1,0:T(8,128)S(1)}) %tuple.175), branch_computations={%region_0.1_spmd, %region_1.4_spmd} | conditional | flops 12584960 | bytes 12644408 | solution.py:652
  68.4 12.4 %collective-permute-done.1 = bf16[512,1024]{1,0:T(8,128)(2,1)} collective-permute-done((bf16[512,1024]{1,0:T(8,128)(2,1)S(1)}, bf16[512,1024]{1,0:T(8,128)(2,1)}, u32[]{:S(2)}, u32[]{:S(2)}) %collective-permute-start.1) | collective-permute-done | bytes 1048608 | tf_op jit(solution)/shard_map/cond/branch_1_fun/ppermute | solution.py:580
  82.2 23.2 %conditional.11 = (bf16[1024,512]{1,0:T(8,128)(2,1)}, bf16[1024,768]{1,0:T(8,128)(2,1)}, bf16[1024,256]{1,0:T(8,128)(2,1)}, f32[2,2,1024]{2,1,0:T(2,128)S(1)}) conditional(s32[]{:T(128)} %convert_element_type.136, () %tuple.108, (bf16[1024,512]{1,0:T(8,128)(2,1)S(1)}, bf16[1024,2048]{1,0:T(8,128)(2,1)}, bf16[1024,1024]{1,0:T(8,128)(2,1)}, ...), branch_computations={%region_4.5_spmd, %region_5.6_spmd} | conditional | flops 5907154432 | bytes 11548748 | solution.py:652
  88.8 8.4 %attend.2 = (bf16[1024,256]{1,0:T(8,128)(2,1)}, f32[2,2,1024]{2,1,0:T(2,128)S(1)}) custom-call(bf16[1024,768]{1,0:T(8,128)(2,1)} %add_convert_fusion.q_ref.k_ref.v_ref, bf16[1024,768]{1,0:T(8,128)(2,1)} %add_convert_fusion.q_ref.k_ref.v_ref, bf16[1024,768]{1,0:T(8,128)(2,1)} %add_convert_fusion.q_ref.k_ref.v_ref), custom_call_target="tpu_custom_call" | custom-call | flops 4294967296 | bytes 2097152 | tf_op jit(solution)/shard_map/cond/branch_1_fun/attend/pallas_call | solution.py:82
  97.2 8.1 %collective-permute-done.5 = bf16[1024,512]{1,0:T(8,128)(2,1)} collective-permute-done((bf16[1024,512]{1,0:T(8,128)(2,1)S(1)}, bf16[1024,512]{1,0:T(8,128)(2,1)}, u32[]{:S(2)}, u32[]{:S(2)}) %collective-permute-start.5) | collective-permute-done | bytes 1048608 | tf_op jit(solution)/shard_map/cond/branch_1_fun/ppermute | solution.py:580
  105.3 15.8 %conditional.12 = (bf16[1024,256]{1,0:T(8,128)(2,1)}, bf16[1024,768]{1,0:T(8,128)(2,1)}, bf16[1024,256]{1,0:T(8,128)(2,1)}, f32[2,2,1024]{2,1,0:T(2,128)S(1)}, bf16[1,1024,256]{2,1,0:T(8,128)(2,1)S(1)}) conditional(s32[]{:T(128)} %convert_element_type.136, () %tuple.112, (bf16[1024,256]{1,0:T(8,128)(2,1)}, bf16[1024,2048]{1,0:T(8,128)(2,1)}, ...), branch_computations={%region_6.7_spmd, %region_7.8_spmd} | conditional | flops 5907154432 | bytes 10500180 | solution.py:652
  111.9 8.1 %attend.3 = (bf16[1024,256]{1,0:T(8,128)(2,1)}, f32[2,2,1024]{2,1,0:T(2,128)S(1)}) custom-call(bf16[1024,768]{1,0:T(8,128)(2,1)} %add_convert_fusion.1.q_ref.k_ref.v_ref, bf16[1024,768]{1,0:T(8,128)(2,1)} %add_convert_fusion.1.q_ref.k_ref.v_ref, bf16[1024,768]{1,0:T(8,128)(2,1)} %add_convert_fusion.1.q_ref.k_ref.v_ref), custom_call_target="tpu_custom_call" | custom-call | flops 4294967296 | bytes 2097152 | tf_op jit(solution)/shard_map/cond/branch_1_fun/attend/pallas_call | solution.py:82
  131.3 9.0 %middle_part.1 = (bf16[1024,1024]{1,0:T(8,128)(2,1)}, bf16[1024,1024]{1,0:T(8,128)(2,1)}, f32[1,1024]{1,0:T(1,128)S(1)}, f32[512,1024]{1,0:T(8,128)S(1)}, f32[51...) custom-call(bf16[1024,256]{1,0:T(8,128)(2,1)} %get-tuple-element.436.refs_0_, ...), custom_call_target="tpu_custom_call" | custom-call | flops 2147483648 | bytes 16777216 | tf_op jit(solution)/shard_map/middle_part/pallas_call | solution.py:392
  141.6 19.8 %mlp_both.1 = (bf16[1024,2048]{1,0:T(8,128)(2,1)}, bf16[1024,2048]{1,0:T(8,128)(2,1)}, f32[1,2048]{1,0:T(1,128)S(1)}, f32[512,1024]{1,0:T(8,128)S(1)}, bf16[512,1024]{1,0:T(8,128)(2,1)}) custom-call(bf16[1024,1024]{1,0:T(8,128)(2,1)} %get-tuple-element.441.h_ref, bf16[1024,1024]{1,0:T(8,128)(2,1)} %get-tuple-element.442.dm_ref, ...), custom_call_target="tpu_custom_call" | custom-call | flops 12884901888 | bytes 29360128 | tf_op jit(solution)/shard_map/mlp_both/pallas_call | solution.py:236
  162.8 25.5 %conditional.13 = (bf16[512,1024]{1,0:T(8,128)(2,1)}, bf16[1024,4096]{1,0:T(8,128)(2,1)}, f32[512,1024]{1,0:T(8,128)}, bf16[512,1024]{1,0:T(8,128)(2,1)}, f32[1,1024]{1,0:T(1,128)S(1)}) conditional(s32[]{:T(128)} %convert_element_type.136, () %tuple.107, (bf16[512,1024]{1,0:T(8,128)(2,1)}, bf16[1024,1024]{1,0:T(8,128)(2,1)}, ...), branch_computations={%region_8.9_spmd, %region_9.10_spmd} | conditional | flops 12884901888 | bytes 33554512 | solution.py:652
  164.2 22.9 %mlp_weight_grads.1 = (bf16[1024,4096]{1,0:T(8,128)(2,1)}, f32[512,1024]{1,0:T(8,128)}, bf16[512,1024]{1,0:T(8,128)(2,1)}, f32[1,1024]{1,0:T(1,128)S(1)}) custom-call(bf16[1024,1024]{1,0:T(8,128)(2,1)} %get-tuple-element.259.h_ref, bf16[1024,1024]{1,0:T(8,128)(2,1)} %get-tuple-element.260.dm_ref, bf16[1024,2048]{1,0:T(8,128)(2,1)} %get-tuple-element.261.dpre_ref, ...), custom_call_target="tpu_custom_call" | custom-call | flops 12884901888 | bytes 29360128 | tf_op jit(solution)/shard_map/cond/branch_1_fun/mlp_weight_grads/pallas_call | solution.py:307
  191.6 5.7 %middle_back.1 = (f32[512,1024]{1,0:T(8,128)}, bf16[512,1024]{1,0:T(8,128)(2,1)}, f32[4,1024]{1,0:T(4,128)S(1)}, bf16[512,256]{1,0:T(8,128)(2,1)S(1)}, bf16[512,...) custom-call(f32[512,1024]{1,0:T(8,128)S(1)} %copy-done.3, ...), custom_call_target="tpu_custom_call" | custom-call | flops 1073741824 | bytes 14680064 | tf_op jit(solution)/shard_map/middle_back/pallas_call | solution.py:462
  199.0 5.7 %collective-permute-done.36 = bf16[512,256]{1,0:T(8,128)(2,1)S(1)} collective-permute-done((bf16[512,256]{1,0:T(8,128)(2,1)S(1)}, bf16[512,256]{1,0:T(8,128)(2,1)S(1)}, u32[]{:S(2)}, u32[]{:S(2)}) %collective-permute-start.36) | collective-permute-done | bytes 262176 | tf_op jit(solution)/shard_map/ppermute | solution.py:580
  204.8 19.2 %conditional.14 = (bf16[1024,256]{1,0:T(8,128)(2,1)S(1)}, bf16[3,1024,256]{2,1,0:T(8,128)(2,1)}, bf16[512,768]{1,0:T(8,128)(2,1)S(1)}, bf16[512,768]{1,0:T(8,128)(2,1)S(1)}) conditional(s32[]{:T(128)} %convert_element_type.136, () %tuple.117, (bf16[512,256]{1,0:T(8,128)(2,1)}, bf16[512,256]{1,0:T(8,128)(2,1)}, bf16[1024,768]{1,0:T(8,128)(2,1)}, ...), branch_computations={%region_10.11_spmd, %region_11.12_spmd} | conditional | flops 12349079552 | bytes 12058724 | solution.py:652
  206.4 13.5 %attend_back.2.refs_0_ = bf16[3,1024,256]{2,1,0:T(8,128)(2,1)} custom-call(bf16[1024,768]{1,0:T(8,128)(2,1)} %get-tuple-element.272.q_ref.k_ref.v_ref, bf16[1024,768]{1,0:T(8,128)(2,1)} %get-tuple-element.272.q_ref.k_ref.v_ref, bf16[1024,768]{1,0:T(8,128)(2,1)} %get-tuple-element.272.q_ref.k_ref.v_ref, bf16[1024,256]{1,0:T(8,128)(2,1)S(1)} %get-tuple-element.273.do_ref, ...), custom_call_target="tpu_custom_call" | custom-call | flops 10737418240 | bytes 3670016 | tf_op jit(solution)/shard_map/cond/branch_1_fun/attend_back/pallas_call | solution.py:153
  224.0 24.1 %conditional.15 = (bf16[1024,1024]{1,0:T(8,128)(2,1)S(1)}, bf16[512,768]{1,0:T(8,128)(2,1)S(1)}, bf16[3,1024,256]{2,1,0:T(8,128)(2,1)S(1)}, f32[512,1024]{1,0:T(...) conditional(s32[]{:T(128)} %convert_element_type.136, () %tuple.116, (bf16[512,1024]{1,0:T(8,128)(2,1)}, ...), branch_computations={%region_12.13_spmd, %region_13.14_spmd} | conditional | flops 13964410880 | bytes 63701260 | solution.py:652
  224.8 13.1 %attend_back.3.refs_1_ = bf16[3,1024,256]{2,1,0:T(8,128)(2,1)S(1)} custom-call(bf16[1024,768]{1,0:T(8,128)(2,1)} %get-tuple-element.282.q_ref.k_ref.v_ref, bf16[1024,768]{1,0:T(8,128)(2,1)} %get-tuple-element.282.q_ref.k_ref.v_ref, bf16[1024,768]{1,0:T(8,128)(2,1)} %get-tuple-element.282.q_ref.k_ref.v_ref, bf16[1024,256]{1,0:T(8,128)(2,1)} %copy-done.19, ...), custom_call_target="tpu_custom_call" | custom-call | flops 10737418240 | bytes 3670016 | tf_op jit(solution)/shard_map/cond/branch_1_fun/attend_back/pallas_call | solution.py:153
  237.9 8.2 %hidden_back.1 = (f32[512,1024]{1,0:T(8,128)}, bf16[512,1024]{1,0:T(8,128)(2,1)}, f32[2,1024]{1,0:T(2,128)S(1)}) custom-call(bf16[1024,1024]{1,0:T(8,128)(2,1)} %get-tuple-element.285.x_ref, bf16[1024,2048]{1,0:T(8,128)(2,1)S(1)} %copy-done.22, bf16[3,1024,256]{2,1,0:T(8,128)(2,1)} %get-tuple-element.287.refs_0_, bf16[3,1024,256]{2,1,0:T(8,128)(2,1)S(1)} %attend_back.3.refs_1_), custom_call_target="tpu_custom_call" | custom-call | flops 3221225472 | bytes 10485760 | tf_op jit(solution)/shard_map/cond/branch_1_fun/hidden_back/pallas_call | solution.py:553
  261.5 42.7 %conditional.16 = (bf16[512,1024]{1,0:T(8,128)(2,1)}, bf16[64,2048]{1,0:T(8,128)(2,1)}, bf16[64,2048]{1,0:T(8,128)(2,1)}, bf16[64,2048]{1,0:T(8,128)(2,1)}, bf16...) conditional(s32[]{:T(128)} %convert_element_type.136, () %tuple.115, ...), branch_computations={%region_18.19_spmd, %region_19.22_spmd} | conditional | flops 8699981 | bytes 17683888 | solution.py:652
  264.9 36.4 %conditional = (bf16[16,3072]{1,0:T(8,128)(2,1)}, f32[16,64]{1,0:T(8,128)}, f32[4096]{0:T(1024)}) conditional(s32[]{:T(128)} %convert_element_type.110, () %tuple.78, (bf16[7,512]{1,0:T(8,128)(2,1)S(1)}, bf16[64,3072]{1,0:T(8,128)(2,1)S(1)}, f32[4096]{0:T(1024)}) %tuple.180), branch_computations={%region_20.20_spmd, %region_21.21_spmd} | conditional | flops 6602752 | bytes 1888684 | solution.py:652
  285.4 10.7 %collective-permute-done.14 = f32[4096]{0:T(1024)S(1)} collective-permute-done((f32[4096]{0:T(1024)S(1)}, f32[4096]{0:T(1024)S(1)}, u32[]{:S(2)}, u32[]{:S(2)}) %collective-permute-start.14) | collective-permute-done | bytes 16416 | tf_op jit(solution)/shard_map/cond/branch_1_fun/cond/branch_1_fun/ppermute | solution.py:585
  304.2 38.7 %conditional.17 = (bf16[512,1024]{1,0:T(8,128)(2,1)}, f32[64,2048]{1,0:T(8,128)}, bf16[512,1024]{1,0:T(8,128)(2,1)}, f32[1,1024]{1,0:T(1,128)}, f32[6,32]{1,0:T(...) conditional(s32[]{:T(128)} %convert_element_type.136, ...), branch_computations={%region_23.24_spmd, %region_24.0_spmd} | conditional | flops 23052948 | bytes 68689384 | solution.py:652
  310.4 24.8 %conditional.1 = (bf16[512,1024]{1,0:T(8,128)(2,1)}, f32[1,1024]{1,0:T(1,128)}, f32[64,6,512]{2,1,0:T(8,128)S(1)}, f32[6,32]{1,0:T(8,128)}, f32[2,32]{1,0:T(2,12...) conditional(s32[]{:T(128)} %convert_element_type.122, () %tuple.85, ...), branch_computations={%region_25.25_spmd, %region_26.32_spmd} | conditional | flops 18989716 | bytes 43490388 | solution.py:652
  (308 shorter events, 183.1 us)
Async XLA Ops:
  7.3 73.6 %all-gather.3.cloned.1.call-start = ((), (), s32[]{:S(2)}) async-start(), calls=%async_computation.1 | async-start | bytes 4456448 | tf_op jit(solution)/shard_map/all_gather | solution.py:717
  9.9 131.7 %all-gather.5.cloned.1.call-start = ((), (), s32[]{:S(2)}) async-start(), calls=%async_computation.2 | async-start | bytes 8912896 | tf_op jit(solution)/shard_map/all_gather | solution.py:718
  11.9 292.4 %reduce-scatter.2.cloned.1.call-start = ((), (), s32[]{:S(2)}) async-start(), calls=%async_computation.3 | async-start | bytes 8912896 | tf_op jit(solution)/shard_map/reduce_scatter | solution.py:805
  35.2 22.7 %collective-permute-start.34 = (bf16[512,1024]{1,0:T(8,128)(2,1)}, bf16[512,1024]{1,0:T(8,128)(2,1)S(1)}, u32[]{:S(2)}, u32[]{:S(2)}) collective-permute-start(bf16[512,1024]{1,0:T(8,128)(2,1)} %param.33), channel_id=1, source_target_pairs={{0,1},{1,0},{2,3},{3,2},{4,5},{5,4},{6,7},{7,6},{8,9},{9,8},{10,11... | collective-permute-start | bytes 3145736 | tf_op jit(solution)/shard_map/ppermute | solution.py:580
  44.7 13.1 %collective-permute-start.33 = (f32[8,512]{1,0:T(8,128)S(1)}, f32[8,512]{1,0:T(8,128)S(1)}, u32[]{:S(2)}, u32[]{:S(2)}) collective-permute-start(f32[8,512]{1,0:T(8,128)S(1)} %reshape_squeeze.3), channel_id=1, source_target_pairs={{0,1},{1,0},{2,3},{3,2},{4,5},{5,4},{6,7},{7,6},{8,9},{9,8},{10,11... | collective-permute-start | bytes 49160 | tf_op jit(solution)/shard_map/ppermute | solution.py:580
  59.0 21.9 %collective-permute-start.1 = (bf16[512,1024]{1,0:T(8,128)(2,1)S(1)}, bf16[512,1024]{1,0:T(8,128)(2,1)}, u32[]{:S(2)}, u32[]{:S(2)}) collective-permute-start(bf16[512,1024]{1,0:T(8,128)(2,1)S(1)} %get-tuple-element.242), channel_id=1, source_target_pairs={{0,1},{1,0},{2,3},{3,2},{4,5},{5,4},{6,7},{7,6},{8,9},{9,8},{10,11... | collective-permute-start | bytes 3145736 | tf_op jit(solution)/shard_map/cond/branch_1_fun/ppermute | solution.py:580
  82.2 23.2 %collective-permute-start.5 = (bf16[1024,512]{1,0:T(8,128)(2,1)S(1)}, bf16[1024,512]{1,0:T(8,128)(2,1)}, u32[]{:S(2)}, u32[]{:S(2)}) collective-permute-start(bf16[1024,512]{1,0:T(8,128)(2,1)S(1)} %get-tuple-element.246), channel_id=1, source_target_pairs={{0,1},{1,0},{2,3},{3,2},{4,5},{5,4},{6,7},{7,6},{8,9},{9,8},{10,11... | collective-permute-start | bytes 3145736 | tf_op jit(solution)/shard_map/cond/branch_1_fun/ppermute | solution.py:580
  105.3 15.8 %collective-permute-start.6 = (bf16[1024,256]{1,0:T(8,128)(2,1)}, bf16[1024,256]{1,0:T(8,128)(2,1)}, u32[]{:S(2)}, u32[]{:S(2)}) collective-permute-start(bf16[1024,256]{1,0:T(8,128)(2,1)} %get-tuple-element.252), channel_id=1, source_target_pairs={{0,1},{1,0},{2,3},{3,2},{4,5},{5,4},{6,7},{7,6},{8,9},{9,8},{10,11... | collective-permute-start | bytes 1572872 | tf_op jit(solution)/shard_map/cond/branch_1_fun/ppermute | solution.py:580
  121.9 9.4 %collective-permute-start.35 = (bf16[1024,256]{1,0:T(8,128)(2,1)}, bf16[1024,256]{1,0:T(8,128)(2,1)S(1)}, u32[]{:S(2)}, u32[]{:S(2)}) collective-permute-start(bf16[1024,256]{1,0:T(8,128)(2,1)} %get-tuple-element.437.refs_1_), channel_id=1, source_target_pairs={{0,1},{1,0},{2,3},{3,2},{4,5},{5,4},{6,7},{7,6},{8,9},{9,8},{10,11... | collective-permute-start | bytes 1572872 | tf_op jit(solution)/shard_map/ppermute | solution.py:580
  162.8 25.5 %collective-permute-start = (bf16[512,1024]{1,0:T(8,128)(2,1)}, bf16[512,1024]{1,0:T(8,128)(2,1)}, u32[]{:S(2)}, u32[]{:S(2)}) collective-permute-start(bf16[512,1024]{1,0:T(8,128)(2,1)} %get-tuple-element.258), channel_id=1, source_target_pairs={{0,1},{1,0},{2,3},{3,2},{4,5},{5,4},{6,7},{7,6},{8,9},{9,8},{10,11... | collective-permute-start | bytes 3145736 | tf_op jit(solution)/shard_map/cond/branch_1_fun/ppermute | solution.py:580
  197.3 7.5 %collective-permute-start.36 = (bf16[512,256]{1,0:T(8,128)(2,1)S(1)}, bf16[512,256]{1,0:T(8,128)(2,1)S(1)}, u32[]{:S(2)}, u32[]{:S(2)}) collective-permute-start(bf16[512,256]{1,0:T(8,128)(2,1)S(1)} %get-tuple-element.459), channel_id=1, source_target_pairs={{0,1},{1,0},{2,3},{3,2},{4,5},{5,4},{6,7},{7,6},{8,9},{9,8},{10,11... | collective-permute-start | bytes 786440 | tf_op jit(solution)/shard_map/ppermute | solution.py:580
  204.8 19.2 %collective-permute-start.2 = (bf16[512,256]{1,0:T(8,128)(2,1)}, bf16[512,256]{1,0:T(8,128)(2,1)S(1)}, u32[]{:S(2)}, u32[]{:S(2)}) collective-permute-start(bf16[512,256]{1,0:T(8,128)(2,1)} %get-tuple-element.271), channel_id=1, source_target_pairs={{0,1},{1,0},{2,3},{3,2},{4,5},{5,4},{6,7},{7,6},{8,9},{9,8},{10,11... | collective-permute-start | bytes 786440 | tf_op jit(solution)/shard_map/cond/branch_1_fun/ppermute | solution.py:580
  224.0 23.9 %collective-permute-start.3 = (bf16[512,1024]{1,0:T(8,128)(2,1)}, bf16[512,1024]{1,0:T(8,128)(2,1)S(1)}, u32[]{:S(2)}, u32[]{:S(2)}) collective-permute-start(bf16[512,1024]{1,0:T(8,128)(2,1)} %get-tuple-element.279), channel_id=1, source_target_pairs={{0,1},{1,0},{2,3},{3,2},{4,5},{5,4},{6,7},{7,6},{8,9},{9,8},{10,11... | collective-permute-start | bytes 3145736 | tf_op jit(solution)/shard_map/cond/branch_1_fun/ppermute | solution.py:580
  224.8 21.4 %collective-permute-start.4 = (bf16[512,768]{1,0:T(8,128)(2,1)S(1)}, bf16[512,768]{1,0:T(8,128)(2,1)S(1)}, u32[]{:S(2)}, u32[]{:S(2)}) collective-permute-start(bf16[512,768]{1,0:T(8,128)(2,1)S(1)} %get-tuple-element.281), channel_id=1, source_target_pairs={{0,2},{2,0},{4,6},{6,4},{8,10},{10,8},{12,14},{14,12},{16,18},{18,... | collective-permute-start | bytes 2359304 | tf_op jit(solution)/shard_map/cond/branch_1_fun/ppermute | solution.py:585
  248.2 10.4 %collective-permute-start.38 = (f32[7,512]{1,0:T(8,128)S(1)}, f32[7,512]{1,0:T(8,128)S(1)}, u32[]{:S(2)}, u32[]{:S(2)}) collective-permute-start(f32[7,512]{1,0:T(8,128)S(1)} %constant_dynamic-slice_fusion.1), channel_id=1, source_target_pairs={{0,1},{1,0},{2,3},{3,2},{4,5},{5,4},{6,7},{7,6},{8,9},{9,8},{10,11... | collective-permute-start | bytes 43016 | tf_op jit(solution)/shard_map/ppermute | solution.py:580
  263.5 37.8 %collective-permute-start.16 = (bf16[4,64,2048]{2,1,0:T(8,128)(2,1)S(1)}, bf16[4,64,2048]{2,1,0:T(8,128)(2,1)}, u32[]{:S(2)}, u32[]{:S(2)}) collective-permute-start(bf16[4,64,2048]{2,1,0:T(8,128)(2,1)S(1)} %dynamic-slice_bitcast_fusion), channel_id=1, source_target_pairs={{0,4},{2,6},{4,0},{6,2},{8,12},{10,14},{12,8},{14,10},{16,20},{18,... | collective-permute-start | bytes 3145736 | tf_op jit(solution)/shard_map/cond/branch_1_fun/ppermute | solution.py:585
  263.9 40.3 %collective-permute-start.15 = (bf16[512,1024]{1,0:T(8,128)(2,1)}, bf16[512,1024]{1,0:T(8,128)(2,1)}, u32[]{:S(2)}, u32[]{:S(2)}) collective-permute-start(bf16[512,1024]{1,0:T(8,128)(2,1)} %get-tuple-element.294), channel_id=1, source_target_pairs={{0,1},{1,0},{2,3},{3,2},{4,5},{5,4},{6,7},{7,6},{8,9},{9,8},{10,11... | collective-permute-start | bytes 3145736 | tf_op jit(solution)/shard_map/cond/branch_1_fun/ppermute | solution.py:580
  275.4 21.3 %collective-permute-start.10 = (bf16[8,3072]{1,0:T(8,128)(2,1)S(1)}, bf16[8,3072]{1,0:T(8,128)(2,1)}, u32[]{:S(2)}, u32[]{:S(2)}) collective-permute-start(bf16[8,3072]{1,0:T(8,128)(2,1)S(1)} %pad_maximum_fusion.4), channel_id=1, source_target_pairs={{0,4},{2,6},{4,0},{6,2},{8,12},{10,14},{12,8},{14,10},{16,20},{18,... | collective-permute-start | bytes 147464 | tf_op jit(solution)/shard_map/cond/branch_1_fun/cond/branch_1_fun/ppermute | solution.py:585
  283.8 12.3 %collective-permute-start.14 = (f32[4096]{0:T(1024)S(1)}, f32[4096]{0:T(1024)S(1)}, u32[]{:S(2)}, u32[]{:S(2)}) collective-permute-start(f32[4096]{0:T(1024)S(1)} %add.264), channel_id=1, source_target_pairs={{0,4},{2,6},{4,0},{6,2},{8,12},{10,14},{12,8},{14,10},{16,20},{18,... | collective-permute-start | bytes 49160 | tf_op jit(solution)/shard_map/cond/branch_1_fun/cond/branch_1_fun/ppermute | solution.py:585
  304.2 35.2 %collective-permute-start.21 = (bf16[512,1024]{1,0:T(8,128)(2,1)}, bf16[512,1024]{1,0:T(8,128)(2,1)}, u32[]{:S(2)}, u32[]{:S(2)}) collective-permute-start(bf16[512,1024]{1,0:T(8,128)(2,1)} %get-tuple-element.325), channel_id=1, source_target_pairs={{0,1},{1,0},{2,3},{3,2},{4,5},{5,4},{6,7},{7,6},{8,9},{9,8},{10,11... | collective-permute-start | bytes 3145736 | tf_op jit(solution)/shard_map/cond/branch_1_fun/ppermute | solution.py:580
  305.6 31.7 %collective-permute-start.22 = (bf16[64,2048]{1,0:T(8,128)(2,1)}, bf16[64,2048]{1,0:T(8,128)(2,1)}, u32[]{:S(2)}, u32[]{:S(2)}) collective-permute-start(bf16[64,2048]{1,0:T(8,128)(2,1)} %get-tuple-element.328), channel_id=1, source_target_pairs={{0,8},{2,10},{4,12},{6,14},{8,16},{10,18},{12,20},{14,22},{16,24},... | collective-permute-start | bytes 786440 | tf_op jit(solution)/shard_map/cond/branch_1_fun/ppermute | solution.py:666
  305.9 31.3 %collective-permute-start.23 = (bf16[64,2048]{1,0:T(8,128)(2,1)}, bf16[64,2048]{1,0:T(8,128)(2,1)}, u32[]{:S(2)}, u32[]{:S(2)}) collective-permute-start(bf16[64,2048]{1,0:T(8,128)(2,1)} %get-tuple-element.329), channel_id=1, source_target_pairs={{0,16},{2,18},{4,20},{6,22},{8,24},{10,26},{12,28},{14,30},{16,0},... | collective-permute-start | bytes 786440 | tf_op jit(solution)/shard_map/cond/branch_1_fun/ppermute | solution.py:666
  307.8 29.5 %collective-permute-start.24 = (bf16[64,2048]{1,0:T(8,128)(2,1)}, bf16[64,2048]{1,0:T(8,128)(2,1)}, u32[]{:S(2)}, u32[]{:S(2)}) collective-permute-start(bf16[64,2048]{1,0:T(8,128)(2,1)} %get-tuple-element.330), channel_id=1, source_target_pairs={{0,24},{2,26},{4,28},{6,30},{8,0},{10,2},{12,4},{14,6},{16,8},{18,... | collective-permute-start | bytes 786440 | tf_op jit(solution)/shard_map/cond/branch_1_fun/ppermute | solution.py:666
  316.9 10.4 %collective-permute-start.19 = (f32[4,16,64]{2,1,0:T(8,128)S(1)}, f32[4,16,64]{2,1,0:T(8,128)S(1)}, u32[]{:S(2)}, u32[]{:S(2)}) collective-permute-start(f32[4,16,64]{2,1,0:T(8,128)S(1)} %pad_maximum_fusion.8), channel_id=1, source_target_pairs={{0,8},{2,10},{4,12},{6,14},{8,0},{10,2},{12,4},{14,6},{16,24},{18,... | collective-permute-start | bytes 49160 | tf_op jit(solution)/shard_map/cond/branch_1_fun/cond/branch_1_fun/ppermute | solution.py:585
  (59 other events, 589.2 us)
Sparse Core Ops, SparseCore 0:
  10.8 54.4 all-gather.2
  68.1 73.3 all-gather.4
  188.5 107.7 reduce-scatter.1
